TPU v7x, 32 devices: a whole 2x2x4 slice. The times are simulated.
32 devices in a mesh: section: 4 (over y, x), fsdp: 2 (over core), dp: 4 (over z).
Axes of the slice: x: 2, y: 2, z: 4, core: 2. Of those that a mesh axis runs over, the one named last changes fastest.
Arguments:
- inputs: bfloat16 [4, 256, 4096], P(None, ('fsdp', 'dp')), may hold values from -6 to 6
- cotangent: bfloat16 [4, 256, 4096], P(None, ('fsdp', 'dp')), may hold values from -0.09375 to 0.09375
- norm_gain: bfloat16 [4, 4096], P('section', 'fsdp'), may hold values from 0.25 to 1.75
- up_blocks: bfloat16 [4, 128, 128, 128], P('section', 'fsdp'), may hold values from -0.5 to 0.5
- down_blocks: bfloat16 [4, 128, 128, 128], P('section', 'fsdp'), may hold values from -0.25 to 0.25
- up_left: bfloat16 [4, 16, 4096], P('section', None, 'fsdp'), may hold values from -0.09375 to 0.09375
- up_right: bfloat16 [4, 16, 16384], P('section', None, 'fsdp'), may hold values from -1.5 to 1.5
- down_left: bfloat16 [4, 16, 16384], P('section', None, 'fsdp'), may hold values from -0.046875 to 0.046875
- down_right: bfloat16 [4, 16, 4096], P('section', None, 'fsdp'), may hold values from -1.5 to 1.5
- up_pattern: int32 [4, 128], P('section'), may hold values from 0 to 31, as said below
- down_pattern: int32 [4, 128], P('section'), may hold values from 0 to 127, as said below
Outputs:
- grad_norm_gain: float32 [4, 4096], P('section', 'fsdp')
- grad_up_blocks: float32 [4, 128, 128, 128], P('section', 'fsdp')
- grad_down_blocks: float32 [4, 128, 128, 128], P('section', 'fsdp')
- grad_up_left: float32 [4, 16, 4096], P('section', None, 'fsdp')
- grad_up_right: float32 [4, 16, 16384], P('section', None, 'fsdp')
- grad_down_left: float32 [4, 16, 16384], P('section', None, 'fsdp')
- grad_down_right: float32 [4, 16, 4096], P('section', None, 'fsdp')
Inputs may be any that keep to these rules, and one draw needn't show every extreme that they name: Each row of up_pattern names every one of the 32 model blocks exactly 4 times. Each row of down_pattern names every one of the 128 hidden blocks exactly once.
All inputs are finite; a program needn't handle non-finite values.
Results may differ from a plain program's by a relative error of at most 0.023.
Values may be sent and summed in bfloat16 or wider, within the bound.
No kernel may reach another device: no remote copies, remote signals or barrier semaphores. Data moves between devices by JAX's collectives and lax.ppermute only.
A program may use at most 192 MiB of HBM per device.

v0:
```python
import jax
import jax.numpy as jnp
from jax import lax
from jax.sharding import PartitionSpec as P

EPSILON = 1e-05
ROOT_HALF = 0.7071067811865476
NORMAL_PEAK = 0.3989422804014327


def passed_along(block, axis, distance):
    devices = range(lax.axis_size(axis))
    route = [(i - distance, i) for i in devices if i - distance in devices]
    return lax.ppermute(block, axis, route)


def gelu_pair(pre_act):
    normal_cdf = 0.5 * (1.0 + lax.erf(pre_act * ROOT_HALF))
    normal_pdf = jnp.exp(-0.5 * pre_act * pre_act) * NORMAL_PEAK
    return (pre_act * normal_cdf, normal_cdf + pre_act * normal_pdf)


def layer_forward(layer_in, weights, up_order, down_order):
    gain, up_blocks, down_blocks, up_left, up_right, down_left, down_right = weights
    row_count, model_width = layer_in.shape
    block_size = up_blocks.shape[-1]
    model_blocks = model_width // block_size
    hidden_blocks = up_order.shape[0]
    group_size = hidden_blocks // model_blocks
    wide_in = layer_in.astype(jnp.float32)
    inv_rms = lax.rsqrt(jnp.mean(wide_in * wide_in, axis=-1, keepdims=True) + EPSILON)
    normed = (wide_in * inv_rms * gain.astype(jnp.float32)).astype(jnp.bfloat16)
    up_low = jnp.einsum("rd,kd->rk", normed, up_left, preferred_element_type=jnp.float32).astype(
        jnp.bfloat16
    )
    picked = jnp.take(normed.reshape(row_count, model_blocks, block_size), up_order, axis=1)
    pre_act = jnp.einsum(
        "rjb,jbe->rje", picked, up_blocks, preferred_element_type=jnp.float32
    ).reshape(row_count, hidden_blocks * block_size)
    pre_act = pre_act + jnp.einsum(
        "rk,kf->rf", up_low, up_right, preferred_element_type=jnp.float32
    )
    hidden = gelu_pair(pre_act)[0].astype(jnp.bfloat16)
    down_low = jnp.einsum(
        "rf,kf->rk", hidden, down_left, preferred_element_type=jnp.float32
    ).astype(jnp.bfloat16)
    chosen = jnp.take(
        hidden.reshape(row_count, hidden_blocks, block_size), down_order, axis=1
    ).reshape(row_count, model_blocks, group_size, block_size)
    mixed = jnp.einsum(
        "ricb,icbe->rie",
        chosen,
        down_blocks.reshape(model_blocks, group_size, block_size, block_size),
        preferred_element_type=jnp.float32,
    ).reshape(row_count, model_width)
    mixed = mixed + jnp.einsum(
        "rk,kd->rd", down_low, down_right, preferred_element_type=jnp.float32
    )
    return ((wide_in + mixed).astype(jnp.bfloat16), normed, up_low, pre_act, down_low)


def layer_backward(layer_in, pre_act, grad_out, weights, grouped_order, inverse_down):
    gain, up_blocks, down_blocks, up_left, up_right, down_left, down_right = weights
    row_count, model_width = layer_in.shape
    block_size = up_blocks.shape[-1]
    model_blocks = model_width // block_size
    hidden_blocks = up_blocks.shape[0]
    group_size = hidden_blocks // model_blocks
    wide_in = layer_in.astype(jnp.float32)
    inv_rms = lax.rsqrt(jnp.mean(wide_in * wide_in, axis=-1, keepdims=True) + EPSILON)
    hidden, gelu_slope = gelu_pair(pre_act)
    hidden = hidden.astype(jnp.bfloat16)
    grad_down_low = jnp.einsum(
        "rd,kd->rk", grad_out, down_right, preferred_element_type=jnp.float32
    ).astype(jnp.bfloat16)
    spread = jnp.einsum(
        "rie,icbe->ricb",
        grad_out.reshape(row_count, model_blocks, block_size),
        down_blocks.reshape(model_blocks, group_size, block_size, block_size),
        preferred_element_type=jnp.float32,
    ).reshape(row_count, hidden_blocks, block_size)
    grad_hidden = jnp.take(spread, inverse_down, axis=1).reshape(
        row_count, hidden_blocks * block_size
    )
    grad_hidden = grad_hidden + jnp.einsum(
        "rk,kf->rf", grad_down_low, down_left, preferred_element_type=jnp.float32
    )
    grad_pre = (grad_hidden * gelu_slope).astype(jnp.bfloat16)
    grad_up_low = jnp.einsum(
        "rf,kf->rk", grad_pre, up_right, preferred_element_type=jnp.float32
    ).astype(jnp.bfloat16)
    sent_back = jnp.einsum(
        "rje,jbe->rjb",
        grad_pre.reshape(row_count, hidden_blocks, block_size),
        up_blocks,
        preferred_element_type=jnp.float32,
    )
    grouped = jnp.take(sent_back, grouped_order, axis=1).reshape(
        row_count, model_blocks, group_size, block_size
    )
    grad_normed = jnp.sum(grouped, axis=2).reshape(row_count, model_width)
    grad_normed = grad_normed + jnp.einsum(
        "rk,kd->rd", grad_up_low, up_left, preferred_element_type=jnp.float32
    )
    scaled = grad_normed * gain.astype(jnp.float32)
    grad_gain = jnp.sum(grad_normed * wide_in * inv_rms, axis=0)
    grad_in = (
        grad_out.astype(jnp.float32)
        + inv_rms * scaled
        - wide_in * inv_rms * inv_rms * inv_rms * jnp.mean(wide_in * scaled, axis=-1, keepdims=True)
    )
    return (grad_in.astype(jnp.bfloat16), grad_pre, grad_up_low, grad_down_low, hidden, grad_gain)


def block_terms(normed, grad_pre, hidden, grad_out, up_order, down_order, block_count):
    row_count, model_width = normed.shape
    hidden_blocks = up_order.shape[0]
    block_size = grad_pre.shape[1] // hidden_blocks
    group_size = hidden_blocks // (model_width // block_size)
    picked = jnp.take(normed.reshape(row_count, -1, block_size), up_order, axis=1)
    grad_slice = grad_pre.reshape(row_count, hidden_blocks, block_size)
    grad_up = jnp.einsum("rjb,rje->jbe", picked, grad_slice, preferred_element_type=jnp.float32)
    chosen = jnp.take(hidden.reshape(row_count, hidden_blocks, block_size), down_order, axis=1)
    owner = jnp.arange(block_count, dtype=jnp.int32) // group_size
    spread = jnp.take(grad_out.reshape(row_count, -1, block_size), owner, axis=1)
    grad_down = jnp.einsum("rkb,rke->kbe", chosen, spread, preferred_element_type=jnp.float32)
    return jnp.stack([grad_up, grad_down], axis=1)


def factor_terms(normed, up_low, grad_pre, grad_up_low, hidden, down_low, grad_down_low, grad_out):
    grad_up_left = jnp.einsum("rk,rd->kd", grad_up_low, normed, preferred_element_type=jnp.float32)
    grad_up_right = jnp.einsum("rk,rf->kf", up_low, grad_pre, preferred_element_type=jnp.float32)
    grad_down_left = jnp.einsum(
        "rk,rf->kf", grad_down_low, hidden, preferred_element_type=jnp.float32
    )
    grad_down_right = jnp.einsum(
        "rk,rd->kd", down_low, grad_out, preferred_element_type=jnp.float32
    )
    return (grad_up_left, grad_up_right, grad_down_left, grad_down_right)


def shards(
    inputs,
    cotangent,
    norm_gain,
    up_blocks,
    down_blocks,
    up_left,
    up_right,
    down_left,
    down_right,
    up_pattern,
    down_pattern,
):
    gathered = (
        lax.all_gather(norm_gain, "fsdp", axis=1, tiled=True),
        lax.all_gather(up_blocks, "fsdp", axis=1, tiled=True),
        lax.all_gather(down_blocks, "fsdp", axis=1, tiled=True),
        lax.all_gather(up_left, "fsdp", axis=2, tiled=True),
        lax.all_gather(up_right, "fsdp", axis=2, tiled=True),
        lax.all_gather(down_left, "fsdp", axis=2, tiled=True),
        lax.all_gather(down_right, "fsdp", axis=2, tiled=True),
    )
    weights = tuple((gathered_piece[0] for gathered_piece in gathered))
    up_order = up_pattern[0]
    down_order = down_pattern[0]
    micro_count, row_count, model_width = inputs.shape
    block_size = weights[1].shape[-1]
    hidden_blocks = up_order.shape[0]
    hidden_width = hidden_blocks * block_size
    rank_size = weights[3].shape[0]
    grouped_order = jnp.argsort(up_order, stable=True)
    positions = jnp.arange(hidden_blocks, dtype=jnp.int32)
    inverse_down = jnp.sum(
        jnp.where(down_order[None, :] == positions[:, None], positions[None, :], 0), axis=1
    )
    section_count = lax.axis_size("section")
    section_index = lax.axis_index("section")
    step_count = micro_count + section_count - 1
    buffers = (
        jnp.zeros((micro_count, row_count, model_width), jnp.bfloat16),
        jnp.zeros((micro_count, row_count, model_width), jnp.bfloat16),
        jnp.zeros((micro_count, row_count, rank_size), jnp.bfloat16),
        jnp.zeros((micro_count, row_count, hidden_width), jnp.float32),
        jnp.zeros((micro_count, row_count, rank_size), jnp.bfloat16),
    )

    def forward_step(step, carry):
        received, stored = carry
        micro_batch = step - section_index
        is_live = (micro_batch >= 0) & (micro_batch < micro_count)
        slot = jnp.clip(micro_batch, 0, micro_count - 1)
        first_in = lax.dynamic_index_in_dim(inputs, slot, 0, keepdims=False)
        layer_in = jnp.where(section_index == 0, first_in, received)

        def forward_run_layer(stored):
            layer_out, normed, up_low, pre_act, down_low = layer_forward(
                layer_in, weights, up_order, down_order
            )
            fresh = (layer_in, normed, up_low, pre_act, down_low)
            return (
                layer_out,
                tuple(
                    (
                        lax.dynamic_update_index_in_dim(buffer, value, slot, 0)
                        for buffer, value in zip(stored, fresh)
                    )
                ),
            )

        def forward_pass_through(stored):
            return (jnp.zeros_like(layer_in), stored)

        layer_out, stored = lax.cond(is_live, forward_run_layer, forward_pass_through, stored)
        received = passed_along(layer_out, "section", 1)
        return (received, stored)

    start_rows = jnp.zeros((row_count, model_width), jnp.bfloat16)
    _, buffers = lax.fori_loop(0, step_count, forward_step, (start_rows, buffers))
    extra_state = (
        jnp.zeros((hidden_blocks, 2, block_size, block_size), jnp.float32),
        jnp.zeros((rank_size, model_width), jnp.float32),
        jnp.zeros((rank_size, hidden_width), jnp.float32),
        jnp.zeros((rank_size, hidden_width), jnp.float32),
        jnp.zeros((rank_size, model_width), jnp.float32),
    )

    def record(extra_state, pieces):
        normed, up_low, grad_pre, grad_up_low, hidden, down_low, grad_down_low, grad_out = pieces
        blocks = block_terms(
            normed, grad_pre, hidden, grad_out, up_order, down_order, hidden_blocks
        )
        factors = factor_terms(
            normed, up_low, grad_pre, grad_up_low, hidden, down_low, grad_down_low, grad_out
        )
        return (
            extra_state[0] + blocks,
            extra_state[1] + factors[0],
            extra_state[2] + factors[1],
            extra_state[3] + factors[2],
            extra_state[4] + factors[3],
        )

    def backward_step(step, carry):
        received, gain_total, extra_state = carry
        micro_batch = step - (section_count - 1 - section_index)
        is_live = (micro_batch >= 0) & (micro_batch < micro_count)
        slot = jnp.clip(micro_batch, 0, micro_count - 1)
        last_grad = lax.dynamic_index_in_dim(cotangent, slot, 0, keepdims=False)
        grad_out = jnp.where(section_index == section_count - 1, last_grad, received)

        def backward_run_layer(state):
            gain_total, extra_state = state
            layer_in, normed, up_low, pre_act, down_low = tuple(
                (lax.dynamic_index_in_dim(buffer, slot, 0, keepdims=False) for buffer in buffers)
            )
            grad_in, grad_pre, grad_up_low, grad_down_low, hidden, grad_gain = layer_backward(
                layer_in, pre_act, grad_out, weights, grouped_order, inverse_down
            )
            extra_state = record(
                extra_state,
                (normed, up_low, grad_pre, grad_up_low, hidden, down_low, grad_down_low, grad_out),
            )
            return (grad_in, (gain_total + grad_gain, extra_state))

        def backward_pass_through(state):
            return (jnp.zeros_like(grad_out), state)

        grad_in, (gain_total, extra_state) = lax.cond(
            is_live, backward_run_layer, backward_pass_through, (gain_total, extra_state)
        )
        received = passed_along(grad_in, "section", -1)
        return (received, gain_total, extra_state)

    gain_start = jnp.zeros((model_width,), jnp.float32)
    _, gain_total, extra_state = lax.fori_loop(
        0, step_count, backward_step, (start_rows, gain_start, extra_state)
    )
    factors = (extra_state[1], extra_state[2], extra_state[3], extra_state[4])
    block_total = extra_state[0]
    low_rank = (
        lax.psum_scatter(
            factors[0].astype(jnp.bfloat16), "fsdp", scatter_dimension=1, tiled=True
        ).astype(jnp.float32),
        lax.psum_scatter(
            factors[1].astype(jnp.bfloat16), "fsdp", scatter_dimension=1, tiled=True
        ).astype(jnp.float32),
        lax.psum_scatter(
            factors[2].astype(jnp.bfloat16), "fsdp", scatter_dimension=1, tiled=True
        ).astype(jnp.float32),
        lax.psum_scatter(
            factors[3].astype(jnp.bfloat16), "fsdp", scatter_dimension=1, tiled=True
        ).astype(jnp.float32),
        lax.psum_scatter(
            gain_total.astype(jnp.bfloat16), "fsdp", scatter_dimension=0, tiled=True
        ).astype(jnp.float32),
    )
    block_sums = lax.psum_scatter(
        block_total.astype(jnp.bfloat16), "fsdp", scatter_dimension=0, tiled=True
    )
    summed = (
        lax.psum(block_sums, "dp").astype(jnp.float32),
        lax.psum(low_rank[0].astype(jnp.bfloat16), "dp").astype(jnp.float32),
        lax.psum(low_rank[1].astype(jnp.bfloat16), "dp").astype(jnp.float32),
        lax.psum(low_rank[2].astype(jnp.bfloat16), "dp").astype(jnp.float32),
        lax.psum(low_rank[3].astype(jnp.bfloat16), "dp").astype(jnp.float32),
        lax.psum(low_rank[4].astype(jnp.bfloat16), "dp").astype(jnp.float32),
    )
    block_part = summed[0]
    small_sums = summed[1:]
    return (
        small_sums[4][None],
        block_part[:, 0][None],
        block_part[:, 1][None],
        small_sums[0][None],
        small_sums[1][None],
        small_sums[2][None],
        small_sums[3][None],
    )


def solution(mesh):
    placed = (
        P(None, ("fsdp", "dp"), None),
        P(None, ("fsdp", "dp"), None),
        P("section", "fsdp"),
        P("section", "fsdp", None, None),
        P("section", "fsdp", None, None),
        P("section", None, "fsdp"),
        P("section", None, "fsdp"),
        P("section", None, "fsdp"),
        P("section", None, "fsdp"),
        P("section", None),
        P("section", None),
    )
    return jax.shard_map(
        shards,
        mesh=mesh,
        in_specs=placed,
        out_specs=(
            P("section", "fsdp"),
            P("section", "fsdp", None, None),
            P("section", "fsdp", None, None),
            P("section", None, "fsdp"),
            P("section", None, "fsdp"),
            P("section", None, "fsdp"),
            P("section", None, "fsdp"),
        ),
        check_vma=False,
    )
```

profile of v0, /device:TPU:13, one launch (start us, length us, event | category | flops | bytes accessed | tf_op | source)
XLA Modules:
  0.0 1118.7 jit_solution(12204579233964528389)
XLA Ops:
  25.5 16.5 %all-gather.5.cloned.1.call-done = bf16[1,128,128,128]{3,2,0,1:T(8,128)(2,1)} async-done(((bf16[1,64,128,128]{3,2,0,1:T(8,128)(2,1)}), bf16[1,128,128,128]{3,2,0,1:T(8,128)(2,1)}) %all-gather.5.cloned.1.call-update) | async-done | bytes 4194320 | tf_op jit(solution)/shard_map/all_gather | solution.py:158
  49.0 217.1 %while.51 = (s32[]{:T(128)}, bf16[32,4096]{1,0:T(8,128)(2,1)S(1)}, bf16[4,32,4096]{2,1,0:T(8,128)(2,1)}, bf16[4,32,4096]{2,1,0:T(8,128)(2,1)}, bf16[4,32,16]{1,2...) while((s32[]{:T(128)}, bf16[32,4096]{1,0:T(8,128)(2,1)S(1)}, ...), condition=%wide.region_4.7_spmd, body=%wide.region_0.6_spmd.sunk | while | flops 317203744 | bytes 38148832 | solution.py:219
  63.3 49.0 %collective-permute-done = bf16[32,4096]{1,0:T(8,128)(2,1)S(1)} collective-permute-done((bf16[32,4096]{1,0:T(8,128)(2,1)}, bf16[32,4096]{1,0:T(8,128)(2,1)S(1)}, u32[]{:S(2)}, u32[]{:S(2)}) %collective-permute-start) | collective-permute-done | bytes 262176 | tf_op jit(solution)/shard_map/while/body/eval_jaxpr/ppermute | solution.py:14
  112.3 22.9 %conditional.4 = (bf16[32,4096]{1,0:T(8,128)(2,1)}, bf16[4,32,4096]{2,1,0:T(8,128)(2,1)}, bf16[4,32,4096]{2,1,0:T(8,128)(2,1)}, bf16[4,32,16]{1,2,0:T(8,128)(2,1...) conditional(s32[]{:T(128)} %convert_element_type.200, (bf16[4,32,4096]{2,1,0:T(8,128)(2,1)}, ...), branch_computations={%region_1.1_spmd, %region_2.5_spmd} | conditional | flops 317203744 | bytes 37099796 | solution.py:214
  144.8 22.9 %conditional.4 = (bf16[32,4096]{1,0:T(8,128)(2,1)}, bf16[4,32,4096]{2,1,0:T(8,128)(2,1)}, bf16[4,32,4096]{2,1,0:T(8,128)(2,1)}, bf16[4,32,16]{1,2,0:T(8,128)(2,1...) conditional(s32[]{:T(128)} %convert_element_type.200, (bf16[4,32,4096]{2,1,0:T(8,128)(2,1)}, ...), branch_computations={%region_1.1_spmd, %region_2.5_spmd} | conditional | flops 317203744 | bytes 37099796 | solution.py:214
  176.2 22.9 %conditional.4 = (bf16[32,4096]{1,0:T(8,128)(2,1)}, bf16[4,32,4096]{2,1,0:T(8,128)(2,1)}, bf16[4,32,4096]{2,1,0:T(8,128)(2,1)}, bf16[4,32,16]{1,2,0:T(8,128)(2,1...) conditional(s32[]{:T(128)} %convert_element_type.200, (bf16[4,32,4096]{2,1,0:T(8,128)(2,1)}, ...), branch_computations={%region_1.1_spmd, %region_2.5_spmd} | conditional | flops 317203744 | bytes 37099796 | solution.py:214
  207.3 22.9 %conditional.4 = (bf16[32,4096]{1,0:T(8,128)(2,1)}, bf16[4,32,4096]{2,1,0:T(8,128)(2,1)}, bf16[4,32,4096]{2,1,0:T(8,128)(2,1)}, bf16[4,32,16]{1,2,0:T(8,128)(2,1...) conditional(s32[]{:T(128)} %convert_element_type.200, (bf16[4,32,4096]{2,1,0:T(8,128)(2,1)}, ...), branch_computations={%region_1.1_spmd, %region_2.5_spmd} | conditional | flops 317203744 | bytes 37099796 | solution.py:214
  239.2 23.2 %collective-permute-start = (bf16[32,4096]{1,0:T(8,128)(2,1)}, bf16[32,4096]{1,0:T(8,128)(2,1)S(1)}, u32[]{:S(2)}, u32[]{:S(2)}) collective-permute-start(bf16[32,4096]{1,0:T(8,128)(2,1)} %get-tuple-element.1961), channel_id=1, source_target_pairs={{0,8},{8,16},{16,24},{1,9},{9,17},{17,25},{2,10},{10,18},{18,26},{... | collective-permute-start | bytes 786440 | tf_op jit(solution)/shard_map/while/body/eval_jaxpr/ppermute | solution.py:14
  274.8 466.4 %while.52 = (s32[]{:T(128)}, bf16[32,4096]{1,0:T(8,128)(2,1)S(1)}, f32[4096]{0:T(1024)S(1)}, f32[128,2,128,128]{3,2,0,1:T(8,128)}, f32[16,4096]{1,0:T(8,128)S(1)...) while((s32[]{:T(128)}, bf16[32,4096]{1,0:T(8,128)(2,1)S(1)}, ...), condition=%wide.region_14.18_spmd, body=%wide.region_7.17_spmd.sunk | while | flops 646858368 | bytes 186830080 | solution.py:276
  277.4 73.1 %collective-permute-done.1 = bf16[32,4096]{1,0:T(8,128)(2,1)S(1)} collective-permute-done((bf16[32,4096]{1,0:T(8,128)(2,1)}, bf16[32,4096]{1,0:T(8,128)(2,1)S(1)}, u32[]{:S(2)}, u32[]{:S(2)}) %collective-permute-start.1) | collective-permute-done | bytes 262176 | tf_op jit(solution)/shard_map/while/body/eval_jaxpr/ppermute | solution.py:14
  350.5 68.6 %conditional.5 = (bf16[32,4096]{1,0:T(8,128)(2,1)}, f32[4096]{0:T(1024)S(1)}, f32[128,2,128,128]{3,2,0,1:T(8,128)}, f32[16,4096]{1,0:T(8,128)S(1)}, f32[16,16384...) conditional(s32[]{:T(128)} %convert_element_type.201, (f32[4096]{0:T(1024)S(1)}, ...), branch_computations={%region_8.10_spmd, %region_9.16_spmd} | conditional | flops 646858368 | bytes 185780896 | solution.py:269
  406.7 12.4 %maximum_add_fusion = f32[128,2,128,128]{3,2,0,1:T(8,128)} fusion(f32[128,2,128,128]{3,2,0,1:T(8,128)} %get-tuple-element.1407, f32[128,1,128,128]{3,2,0,1:T(8,128)S(1)} %convolution_bitcast_fusion.2, f32[128,1,128,128]{3,2,0,1:T(8,128)S(1)} %convolution_bitcast_fusion.3), kind=kLoop, calls=%fused_computation.48 | loop fusion | flops 8388608 | bytes 50331648 | tf_op jit(solution)/shard_map/while/body/eval_jaxpr/cond/branch_1_fun/add | solution.py:237
  426.4 68.7 %conditional.5 = (bf16[32,4096]{1,0:T(8,128)(2,1)}, f32[4096]{0:T(1024)S(1)}, f32[128,2,128,128]{3,2,0,1:T(8,128)}, f32[16,4096]{1,0:T(8,128)S(1)}, f32[16,16384...) conditional(s32[]{:T(128)} %convert_element_type.201, (f32[4096]{0:T(1024)S(1)}, ...), branch_computations={%region_8.10_spmd, %region_9.16_spmd} | conditional | flops 646858368 | bytes 185780896 | solution.py:269
  482.7 12.4 %maximum_add_fusion = f32[128,2,128,128]{3,2,0,1:T(8,128)} fusion(f32[128,2,128,128]{3,2,0,1:T(8,128)} %get-tuple-element.1407, f32[128,1,128,128]{3,2,0,1:T(8,128)S(1)} %convolution_bitcast_fusion.2, f32[128,1,128,128]{3,2,0,1:T(8,128)S(1)} %convolution_bitcast_fusion.3), kind=kLoop, calls=%fused_computation.48 | loop fusion | flops 8388608 | bytes 50331648 | tf_op jit(solution)/shard_map/while/body/eval_jaxpr/cond/branch_1_fun/add | solution.py:237
  502.4 68.7 %conditional.5 = (bf16[32,4096]{1,0:T(8,128)(2,1)}, f32[4096]{0:T(1024)S(1)}, f32[128,2,128,128]{3,2,0,1:T(8,128)}, f32[16,4096]{1,0:T(8,128)S(1)}, f32[16,16384...) conditional(s32[]{:T(128)} %convert_element_type.201, (f32[4096]{0:T(1024)S(1)}, ...), branch_computations={%region_8.10_spmd, %region_9.16_spmd} | conditional | flops 646858368 | bytes 185780896 | solution.py:269
  558.6 12.4 %maximum_add_fusion = f32[128,2,128,128]{3,2,0,1:T(8,128)} fusion(f32[128,2,128,128]{3,2,0,1:T(8,128)} %get-tuple-element.1407, f32[128,1,128,128]{3,2,0,1:T(8,128)S(1)} %convolution_bitcast_fusion.2, f32[128,1,128,128]{3,2,0,1:T(8,128)S(1)} %convolution_bitcast_fusion.3), kind=kLoop, calls=%fused_computation.48 | loop fusion | flops 8388608 | bytes 50331648 | tf_op jit(solution)/shard_map/while/body/eval_jaxpr/cond/branch_1_fun/add | solution.py:237
  578.4 68.7 %conditional.5 = (bf16[32,4096]{1,0:T(8,128)(2,1)}, f32[4096]{0:T(1024)S(1)}, f32[128,2,128,128]{3,2,0,1:T(8,128)}, f32[16,4096]{1,0:T(8,128)S(1)}, f32[16,16384...) conditional(s32[]{:T(128)} %convert_element_type.201, (f32[4096]{0:T(1024)S(1)}, ...), branch_computations={%region_8.10_spmd, %region_9.16_spmd} | conditional | flops 646858368 | bytes 185780896 | solution.py:269
  634.7 12.4 %maximum_add_fusion = f32[128,2,128,128]{3,2,0,1:T(8,128)} fusion(f32[128,2,128,128]{3,2,0,1:T(8,128)} %get-tuple-element.1407, f32[128,1,128,128]{3,2,0,1:T(8,128)S(1)} %convolution_bitcast_fusion.2, f32[128,1,128,128]{3,2,0,1:T(8,128)S(1)} %convolution_bitcast_fusion.3), kind=kLoop, calls=%fused_computation.48 | loop fusion | flops 8388608 | bytes 50331648 | tf_op jit(solution)/shard_map/while/body/eval_jaxpr/cond/branch_1_fun/add | solution.py:237
  656.1 72.6 %collective-permute-start.1 = (bf16[32,4096]{1,0:T(8,128)(2,1)}, bf16[32,4096]{1,0:T(8,128)(2,1)S(1)}, u32[]{:S(2)}, u32[]{:S(2)}) collective-permute-start(bf16[32,4096]{1,0:T(8,128)(2,1)} %get-tuple-element.1994), channel_id=1, source_target_pairs={{8,0},{16,8},{24,16},{9,1},{17,9},{25,17},{10,2},{18,10},{26,18},{... | collective-permute-start | bytes 786440 | tf_op jit(solution)/shard_map/while/body/eval_jaxpr/ppermute | solution.py:14
  760.7 13.7 %copy.116 = bf16[16,8,256,128]{3,1,2,0:T(8,128)(2,1)} copy(bf16[16,8,256,128]{3,2,1,0:T(8,128)(2,1)} %bitcast.205) | data formatting | bytes 16777216
  777.9 93.7 %reduce-scatter.17.cloned.1.call-done = bf16[64,32768]{1,0:T(8,128)(2,1)} async-done(((bf16[128,32768]{1,0:T(8,128)(2,1)}), bf16[64,32768]{1,0:T(8,128)(2,1)}) %reduce-scatter.17.cloned.1.call-update) | async-done | bytes 4194320
  894.5 11.9 %reduce-scatter.13.cloned.1.call-done = bf16[16,8192]{1,0:T(8,128)(2,1)} async-done(((bf16[16,16384]{1,0:T(8,128)(2,1)}), bf16[16,8192]{1,0:T(8,128)(2,1)}) %reduce-scatter.13.cloned.1.call-update) | async-done | bytes 262160 | tf_op jit(solution)/shard_map/reduce_scatter | solution.py:288
  906.4 11.9 %reduce-scatter.11.cloned.1.call-done = bf16[16,8192]{1,0:T(8,128)(2,1)} async-done(((bf16[16,16384]{1,0:T(8,128)(2,1)}), bf16[16,8192]{1,0:T(8,128)(2,1)}) %reduce-scatter.11.cloned.1.call-update) | async-done | bytes 262160 | tf_op jit(solution)/shard_map/reduce_scatter | solution.py:285
  930.4 167.7 %all-reduce.4.cloned.1.call-done = (bf16[64,2,128,128]{3,2,0,1:T(8,128)(2,1)}, bf16[1,16,2048]{2,1,0:T(8,128)(2,1)}, bf16[1,16,8192]{2,1,0:T(8,128)(2,1)}, bf16[...) async-done(((bf16[64,2,128,128]{3,2,0,1:T(8,128)(2,1)}, bf16[1,16,2048]{2,1,0:T(8,128)(2,1)}, bf16[1,16,8192]{2,1,0:T(8,128)(2,1)}, bf16[1,16,8192]{2,1,0:T(8,128)(2,1)}, ...) | async-done | bytes 4849680 | tf_op jit(solution)/shard_map/psum | solution.py:302
  (572 shorter events, 523.3 us)
Async XLA Ops:
  7.2 18.3 %all-gather.3.cloned.1.call-start = ((), (), s32[]{:S(2)}) async-start(), calls=%async_computation.5 | async-start | bytes 6291456 | tf_op jit(solution)/shard_map/all_gather | solution.py:157
  7.9 34.1 %all-gather.5.cloned.1.call-start = ((), (), s32[]{:S(2)}) async-start(), calls=%async_computation.6 | async-start | bytes 6291456 | tf_op jit(solution)/shard_map/all_gather | solution.py:158
  8.7 862.9 %reduce-scatter.17.cloned.1.call-start = ((), (), s32[]{:S(2)}) async-start(), calls=%async_computation.11 | async-start | bytes 12582912
  49.7 10.7 collective-permute-start
  61.1 51.2 %collective-permute-start = (bf16[32,4096]{1,0:T(8,128)(2,1)}, bf16[32,4096]{1,0:T(8,128)(2,1)S(1)}, u32[]{:S(2)}, u32[]{:S(2)}) collective-permute-start(bf16[32,4096]{1,0:T(8,128)(2,1)} %get-tuple-element.1961), channel_id=1, source_target_pairs={{0,8},{8,16},{16,24},{1,9},{9,17},{17,25},{2,10},{10,18},{18,26},{... | collective-permute-start | bytes 786440 | tf_op jit(solution)/shard_map/while/body/eval_jaxpr/ppermute | solution.py:14
  135.2 9.5 collective-permute-start
  167.6 8.6 collective-permute-start
  199.1 8.2 collective-permute-start
  230.3 8.2 collective-permute-start
  239.2 26.9 %collective-permute-start = (bf16[32,4096]{1,0:T(8,128)(2,1)}, bf16[32,4096]{1,0:T(8,128)(2,1)S(1)}, u32[]{:S(2)}, u32[]{:S(2)}) collective-permute-start(bf16[32,4096]{1,0:T(8,128)(2,1)} %get-tuple-element.1961), channel_id=1, source_target_pairs={{0,8},{8,16},{16,24},{1,9},{9,17},{17,25},{2,10},{10,18},{18,26},{... | collective-permute-start | bytes 786440 | tf_op jit(solution)/shard_map/while/body/eval_jaxpr/ppermute | solution.py:14
  275.5 75.0 %collective-permute-start.1 = (bf16[32,4096]{1,0:T(8,128)(2,1)}, bf16[32,4096]{1,0:T(8,128)(2,1)S(1)}, u32[]{:S(2)}, u32[]{:S(2)}) collective-permute-start(bf16[32,4096]{1,0:T(8,128)(2,1)} %get-tuple-element.1994), channel_id=1, source_target_pairs={{8,0},{16,8},{24,16},{9,1},{17,9},{25,17},{10,2},{18,10},{26,18},{... | collective-permute-start | bytes 786440 | tf_op jit(solution)/shard_map/while/body/eval_jaxpr/ppermute | solution.py:14
  350.5 17.1 %copy-start.1 = (f32[16,16384]{1,0:T(8,128)}, f32[16,16384]{1,0:T(8,128)S(1)}, u32[]{:S(2)}) copy-start(f32[16,16384]{1,0:T(8,128)S(1)} %get-tuple-element.1414) | copy-start | bytes 3145732 | tf_op jit(solution)/shard_map/while/body/eval_jaxpr/cond
  419.1 7.3 collective-permute-start.1
  495.1 7.3 collective-permute-start.1
  502.4 17.1 %copy-start.1 = (f32[16,16384]{1,0:T(8,128)}, f32[16,16384]{1,0:T(8,128)S(1)}, u32[]{:S(2)}) copy-start(f32[16,16384]{1,0:T(8,128)S(1)} %get-tuple-element.1414) | copy-start | bytes 3145732 | tf_op jit(solution)/shard_map/while/body/eval_jaxpr/cond
  571.1 7.3 collective-permute-start.1
  647.1 8.2 collective-permute-start.1
  656.1 76.2 %collective-permute-start.1 = (bf16[32,4096]{1,0:T(8,128)(2,1)}, bf16[32,4096]{1,0:T(8,128)(2,1)S(1)}, u32[]{:S(2)}, u32[]{:S(2)}) collective-permute-start(bf16[32,4096]{1,0:T(8,128)(2,1)} %get-tuple-element.1994), channel_id=1, source_target_pairs={{8,0},{16,8},{24,16},{9,1},{17,9},{25,17},{10,2},{18,10},{26,18},{... | collective-permute-start | bytes 786440 | tf_op jit(solution)/shard_map/while/body/eval_jaxpr/ppermute | solution.py:14
  733.0 8.2 collective-permute-start.1
  774.5 108.5 %reduce-scatter.15.cloned.1.call-start = ((), (), s32[]{:S(2)}) async-start(), calls=%async_computation.10 | async-start | bytes 196608 | tf_op jit(solution)/shard_map/reduce_scatter | solution.py:291
  775.2 119.2 %reduce-scatter.9.cloned.1.call-start = ((), (), s32[]{:S(2)}) async-start(), calls=%async_computation.7 | async-start | bytes 196608 | tf_op jit(solution)/shard_map/reduce_scatter | solution.py:282
  776.0 130.4 %reduce-scatter.13.cloned.1.call-start = ((), (), s32[]{:S(2)}) async-start(), calls=%async_computation.9 | async-start | bytes 786432 | tf_op jit(solution)/shard_map/reduce_scatter | solution.py:288
  776.9 141.4 %reduce-scatter.11.cloned.1.call-start = ((), (), s32[]{:S(2)}) async-start(), calls=%async_computation.8 | async-start | bytes 786432 | tf_op jit(solution)/shard_map/reduce_scatter | solution.py:285
  777.8 320.3 %all-reduce.4.cloned.1.call-start = ((), (), s32[]{:S(2)}) async-start(), calls=%async_computation.12 | async-start | bytes 9699328 | tf_op jit(solution)/shard_map/psum | solution.py:302
  (105 other events, 653.5 us)
Sparse Core Ops, SparseCore 0:
  9.5 15.9 all-gather.2
  27.0 14.9 all-gather.4
  774.6 96.8 reduce-scatter.16
  874.3 8.7 reduce-scatter.14
  885.7 8.6 reduce-scatter.8
  897.2 9.1 reduce-scatter.12
  909.2 9.0 reduce-scatter.10
  921.9 176.2 all-reduce.3
where the time goes:
time: 1130 us; the launch traced here: 1120 us
  waiting for transfers between devices  505 us (45%)
  other arithmetic  163 us (14%)
  matrix products  152 us (13%)
  local copies, waits for them, and re-layouts  132 us (12%)
  starting transfers between devices  129 us (11%)
  blocking collectives  20.6 us (2%)
  between operations  15 us (1%)
    ppermute x14, waiting for transfers between devices, passed_along(): return lax.ppermute(block, axis, route)  184 us
    psum x1, waiting for transfers between devices, shards(): lax.psum(block_sums, 'dp').astype(jnp.float32)  168 us
    ppermute x14, starting transfers between devices, passed_along(): return lax.ppermute(block, axis, route)  128 us
    unnamed x9, waiting for transfers between devices  95.1 us
    add x4, other arithmetic, record(): extra_state[0] + blocks  49.6 us
    unnamed x20, local copies, waits for them, and re-layouts  31.6 us
  transfers between devices with their start and end apart: 22, of which 22 were waited for; matrix products, arithmetic and copies ran while one was open for 1% of the time, Pallas kernels for 0%

commit v1 on v0

v1 whole, which is shorter than its diff:
```python
import functools

import jax
import jax.numpy as jnp
from jax import lax
from jax.experimental import pallas as pl
from jax.experimental.pallas import tpu as pltpu
from jax.sharding import PartitionSpec as P

EPSILON = 1e-05
NORMAL_PEAK = 0.3989422804014327
TAIL_SCALE = 0.3
TAIL = (
    0.11962930931947272,
    0.12075380294875883,
    0.09991439682547013,
    0.12855881360857063,
    -0.05367866289105895,
    0.20634847173237508,
    -0.15720038925639956,
    0.03567418525278745,
)
BLK = 128
RANK = 16
BF = jnp.bfloat16
F32 = jnp.float32
NN = (((1,), (0,)), ((), ()))
NT = (((1,), (1,)), ((), ()))
TN = (((0,), (0,)), ((), ()))
ANY = pl.BlockSpec(memory_space=pl.ANY)
SMEM = pl.BlockSpec(memory_space=pltpu.SMEM)


def dot(a, b, dims=NN):
    return lax.dot_general(a, b, dims, preferred_element_type=F32)


def gelu_both(value):
    bell = jnp.exp(-0.5 * value * value)
    denom = 1.0 + TAIL_SCALE * jnp.abs(value)
    guess = pl.reciprocal(denom, approx=True)
    t = guess * (2.0 - denom * guess)
    poly = jnp.full_like(t, TAIL[-1])
    for coef in TAIL[-2::-1]:
        poly = poly * t + coef
    tail = bell * (t * poly)
    cdf = jnp.where(value < 0.0, tail, 1.0 - tail)
    return value * cdf, cdf + value * (bell * NORMAL_PEAK)


class Dims:
    def __init__(self, width, hidden_blocks, parts):
        self.parts = parts
        self.width = width
        self.model = width // BLK
        self.hidden = hidden_blocks
        self.group = hidden_blocks // self.model
        self.mh = self.model // parts
        self.hh = hidden_blocks // parts
        self.ul = 0
        self.dr = self.mh * BLK
        self.ur = 2 * self.mh * BLK
        self.dl = self.ur + self.hh * BLK
        self.gain = self.dl + self.hh * BLK
        self.packed = self.gain + self.mh * BLK


def lanes(start, count=BLK):
    return pl.ds(pl.multiple_of(start, BLK), count)


def load_weights(f, srcs, dsts, sems):
    copies = []
    for n, (src, dst) in enumerate(zip(srcs, dsts)):
        if len(src) == 1:
            whole = pltpu.make_async_copy(src[0], dst, sems.at[2 * n])
            whole.start()
            copies.append((whole,))
            continue
        own, other = src
        half = dst.shape[0] // 2
        if own.ndim < dst.ndim:
            mine, theirs = f, 1 - f
        else:
            mine, theirs = pl.ds(f * half, half), pl.ds((1 - f) * half, half)
        a = pltpu.make_async_copy(own, dst.at[mine], sems.at[2 * n])
        b = pltpu.make_async_copy(other, dst.at[theirs], sems.at[2 * n + 1])
        a.start()
        b.start()
        copies.append((a, b))
    return copies


def done(pair):
    for copy in pair:
        copy.wait()


def inverse_rms(x_s, dims):
    rows = x_s.shape[0]
    total = jnp.zeros((rows, BLK), F32)
    for i in range(dims.model):
        part = x_s[:, i * BLK : (i + 1) * BLK].astype(F32)
        total = total + part * part
    return lax.rsqrt(jnp.sum(total, axis=1, keepdims=True) * (1.0 / dims.width) + EPSILON)


def fwd_body(dims, full, G, copies, f_x_s, small_s, up_s, dn_s, upo, dno, nrm_s, hid_s, slp_s, low_s, y_s):
    x_s = f_x_s
    rows = x_s.shape[0]
    r = inverse_rms(x_s, dims)
    upl = jnp.zeros((rows, RANK), F32)
    for h in range(dims.parts):
        for i in range(dims.mh):
            at = (h * dims.mh + i) * BLK
            gain = small_s[h, 0:1, dims.gain + i * BLK : dims.gain + (i + 1) * BLK].astype(F32)
            nrm_s[:, at : at + BLK] = (x_s[:, at : at + BLK].astype(F32) * r * gain).astype(BF)
        upl = upl + dot(
            nrm_s[:, h * dims.mh * BLK : (h + 1) * dims.mh * BLK],
            small_s[h, :, dims.ul : dims.ul + dims.mh * BLK],
            NT,
        )
    upl = upl.astype(BF)
    low_s[:, 0:RANK] = upl
    done(copies[0])

    def step(it, low):
        j0 = it * G
        h = j0 // dims.hh
        off = (j0 - h * dims.hh) * BLK
        ur = small_s[h, :, lanes(dims.ur + off, G * BLK)]
        dl = small_s[h, :, lanes(dims.dl + off, G * BLK)]
        hids = []
        for g in range(G):
            src = nrm_s[:, lanes(upo[j0 + g] * BLK)]
            lhs = jnp.concatenate([src, upl], axis=1)
            rhs = jnp.concatenate([up_s[j0 + g], ur[:, g * BLK : (g + 1) * BLK]], axis=0)
            hid, slope = gelu_both(dot(lhs, rhs))
            hid = hid.astype(BF)
            hid_s[j0 + g] = hid
            slp_s[j0 + g] = slope.astype(BF)
            hids.append(hid)
        return low + dot(jnp.concatenate(hids, axis=1), dl, NT)

    low = lax.fori_loop(0, dims.hidden // G, step, jnp.zeros((rows, RANK), F32))
    low = low.astype(BF)
    low_s[:, BLK : BLK + RANK] = low
    if full:
        done(copies[1])

        def down(it, _):
            for u in range(4):
                i = it * 4 + u
                h = i // dims.mh
                at = i * BLK
                dr = small_s[h, :, lanes(dims.dr + (i - h * dims.mh) * BLK)]
                parts = [hid_s[dno[i * dims.group + c]] for c in range(dims.group)]
                lhs = jnp.concatenate(parts + [low], axis=1)
                blocks = dn_s[pl.ds(i * dims.group, dims.group)].reshape(dims.group * BLK, BLK)
                mixed = dot(lhs, jnp.concatenate([blocks, dr], axis=0))
                y_s[:, lanes(at)] = (x_s[:, lanes(at)].astype(F32) + mixed).astype(BF)
            return 0

        lax.fori_loop(0, dims.model // 4, down, 0)


def bwd_hidden(dims, g_s, slp_s, gp_s, small_s, dn_s, dno, low_s):
    rows = g_s.shape[0]
    gdl = jnp.zeros((rows, RANK), F32)
    for h in range(dims.parts):
        gdl = gdl + dot(
            g_s[:, h * dims.mh * BLK : (h + 1) * dims.mh * BLK],
            small_s[h, :, dims.dr : dims.dr + dims.mh * BLK],
            NT,
        )
    gdl = gdl.astype(BF)
    low_s[:, BLK : BLK + RANK] = gdl

    def hid_step(it, gul):
        for u in range(2):
            i = it * 2 + u
            gi = g_s[:, lanes(i * BLK)]
            js = [dno[i * dims.group + c] for c in range(dims.group)]
            hs = [j // dims.hh for j in js]
            offs = [(j - h * dims.hh) * BLK for j, h in zip(js, hs)]
            dl = jnp.concatenate([small_s[h, :, lanes(dims.dl + o)] for h, o in zip(hs, offs)], axis=1)
            ur = jnp.concatenate([small_s[h, :, lanes(dims.ur + o)] for h, o in zip(hs, offs)], axis=1)
            blocks = dn_s[pl.ds(i * dims.group, dims.group)].reshape(dims.group * BLK, BLK)
            gh = dot(gi, blocks, NT) + dot(gdl, dl)
            slope = jnp.concatenate([slp_s[j] for j in js], axis=1).astype(F32)
            gp = (gh * slope).astype(BF)
            for c, j in enumerate(js):
                gp_s[j] = gp[:, c * BLK : (c + 1) * BLK]
            gul = gul + dot(gp, ur, NT)
        return gul

    gul = lax.fori_loop(0, dims.model // 2, hid_step, jnp.zeros((rows, RANK), F32))
    gul = gul.astype(BF)
    low_s[:, 0:RANK] = gul
    return gul


def bwd_input(dims, x_s, g_s, gp_s, small_s, up_s, grouped, gul, gn_s, gain_s, out_s):
    rows = g_s.shape[0]
    r = inverse_rms(x_s, dims)

    def step(it, acc):
        for u in range(2):
            i = it * 2 + u
            h = i // dims.mh
            off = (i - h * dims.mh) * BLK
            js = [grouped[i * dims.group + c] for c in range(dims.group)]
            lhs = jnp.concatenate([gp_s[j] for j in js], axis=1)
            rhs = jnp.concatenate([up_s[j] for j in js], axis=1)
            gn = dot(lhs, rhs, NT) + dot(gul, small_s[h, :, lanes(dims.ul + off)])
            x = x_s[:, lanes(i * BLK)].astype(F32)
            gain = small_s[h, 0:1, lanes(dims.gain + off)].astype(F32)
            scaled = gn * gain
            gn_s[:, lanes(i * BLK)] = scaled
            gain_s[0:1, lanes(i * BLK)] = jnp.sum(gn * x * r, axis=0, keepdims=True)
            acc = acc + x * scaled
        return acc

    acc = lax.fori_loop(0, dims.model // 2, step, jnp.zeros((rows, BLK), F32))
    shift = jnp.sum(acc, axis=1, keepdims=True) * (1.0 / dims.width) * (r * r * r)
    for i in range(dims.model):
        at = slice(i * BLK, (i + 1) * BLK)
        out_s[:, at] = (
            g_s[:, at].astype(F32) + r * gn_s[:, at] - x_s[:, at].astype(F32) * shift
        ).astype(BF)


def params(mib):
    return pltpu.CompilerParams(vmem_limit_bytes=mib * 1024 * 1024)


def fwd_slot(dims, sc, upo, dno, first, recv, weights, bufs, micro):
    rows = recv.shape[0]
    n_buf = 5
    shapes = (
        jax.ShapeDtypeStruct((micro, dims.hidden, rows, BLK), BF),
        jax.ShapeDtypeStruct((micro, dims.hidden, rows, BLK), BF),
        jax.ShapeDtypeStruct((micro, rows, dims.width), BF),
        jax.ShapeDtypeStruct((micro, rows, dims.width), BF),
        jax.ShapeDtypeStruct((micro, rows, 2 * BLK), BF),
    )
    n_w = len(weights[0])
    n_in = 5 + 3 * n_w + (n_buf if bufs is not None else 0)

    def kernel(*refs):
        sc, upo, dno, first, recv = refs[:5]
        up_w, dn_w, small_w = (refs[5 + k * n_w : 5 + (k + 1) * n_w] for k in range(3))
        y, hidb, slpb, nrmb, xb, lowb = refs[n_in : n_in + 6]
        up_s, dn_s, small_s, x_s, nrm_s, hid_s, slp_s, low_s, y_s, sems = refs[n_in + 6 :]

        @pl.when(sc[0] == 1)
        def _():
            m, f = sc[1], sc[2]

            @pl.when(sc[3] == 1)
            def _():
                pltpu.make_async_copy(first.at[m], x_s, sems.at[6]).start()

            @pl.when(sc[3] == 0)
            def _():
                pltpu.make_async_copy(recv, x_s, sems.at[6]).start()

            wait_x = pltpu.make_async_copy(recv, x_s, sems.at[6])
            small, up, dn = load_weights(
                f, (small_w, up_w, dn_w), (small_s, up_s, dn_s), sems
            )
            low_s[...] = jnp.zeros_like(low_s)
            wait_x.wait()
            save_x = pltpu.make_async_copy(x_s, xb.at[m], sems.at[7])
            save_x.start()
            done(small)
            fwd_body(dims, True, 8, (up, dn), x_s, small_s, up_s, dn_s, upo, dno, nrm_s, hid_s, slp_s, low_s, y_s)
            outs = [
                pltpu.make_async_copy(y_s, y, sems.at[8]),
                pltpu.make_async_copy(hid_s, hidb.at[m], sems.at[9]),
                pltpu.make_async_copy(slp_s, slpb.at[m], sems.at[10]),
                pltpu.make_async_copy(nrm_s, nrmb.at[m], sems.at[11]),
                pltpu.make_async_copy(low_s, lowb.at[m], sems.at[12]),
            ]
            for copy in outs:
                copy.start()
            save_x.wait()
            done(outs)

    args = [sc, upo, dno, first, recv] + [w for pair in weights for w in pair]
    aliases = {}
    if bufs is not None:
        aliases = {len(args) + n: n + 1 for n in range(n_buf)}
        args += list(bufs)
    out = pl.pallas_call(
        kernel,
        out_shape=(jax.ShapeDtypeStruct((rows, dims.width), BF),) + shapes,
        in_specs=[SMEM] * 3 + [ANY] * (len(args) - 3),
        out_specs=(ANY,) * 6,
        input_output_aliases=aliases,
        scratch_shapes=[
            pltpu.VMEM((dims.hidden, BLK, BLK), BF),
            pltpu.VMEM((dims.hidden, BLK, BLK), BF),
            pltpu.VMEM((dims.parts, RANK, dims.packed), BF),
            pltpu.VMEM((rows, dims.width), BF),
            pltpu.VMEM((rows, dims.width), BF),
            pltpu.VMEM((dims.hidden, rows, BLK), BF),
            pltpu.VMEM((dims.hidden, rows, BLK), BF),
            pltpu.VMEM((rows, 2 * BLK), BF),
            pltpu.VMEM((rows, dims.width), BF),
            pltpu.SemaphoreType.DMA((13,)),
        ],
        compiler_params=params(40),
        name="forward_rows",
    )(*args)
    return out[0], out[1:]


def bwd_slot(dims, sc, dno, grouped, last, recv, weights, xb, slpb, bufs, micro):
    rows = recv.shape[0]
    n_buf = 4
    shapes = (
        jax.ShapeDtypeStruct((micro, dims.hidden, rows, BLK), BF),
        jax.ShapeDtypeStruct((micro, rows, dims.width), BF),
        jax.ShapeDtypeStruct((micro, rows, 2 * BLK), BF),
        jax.ShapeDtypeStruct((micro, 8, dims.width), F32),
    )
    n_w = len(weights[0])
    n_in = 7 + 3 * n_w + (n_buf if bufs is not None else 0)

    def kernel(*refs):
        sc, dno, grouped, last, recv = refs[:5]
        up_w, dn_w, small_w = (refs[5 + k * n_w : 5 + (k + 1) * n_w] for k in range(3))
        xb, slpb = refs[5 + 3 * n_w : 7 + 3 * n_w]
        out, gpb, gb, lowb, gainb = refs[n_in : n_in + 5]
        up_s, dn_s, small_s, x_s, g_s, slp_s, gp_s, low_s, gn_s, gain_s, out_s, sems = refs[n_in + 5 :]

        @pl.when(sc[0] == 1)
        def _():
            m, f = sc[1], sc[2]

            @pl.when(sc[3] == 1)
            def _():
                pltpu.make_async_copy(last.at[m], g_s, sems.at[6]).start()

            @pl.when(sc[3] == 0)
            def _():
                pltpu.make_async_copy(recv, g_s, sems.at[6]).start()

            wait_g = pltpu.make_async_copy(recv, g_s, sems.at[6])
            get_slope = pltpu.make_async_copy(slpb.at[m], slp_s, sems.at[7])
            get_x = pltpu.make_async_copy(xb.at[m], x_s, sems.at[8])
            small, dn, up = load_weights(
                f, (small_w, dn_w, up_w), (small_s, dn_s, up_s), sems
            )
            get_slope.start()
            get_x.start()
            low_s[...] = jnp.zeros_like(low_s)
            gain_s[...] = jnp.zeros_like(gain_s)
            wait_g.wait()
            save_g = pltpu.make_async_copy(g_s, gb.at[m], sems.at[9])
            save_g.start()
            done(small)
            get_slope.wait()
            done(dn)
            gul = bwd_hidden(dims, g_s, slp_s, gp_s, small_s, dn_s, dno, low_s)
            outs = [
                pltpu.make_async_copy(gp_s, gpb.at[m], sems.at[10]),
                pltpu.make_async_copy(low_s, lowb.at[m], sems.at[11]),
            ]
            for copy in outs:
                copy.start()
            get_x.wait()
            done(up)
            bwd_input(dims, x_s, g_s, gp_s, small_s, up_s, grouped, gul, gn_s, gain_s, out_s)
            more = [
                pltpu.make_async_copy(gain_s, gainb.at[m], sems.at[12]),
                pltpu.make_async_copy(out_s, out, sems.at[13]),
            ]
            for copy in more:
                copy.start()
            save_g.wait()
            done(outs)
            done(more)

    args = [sc, dno, grouped, last, recv] + [w for pair in weights for w in pair] + [xb, slpb]
    aliases = {}
    if bufs is not None:
        aliases = {len(args) + n: n + 1 for n in range(n_buf)}
        args += list(bufs)
    out = pl.pallas_call(
        kernel,
        out_shape=(jax.ShapeDtypeStruct((rows, dims.width), BF),) + shapes,
        in_specs=[SMEM] * 3 + [ANY] * (len(args) - 3),
        out_specs=(ANY,) * 5,
        input_output_aliases=aliases,
        scratch_shapes=[
            pltpu.VMEM((dims.hidden, BLK, BLK), BF),
            pltpu.VMEM((dims.hidden, BLK, BLK), BF),
            pltpu.VMEM((dims.parts, RANK, dims.packed), BF),
            pltpu.VMEM((rows, dims.width), BF),
            pltpu.VMEM((rows, dims.width), BF),
            pltpu.VMEM((dims.hidden, rows, BLK), BF),
            pltpu.VMEM((dims.hidden, rows, BLK), BF),
            pltpu.VMEM((rows, 2 * BLK), BF),
            pltpu.VMEM((rows, dims.width), F32),
            pltpu.VMEM((8, dims.width), F32),
            pltpu.VMEM((rows, dims.width), BF),
            pltpu.SemaphoreType.DMA((14,)),
        ],
        compiler_params=params(40),
        name="backward_rows",
    )(*args)
    return out[0], out[1:]


def weight_grads(dims, sc, upo, dno, hidb, nrmb, lowf, gpb, gb, lowb, gainb):
    micro, _, rows, _ = hidb.shape
    VM = pl.BlockSpec(memory_space=pltpu.VMEM)

    two = dims.parts == 2

    def kernel(*refs):
        sc, upo, dno, hidb, nrmb, lowf, gpb, gb, lowb, gainb = refs[:10]
        outs_hbm = refs[10:-4]
        upg, dng, smg, sems = refs[-4:]
        f = sc[2]

        def cat(parts):
            return jnp.concatenate(parts, axis=0)

        def rows_of(ref, at, count=BLK):
            return cat([ref[m, :, lanes(at, count)] for m in range(micro)])

        def block_of(ref, j):
            return cat([ref[m, j] for m in range(micro)])

        up_low = cat([lowf[m, :, 0:BLK] for m in range(micro)])
        down_low = cat([lowf[m, :, BLK : 2 * BLK] for m in range(micro)])
        gul = cat([lowb[m, :, 0:BLK] for m in range(micro)])
        gdl = cat([lowb[m, :, BLK : 2 * BLK] for m in range(micro)])

        def which(h):
            return jnp.where(h == f, 0, 1) if two else h

        def down(it, _):
            for u in range(2):
                i = it * 2 + u
                h = i // dims.mh
                hid = jnp.concatenate(
                    [block_of(hidb, dno[i * dims.group + c]) for c in range(dims.group)], axis=1
                )
                gi = rows_of(gb, i * BLK)
                grad = dot(hid, gi, TN).astype(BF).reshape(dims.group, BLK, BLK)
                off = i - h * dims.mh
                w = which(h)
                dng[w, pl.ds(off * dims.group, dims.group)] = grad
                nrm = rows_of(nrmb, i * BLK)
                smg[w, :, lanes(dims.dr + off * BLK)] = dot(down_low, gi, TN)[0:RANK].astype(BF)
                smg[w, :, lanes(dims.ul + off * BLK)] = dot(gul, nrm, TN)[0:RANK].astype(BF)
                gain = jnp.zeros((8, BLK), F32)
                for m in range(micro):
                    gain = gain + gainb[m, :, lanes(i * BLK)]
                smg[w, :, lanes(dims.gain + off * BLK)] = jnp.broadcast_to(
                    jnp.sum(gain, axis=0, keepdims=True), (RANK, BLK)
                ).astype(BF)
            return 0

        lax.fori_loop(0, dims.model // 2, down, 0)

        def up(it, _):
            for u in range(4):
                j = it * 4 + u
                h = j // dims.hh
                off = j - h * dims.hh
                w = which(h)
                gp = block_of(gpb, j)
                hid = block_of(hidb, j)
                nrm = rows_of(nrmb, upo[j] * BLK)
                upg[w, off] = dot(nrm, gp, TN).astype(BF)
                smg[w, :, lanes(dims.ur + off * BLK)] = dot(up_low, gp, TN)[0:RANK].astype(BF)
                smg[w, :, lanes(dims.dl + off * BLK)] = dot(gdl, hid, TN)[0:RANK].astype(BF)
            return 0

        lax.fori_loop(0, dims.hidden // 4, up, 0)
        outs = []
        for n, src in enumerate((upg, dng, smg)):
            if two:
                outs.append(pltpu.make_async_copy(src.at[0], outs_hbm[2 * n], sems.at[2 * n]))
                outs.append(pltpu.make_async_copy(src.at[1], outs_hbm[2 * n + 1], sems.at[2 * n + 1]))
            else:
                outs.append(pltpu.make_async_copy(src, outs_hbm[n], sems.at[2 * n]))
        for copy in outs:
            copy.start()
        done(outs)

    lead = () if two else (dims.parts,)
    shapes = [lead + (dims.hh, BLK, BLK)] * 2 + [lead + (RANK, dims.packed)]
    shapes = [jax.ShapeDtypeStruct(shape, BF) for shape in shapes for _ in range(2 if two else 1)]
    got = pl.pallas_call(
        kernel,
        out_shape=tuple(shapes),
        in_specs=[SMEM] * 3 + [VM] * 7,
        out_specs=(ANY,) * len(shapes),
        scratch_shapes=[
            pltpu.VMEM((dims.parts, dims.hh, BLK, BLK), BF),
            pltpu.VMEM((dims.parts, dims.hh, BLK, BLK), BF),
            pltpu.VMEM((dims.parts, RANK, dims.packed), BF),
            pltpu.SemaphoreType.DMA((6,)),
        ],
        compiler_params=params(48),
        name="weight_gradients",
    )(sc, upo, dno, hidb, nrmb, lowf, gpb, gb, lowb, gainb)
    return [got[0:2], got[2:4], got[4:6]] if two else [got[0:1], got[1:2], got[2:3]]


def orders(up_order, down_order, dims):
    at = jnp.arange(dims.hidden, dtype=jnp.int32)
    same = (up_order[:, None] == up_order[None, :]) & (at[None, :] < at[:, None])
    place = up_order * dims.group + jnp.sum(same.astype(jnp.int32), axis=1)
    hit = place[None, :] == at[:, None]
    return jnp.sum(jnp.where(hit, at[None, :], 0), axis=1)


def shards(inputs, cotangent, norm_gain, up_blocks, down_blocks, up_left, up_right, down_left, down_right,
           up_pattern, down_pattern):
    micro, rows, width = inputs.shape
    upo, dno = up_pattern[0], down_pattern[0]
    parts = lax.axis_size("fsdp")
    dims = Dims(width, upo.shape[0], parts)
    n_sec = lax.axis_size("section")
    sec = lax.axis_index("section")
    f = lax.axis_index("fsdp")
    swap = [(0, 1), (1, 0)]
    small = jnp.concatenate(
        [up_left[0], down_right[0], up_right[0], down_left[0],
         jnp.broadcast_to(norm_gain, (RANK, norm_gain.shape[1]))], axis=1)

    def whole_layer(own, stacked):
        if parts == 2:
            return (own, lax.ppermute(own, "fsdp", swap))
        return (lax.all_gather(own, "fsdp", axis=0, tiled=not stacked),)

    small_w = whole_layer(small, True)
    up_w = whole_layer(up_blocks[0], False)
    weights = (up_w, whole_layer(down_blocks[0], False), small_w)
    grouped = orders(upo, dno, dims)
    zero = jnp.int32(0)

    def scalars(m, edge):
        live = (m >= 0) & (m < micro)
        return jnp.stack([live.astype(jnp.int32), jnp.clip(m, 0, micro - 1).astype(jnp.int32),
                          f.astype(jnp.int32), edge.astype(jnp.int32), zero, zero, zero, zero])

    state = {"token": None}

    def chained(*arrays):
        if state["token"] is None:
            return arrays
        out = lax.optimization_barrier(arrays + (state["token"],))
        return out[:-1]

    fbufs, bbufs = None, None
    frecv = inputs[0]
    brecv = inputs[0]
    last = n_sec - 1

    def forward(t):
        nonlocal fbufs, frecv
        (x,) = chained(frecv)
        y, fbufs = fwd_slot(dims, scalars(t - sec, sec == 0), upo, dno, inputs, x, weights, fbufs, micro)
        state["token"] = y
        pairs = [(s, s + 1) for s in range(last) if 0 <= t - s < micro]
        if pairs:
            frecv = lax.ppermute(y, "section", pairs)

    def backward(t):
        nonlocal bbufs, brecv
        (g,) = chained(brecv)
        out, bbufs = bwd_slot(dims, scalars(t - (last - sec), sec == last), dno, grouped, cotangent, g,
                              weights, fbufs[3], fbufs[1], bbufs, micro)
        state["token"] = out
        pairs = [(last - s, last - s - 1) for s in range(last) if 0 <= t - s < micro]
        if pairs:
            brecv = lax.ppermute(out, "section", pairs)

    slots = micro + last
    for t in range(slots):
        forward(t)
        if t >= last:
            backward(t - last)
    for t in range(slots - last, slots):
        backward(t)
    up_g, dn_g, small_g = weight_grads(
        dims, scalars(zero, sec == 0), upo, dno, fbufs[0], fbufs[2], fbufs[4], *bbufs)

    def total(pieces):
        if parts == 2:
            got = lax.ppermute(pieces[1], "fsdp", swap)
            both = (pieces[0].astype(F32) + got.astype(F32)).astype(BF)
        else:
            both = lax.psum_scatter(pieces[0], "fsdp", scatter_dimension=0, tiled=False)
        return lax.psum(both, "dp").astype(F32)

    sm = total(small_g)
    dn = total(dn_g)
    up = total(up_g)
    mw, hw = dims.mh * BLK, dims.hh * BLK
    return (
        sm[0:1, dims.gain : dims.gain + mw],
        up[None],
        dn[None],
        sm[None, :, dims.ul : dims.ul + mw],
        sm[None, :, dims.ur : dims.ur + hw],
        sm[None, :, dims.dl : dims.dl + hw],
        sm[None, :, dims.dr : dims.dr + mw],
    )


def solution(mesh):
    placed = (
        P(None, ("fsdp", "dp"), None),
        P(None, ("fsdp", "dp"), None),
        P("section", "fsdp"),
        P("section", "fsdp", None, None),
        P("section", "fsdp", None, None),
        P("section", None, "fsdp"),
        P("section", None, "fsdp"),
        P("section", None, "fsdp"),
        P("section", None, "fsdp"),
        P("section", None),
        P("section", None),
    )
    return jax.shard_map(
        shards,
        mesh=mesh,
        in_specs=placed,
        out_specs=(
            P("section", "fsdp"),
            P("section", "fsdp", None, None),
            P("section", "fsdp", None, None),
            P("section", None, "fsdp"),
            P("section", None, "fsdp"),
            P("section", None, "fsdp"),
            P("section", None, "fsdp"),
        ),
        check_vma=False,
    )
```

time: 1130 us -> 626 us (0.55)
  waiting for transfers between devices: 505 us -> 281 us
  matrix products: 152 us -> 0 us
  other arithmetic: 163 us -> 14.3 us
  Pallas kernels: 0 us -> 140 us
  starting transfers between devices: 129 us -> 43 us
  blocking collectives: 20.6 us -> 0 us
    dot_general x72 -> x0, matrix products: 152 us -> none  [the longest x4 15.3 us: layer_backward(): jnp.einsum('rk,kf->rf', grad_down_low, down_left, preferred_element_type=...]
    pallas_call x0 -> x15, Pallas kernels: none -> 140 us  [the longest x7 66.6 us: bwd_slot(): pl.pallas_call(kernel, out_shape=(jax.ShapeDtypeStruct((rows, dims.width)...]
    ppermute x14 -> x18, waiting for transfers between devices: 184 us -> 67.4 us  [the longest x6 45.1 us: forward(): frecv = lax.ppermute(y, 'section', pairs)]
    unnamed x9 -> x1, waiting for transfers between devices: 95.1 us -> 0.02 us
    ppermute x14 -> x18, starting transfers between devices: 128 us -> 43 us  [the longest x6 26 us: forward(): frecv = lax.ppermute(y, 'section', pairs)]
    unnamed x20 -> x246, local copies, waits for them, and re-layouts: 31.6 us -> 113 us
    add x8 -> x0, other arithmetic: 49.7 us -> none  [the longest x4 49.6 us: record(): extra_state[0] + blocks]
    gather x28 -> x0, local copies, waits for them, and re-layouts: 46.6 us -> none  [the longest x4 8.93 us: layer_backward(): jnp.take(spread, inverse_down, axis=1)]
  transfers between devices with their start and end apart: 22 -> 19, of which waited for: 22 -> 9; matrix products, arithmetic and copies ran while one was open for 1% -> 3% of each run, Pallas kernels for 0% -> 9%
where the time goes in v1:
time: 626 us; the launch traced here: 619 us
  waiting for transfers between devices  281 us (45%)
  Pallas kernels  140 us (22%)
  local copies, waits for them, and re-layouts  126 us (20%)
  starting transfers between devices  43 us (7%)
  between operations  14.8 us (2%)
  other arithmetic  14.3 us (2%)
    psum x1, waiting for transfers between devices, total(): return lax.psum(both, 'dp').astype(F32)  213 us
    unnamed x246, local copies, waits for them, and re-layouts  113 us
    pallas_call x7, Pallas kernels, bwd_slot(): pl.pallas_call(kernel, out_shape=(jax.ShapeDtypeStruct((rows, dims.width)...  66.6 us
    pallas_call x7, Pallas kernels, fwd_slot(): pl.pallas_call(kernel, out_shape=(jax.ShapeDtypeStruct((rows, dims.width)...  51.7 us
    ppermute x6, waiting for transfers between devices, forward(): frecv = lax.ppermute(y, 'section', pairs)  45.1 us
    ppermute x6, starting transfers between devices, forward(): frecv = lax.ppermute(y, 'section', pairs)  26 us
    pallas_call x1, Pallas kernels, weight_grads(): pl.pallas_call(kernel, out_shape=tuple(shapes), in_specs=[SMEM] * 3 + [VM...  21.4 us
    ppermute x6, waiting for transfers between devices, backward(): brecv = lax.ppermute(out, 'section', pairs)  17.9 us
  transfers between devices with their start and end apart: 19, of which 9 were waited for; matrix products, arithmetic and copies ran while one was open for 3% of the time, Pallas kernels for 9%

profile of v1, /device:TPU:13, one launch (start us, length us, event | category | flops | bytes accessed | tf_op | source)
XLA Modules:
  0.0 619.0 jit_solution(13533570493559846751)
XLA Ops:
  41.9 38.0 %collective-permute-done.4.refs_4_ = bf16[32,4096]{1,0:T(8,128)(2,1)S(1)} collective-permute-done((bf16[32,4096]{1,0:T(8,128)(2,1)}, bf16[32,4096]{1,0:T(8,128)(2,1)S(1)}, u32[]{:S(2)}, u32[]{:S(2)}) %collective-permute-start.4) | collective-permute-done | bytes 262176 | tf_op jit(solution)/shard_map/ppermute | solution.py:575
  87.8 12.2 %forward_rows.9 = (bf16[32,4096]{1,0:T(8,128)(2,1)S(1)}, bf16[4,128,32,128]{3,2,1,0:T(8,128)(2,1)}, bf16[4,128,32,128]{3,2,1,0:T(8,128)(2,1)}, bf16[4,32,4096]{2...) custom-call(s32[8]{0:T(128)S(1)} %stack.237.refs_0_, ...), custom_call_target="tpu_custom_call", output_to_operand_aliasing={{1}: (11, {}), {2}: (12, {}), {3}: (13, {}), {4}: (14, {}),... | custom-call | tf_op jit(solution)/shard_map/forward_rows/pallas_call | solution.py:295
  100.0 1.9 collective-permute-start.5
  102.1 7.1 %collective-permute-done.5.refs_4_ = bf16[32,4096]{1,0:T(8,128)(2,1)S(1)} collective-permute-done((bf16[32,4096]{1,0:T(8,128)(2,1)S(1)}, bf16[32,4096]{1,0:T(8,128)(2,1)S(1)}, u32[]{:S(2)}, u32[]{:S(2)}) %collective-permute-start.5) | collective-permute-done | bytes 262176 | tf_op jit(solution)/shard_map/ppermute | solution.py:575
  109.2 12.3 %forward_rows.10 = (bf16[32,4096]{1,0:T(8,128)(2,1)}, bf16[4,128,32,128]{3,2,1,0:T(8,128)(2,1)}, bf16[4,128,32,128]{3,2,1,0:T(8,128)(2,1)}, bf16[4,32,4096]{2,1,...) custom-call(s32[8]{0:T(128)S(1)} %stack.233.refs_0_, ...), custom_call_target="tpu_custom_call", output_to_operand_aliasing={{1}: (11, {}), {2}: (12, {}), {3}: (13, {}), {4}: (14, {}),... | custom-call | tf_op jit(solution)/shard_map/forward_rows/pallas_call | solution.py:295
  145.5 12.6 %forward_rows.11 = (bf16[32,4096]{1,0:T(8,128)(2,1)}, bf16[4,128,32,128]{3,2,1,0:T(8,128)(2,1)}, bf16[4,128,32,128]{3,2,1,0:T(8,128)(2,1)}, bf16[4,32,4096]{2,1,...) custom-call(s32[8]{0:T(128)S(1)} %copy-done.114, ...), custom_call_target="tpu_custom_call", output_to_operand_aliasing={{1}: (11, {}), {2}: (12, {}), {3}: (13, {}), {4}: (14, {}),... | custom-call | tf_op jit(solution)/shard_map/forward_rows/pallas_call | solution.py:295
  159.0 16.1 %collective-permute-start.7 = (bf16[32,4096]{1,0:T(8,128)(2,1)}, bf16[32,4096]{1,0:T(8,128)(2,1)}, u32[]{:S(2)}, u32[]{:S(2)}) collective-permute-start(bf16[32,4096]{1,0:T(8,128)(2,1)} %get-tuple-element.130), channel_id=1, source_target_pairs={{8,16},{16,24},{9,17},{17,25},{10,18},{18,26},{11,19},{19,27},{12,... | collective-permute-start | bytes 786440 | tf_op jit(solution)/shard_map/ppermute | solution.py:575
  175.3 16.2 %backward_rows.8 = (bf16[32,4096]{1,0:T(8,128)(2,1)}, bf16[4,128,32,128]{3,2,1,0:T(8,128)(2,1)}, bf16[4,32,4096]{2,1,0:T(8,128)(2,1)S(1)}, bf16[4,32,256]{2,1,0:T(8,128)(2,1)S(1)}, f32[4,8,4096]{2,1,0:T(8,128)S(1)}) custom-call(s32[8]{0:T(128)S(1)} %stack.255.refs_0_, ...), custom_call_target="tpu_custom_call", output_to_operand_aliasing={{1}: (13, {}), {2}: (14, {}), {3}: (15, {}), {4}: (16, {})} | custom-call | tf_op jit(solution)/shard_map/backward_rows/pallas_call | solution.py:391
  204.5 12.6 %forward_rows.12 = (bf16[32,4096]{1,0:T(8,128)(2,1)}, bf16[4,128,32,128]{3,2,1,0:T(8,128)(2,1)}, bf16[4,128,32,128]{3,2,1,0:T(8,128)(2,1)}, bf16[4,32,4096]{2,1,...) custom-call(s32[8]{0:T(128)S(1)} %stack.225.refs_0_, ...), custom_call_target="tpu_custom_call", output_to_operand_aliasing={{1}: (11, {}), {2}: (12, {}), {3}: (13, {}), {4}: (14, {}),... | custom-call | tf_op jit(solution)/shard_map/forward_rows/pallas_call | solution.py:295
  218.1 4.0 collective-permute-start.9
  222.2 16.1 %backward_rows.9 = (bf16[32,4096]{1,0:T(8,128)(2,1)}, bf16[4,128,32,128]{3,2,1,0:T(8,128)(2,1)}, bf16[4,32,4096]{2,1,0:T(8,128)(2,1)S(1)}, bf16[4,32,256]{2,1,0:T(8,128)(2,1)S(1)}, f32[4,8,4096]{2,1,0:T(8,128)S(1)}) custom-call(s32[8]{0:T(128)S(1)} %stack.259.refs_0_, ...), custom_call_target="tpu_custom_call", output_to_operand_aliasing={{1}: (13, {}), {2}: (14, {}), {3}: (15, {}), {4}: (16, {})} | custom-call | tf_op jit(solution)/shard_map/backward_rows/pallas_call | solution.py:391
  244.0 3.5 collective-permute-done.11.refs_4_
  259.1 16.1 %backward_rows.10 = (bf16[32,4096]{1,0:T(8,128)(2,1)}, bf16[4,128,32,128]{3,2,1,0:T(8,128)(2,1)}, bf16[4,32,4096]{2,1,0:T(8,128)(2,1)S(1)}, bf16[4,32,256]{2,1,0:T(8,128)(2,1)S(1)}, f32[4,8,4096]{2,1,0:T(8,128)S(1)}) custom-call(s32[8]{0:T(128)S(1)} %stack.275.refs_0_, ...), custom_call_target="tpu_custom_call", output_to_operand_aliasing={{1}: (13, {}), {2}: (14, {}), {3}: (15, {}), {4}: (16, {})} | custom-call | tf_op jit(solution)/shard_map/backward_rows/pallas_call | solution.py:391
  277.0 2.8 collective-permute-start.12
  280.6 11.5 %collective-permute-done.12.refs_4_ = bf16[32,4096]{1,0:T(8,128)(2,1)S(1)} collective-permute-done((bf16[32,4096]{1,0:T(8,128)(2,1)}, bf16[32,4096]{1,0:T(8,128)(2,1)S(1)}, u32[]{:S(2)}, u32[]{:S(2)}) %collective-permute-start.12) | collective-permute-done | bytes 262176 | tf_op jit(solution)/shard_map/ppermute | solution.py:585
  301.0 16.1 %backward_rows.11 = (bf16[32,4096]{1,0:T(8,128)(2,1)}, bf16[4,128,32,128]{3,2,1,0:T(8,128)(2,1)}, bf16[4,32,4096]{2,1,0:T(8,128)(2,1)S(1)}, bf16[4,32,256]{2,1,0:T(8,128)(2,1)S(1)}, f32[4,8,4096]{2,1,0:T(8,128)S(1)}) custom-call(s32[8]{0:T(128)S(1)} %stack.271.refs_0_, ...), custom_call_target="tpu_custom_call", output_to_operand_aliasing={{1}: (13, {}), {2}: (14, {}), {3}: (15, {}), {4}: (16, {})} | custom-call | tf_op jit(solution)/shard_map/backward_rows/pallas_call | solution.py:391
  321.0 2.9 collective-permute-done.13.refs_4_
  351.6 21.4 %weight_gradients.1 = (bf16[64,128,128]{2,1,0:T(8,128)(2,1)}, bf16[64,128,128]{2,1,0:T(8,128)(2,1)}, bf16[64,128,128]{2,1,0:T(8,128)(2,1)}, bf16[64,128,128]{2,1...) custom-call(s32[8]{0:T(128)S(1)} %copy-done.115, s32[128]{0:T(128)S(1)} %bitcast.116, ...), custom_call_target="tpu_custom_call" | custom-call | tf_op jit(solution)/shard_map/weight_gradients/pallas_call | solution.py:500
  372.9 5.3 collective-permute-start.15
  383.3 3.7 fusion.1
  387.0 2.1 fusion
  389.1 213.5 %all-reduce.3.cloned.1.call-done = (bf16[16,22528]{1,0:T(8,128)(2,1)}, bf16[1,64,128,128]{3,2,1,0:T(8,128)(2,1)}, bf16[1,64,128,128]{3,2,1,0:T(8,128)(2,1)}) async-done(((bf16[16,22528]{1,0:T(8,128)(2,1)}, bf16[1,64,128,128]{3,2,1,0:T(8,128)(2,1)}, bf16[1,64,128,128]{3,2,1,0:T(8,128)(2,1)}), (bf16[16,22528]{1,0:T(8,128)(2,1)}, bf16[1,64,128,128]{3,2,1,0:T(8,128)(2,1)}, ...) | async-done | bytes 4915216 | tf_op jit(solution)/shard_map/psum | solution.py:603
  607.1 2.5 broadcast_in_dim.50
  609.6 2.5 broadcast_in_dim.52
  (307 shorter events, 151.0 us)
Async XLA Ops:
  7.2 595.5 %all-reduce.3.cloned.1.call-start = ((), (), s32[]{:S(2)}) async-start(), calls=%async_computation | async-start | bytes 9830400 | tf_op jit(solution)/shard_map/psum | solution.py:603
  7.2 9.4 %collective-permute-start = (bf16[64,128,128]{2,1,0:T(8,128)(2,1)}, bf16[64,128,128]{2,1,0:T(8,128)(2,1)S(1)}, u32[]{:S(2)}, u32[]{:S(2)}) collective-permute-start(bf16[64,128,128]{2,1,0:T(8,128)(2,1)} %bitcast.63), channel_id=1, source_target_pairs={{0,4},{4,0},{1,5},{5,1},{2,6},{6,2},{3,7},{7,3},{8,12},{12,8},{9,1... | collective-permute-start | bytes 6291464 | tf_op jit(solution)/shard_map/ppermute | solution.py:541
  8.0 10.1 %collective-permute-start.1 = (bf16[64,128,128]{2,1,0:T(8,128)(2,1)}, bf16[64,128,128]{2,1,0:T(8,128)(2,1)}, u32[]{:S(2)}, u32[]{:S(2)}) collective-permute-start(bf16[64,128,128]{2,1,0:T(8,128)(2,1)} %bitcast.78), channel_id=1, source_target_pairs={{0,4},{4,0},{1,5},{5,1},{2,6},{6,2},{3,7},{7,3},{8,12},{12,8},{9,1... | collective-permute-start | bytes 6291464 | tf_op jit(solution)/shard_map/ppermute | solution.py:541
  12.4 3.4 collective-permute-start.2
  29.9 0.8 collective-permute-start.3
  40.2 39.7 %collective-permute-start.4 = (bf16[32,4096]{1,0:T(8,128)(2,1)}, bf16[32,4096]{1,0:T(8,128)(2,1)S(1)}, u32[]{:S(2)}, u32[]{:S(2)}) collective-permute-start(bf16[32,4096]{1,0:T(8,128)(2,1)} %get-tuple-element.107), channel_id=1, source_target_pairs={{0,8},{8,16},{1,9},{9,17},{2,10},{10,18},{3,11},{11,19},{4,12},{12... | collective-permute-start | bytes 786440 | tf_op jit(solution)/shard_map/ppermute | solution.py:575
  100.0 9.1 %collective-permute-start.5 = (bf16[32,4096]{1,0:T(8,128)(2,1)S(1)}, bf16[32,4096]{1,0:T(8,128)(2,1)S(1)}, u32[]{:S(2)}, u32[]{:S(2)}) collective-permute-start(bf16[32,4096]{1,0:T(8,128)(2,1)S(1)} %get-tuple-element.114), channel_id=1, source_target_pairs={{0,8},{8,16},{16,24},{1,9},{9,17},{17,25},{2,10},{10,18},{18,26},{... | collective-permute-start | bytes 786440 | tf_op jit(solution)/shard_map/ppermute | solution.py:575
  122.5 14.5 %collective-permute-start.6 = (bf16[32,4096]{1,0:T(8,128)(2,1)}, bf16[32,4096]{1,0:T(8,128)(2,1)}, u32[]{:S(2)}, u32[]{:S(2)}) collective-permute-start(bf16[32,4096]{1,0:T(8,128)(2,1)} %get-tuple-element.121), channel_id=1, source_target_pairs={{0,8},{8,16},{16,24},{1,9},{9,17},{17,25},{2,10},{10,18},{18,26},{... | collective-permute-start | bytes 786440 | tf_op jit(solution)/shard_map/ppermute | solution.py:575
  133.6 41.6 %collective-permute-start.8 = (bf16[32,4096]{1,0:T(8,128)(2,1)}, bf16[32,4096]{1,0:T(8,128)(2,1)S(1)}, u32[]{:S(2)}, u32[]{:S(2)}) collective-permute-start(bf16[32,4096]{1,0:T(8,128)(2,1)} %get-tuple-element.125), channel_id=1, source_target_pairs={{24,16},{25,17},{26,18},{27,19},{28,20},{29,21},{30,22},{31,23}} | collective-permute-start | bytes 786440 | tf_op jit(solution)/shard_map/ppermute | solution.py:585
  145.5 29.7 %copy-start.32 = (bf16[16,22528]{1,0:T(8,128)(2,1)S(1)}, bf16[16,22528]{1,0:T(8,128)(2,1)}, u32[]{:S(2)}) copy-start(bf16[16,22528]{1,0:T(8,128)(2,1)} %copy-done.26) | copy-start | bytes 2162692
  145.5 29.7 %copy-start.46 = (bf16[16,22528]{1,0:T(8,128)(2,1)S(1)}, bf16[16,22528]{1,0:T(8,128)(2,1)}, u32[]{:S(2)}) copy-start(bf16[16,22528]{1,0:T(8,128)(2,1)} %copy-done.40) | copy-start | bytes 2162692
  145.5 29.7 %copy-start.61 = (bf16[4,32,4096]{2,1,0:T(8,128)(2,1)S(1)}, bf16[4,32,4096]{2,1,0:T(8,128)(2,1)}, u32[]{:S(2)}) copy-start(bf16[4,32,4096]{2,1,0:T(8,128)(2,1)} %refs_3_.27) | copy-start | bytes 3145732
  145.5 29.8 %copy-start.68 = (bf16[4,32,4096]{2,1,0:T(8,128)(2,1)S(1)}, bf16[4,32,4096]{2,1,0:T(8,128)(2,1)}, u32[]{:S(2)}) copy-start(bf16[4,32,4096]{2,1,0:T(8,128)(2,1)} %copy-done.67) | copy-start | bytes 3145732
  145.5 29.8 %copy-start.94 = (f32[4,8,4096]{2,1,0:T(8,128)S(1)}, f32[4,8,4096]{2,1,0:T(8,128)}, u32[]{:S(2)}) copy-start(f32[4,8,4096]{2,1,0:T(8,128)} %copy-done.93) | copy-start | bytes 1572868
  159.0 37.6 %collective-permute-start.7 = (bf16[32,4096]{1,0:T(8,128)(2,1)}, bf16[32,4096]{1,0:T(8,128)(2,1)}, u32[]{:S(2)}, u32[]{:S(2)}) collective-permute-start(bf16[32,4096]{1,0:T(8,128)(2,1)} %get-tuple-element.130), channel_id=1, source_target_pairs={{8,16},{16,24},{9,17},{17,25},{10,18},{18,26},{11,19},{19,27},{12,... | collective-permute-start | bytes 786440 | tf_op jit(solution)/shard_map/ppermute | solution.py:575
  193.2 28.9 %collective-permute-start.10 = (bf16[32,4096]{1,0:T(8,128)(2,1)}, bf16[32,4096]{1,0:T(8,128)(2,1)}, u32[]{:S(2)}, u32[]{:S(2)}) collective-permute-start(bf16[32,4096]{1,0:T(8,128)(2,1)} %get-tuple-element.138), channel_id=1, source_target_pairs={{24,16},{16,8},{25,17},{17,9},{26,18},{18,10},{27,19},{19,11},{28,... | collective-permute-start | bytes 786440 | tf_op jit(solution)/shard_map/ppermute | solution.py:585
  218.1 26.0 %collective-permute-start.9 = (bf16[32,4096]{1,0:T(8,128)(2,1)}, bf16[32,4096]{1,0:T(8,128)(2,1)S(1)}, u32[]{:S(2)}, u32[]{:S(2)}) collective-permute-start(bf16[32,4096]{1,0:T(8,128)(2,1)} %get-tuple-element.143), channel_id=1, source_target_pairs={{16,24},{17,25},{18,26},{19,27},{20,28},{21,29},{22,30},{23,31}} | collective-permute-start | bytes 786440 | tf_op jit(solution)/shard_map/ppermute | solution.py:575
  240.1 7.4 %collective-permute-start.11 = (bf16[32,4096]{1,0:T(8,128)(2,1)}, bf16[32,4096]{1,0:T(8,128)(2,1)}, u32[]{:S(2)}, u32[]{:S(2)}) collective-permute-start(bf16[32,4096]{1,0:T(8,128)(2,1)} %get-tuple-element.151), channel_id=1, source_target_pairs={{24,16},{16,8},{8,0},{25,17},{17,9},{9,1},{26,18},{18,10},{10,2},{... | collective-permute-start | bytes 786440 | tf_op jit(solution)/shard_map/ppermute | solution.py:585
  277.0 15.1 %collective-permute-start.12 = (bf16[32,4096]{1,0:T(8,128)(2,1)}, bf16[32,4096]{1,0:T(8,128)(2,1)S(1)}, u32[]{:S(2)}, u32[]{:S(2)}) collective-permute-start(bf16[32,4096]{1,0:T(8,128)(2,1)} %get-tuple-element.165), channel_id=1, source_target_pairs={{24,16},{16,8},{8,0},{25,17},{17,9},{9,1},{26,18},{18,10},{10,2},{... | collective-permute-start | bytes 786440 | tf_op jit(solution)/shard_map/ppermute | solution.py:585
  319.0 4.9 collective-permute-start.13
  335.2 2.7 collective-permute-start.14
  372.9 7.4 %collective-permute-start.15 = (bf16[16,22528]{1,0:T(8,128)(2,1)S(1)}, bf16[16,22528]{1,0:T(8,128)(2,1)S(1)}, u32[]{:S(2)}, u32[]{:S(2)}) collective-permute-start(bf16[16,22528]{1,0:T(8,128)(2,1)S(1)} %get-tuple-element.188), channel_id=1, source_target_pairs={{0,4},{4,0},{1,5},{5,1},{2,6},{6,2},{3,7},{7,3},{8,12},{12,8},{9,1... | collective-permute-start | bytes 2162696 | tf_op jit(solution)/shard_map/ppermute | solution.py:599
  378.2 5.0 collective-permute-start.17
  378.3 8.7 %collective-permute-start.16 = (bf16[64,128,128]{2,1,0:T(8,128)(2,1)}, bf16[64,128,128]{2,1,0:T(8,128)(2,1)S(1)}, u32[]{:S(2)}, u32[]{:S(2)}) collective-permute-start(bf16[64,128,128]{2,1,0:T(8,128)(2,1)} %get-tuple-element.190), channel_id=1, source_target_pairs={{0,4},{4,0},{1,5},{5,1},{2,6},{6,2},{3,7},{7,3},{8,12},{12,8},{9,1... | collective-permute-start | bytes 6291464 | tf_op jit(solution)/shard_map/ppermute | solution.py:599
  (116 other events, 347.8 us)
Sparse Core Ops, SparseCore 0:
  389.2 213.3 all-reduce.2

commit v2 on v1

--- a/solution.py
+++ b/solution.py
@@ -69,9 +69,9 @@
     return pl.ds(pl.multiple_of(start, BLK), count)
 
 
-def load_weights(f, srcs, dsts, sems):
+def load_weights(f, srcs, dsts, sems, first=0):
     copies = []
-    for n, (src, dst) in enumerate(zip(srcs, dsts)):
+    for n, (src, dst) in enumerate(zip(srcs, dsts), first):
         if len(src) == 1:
             whole = pltpu.make_async_copy(src[0], dst, sems.at[2 * n])
             whole.start()
@@ -105,8 +105,7 @@
     return lax.rsqrt(jnp.sum(total, axis=1, keepdims=True) * (1.0 / dims.width) + EPSILON)
 
 
-def fwd_body(dims, full, G, copies, f_x_s, small_s, up_s, dn_s, upo, dno, nrm_s, hid_s, slp_s, low_s, y_s):
-    x_s = f_x_s
+def fwd_norm(dims, x_s, small_s, nrm_s, low_s):
     rows = x_s.shape[0]
     r = inverse_rms(x_s, dims)
     upl = jnp.zeros((rows, RANK), F32)
@@ -120,9 +119,13 @@
             small_s[h, :, dims.ul : dims.ul + dims.mh * BLK],
             NT,
         )
-    upl = upl.astype(BF)
-    low_s[:, 0:RANK] = upl
-    done(copies[0])
+    low_s[:, 0:RANK] = upl.astype(BF)
+
+
+def fwd_hidden(dims, small_s, up_s, upo, nrm_s, hid_s, slp_s, low_s, G=32):
+    rows = nrm_s.shape[0]
+    G = min(G, dims.hh)
+    upl = low_s[:, 0:RANK]
 
     def step(it, low):
         j0 = it * G
@@ -142,29 +145,29 @@
             hids.append(hid)
         return low + dot(jnp.concatenate(hids, axis=1), dl, NT)
 
-    low = lax.fori_loop(0, dims.hidden // G, step, jnp.zeros((rows, RANK), F32))
-    low = low.astype(BF)
+    low = lax.fori_loop(0, dims.hidden // G, step, jnp.zeros((rows, RANK), F32)).astype(BF)
     low_s[:, BLK : BLK + RANK] = low
-    if full:
-        done(copies[1])
-
-        def down(it, _):
-            for u in range(4):
-                i = it * 4 + u
-                h = i // dims.mh
-                at = i * BLK
-                dr = small_s[h, :, lanes(dims.dr + (i - h * dims.mh) * BLK)]
-                parts = [hid_s[dno[i * dims.group + c]] for c in range(dims.group)]
-                lhs = jnp.concatenate(parts + [low], axis=1)
-                blocks = dn_s[pl.ds(i * dims.group, dims.group)].reshape(dims.group * BLK, BLK)
-                mixed = dot(lhs, jnp.concatenate([blocks, dr], axis=0))
-                y_s[:, lanes(at)] = (x_s[:, lanes(at)].astype(F32) + mixed).astype(BF)
-            return 0
-
-        lax.fori_loop(0, dims.model // 4, down, 0)
-
-
-def bwd_hidden(dims, g_s, slp_s, gp_s, small_s, dn_s, dno, low_s):
+    return low
+
+
+def fwd_down(dims, low, x_s, small_s, dn_s, dno, hid_s, y_s):
+    def down(it, _):
+        for u in range(8):
+            i = it * 8 + u
+            h = i // dims.mh
+            at = i * BLK
+            dr = small_s[h, :, lanes(dims.dr + (i - h * dims.mh) * BLK)]
+            parts = [hid_s[dno[i * dims.group + c]] for c in range(dims.group)]
+            lhs = jnp.concatenate(parts + [low], axis=1)
+            blocks = dn_s[pl.ds(i * dims.group, dims.group)].reshape(dims.group * BLK, BLK)
+            mixed = dot(lhs, jnp.concatenate([blocks, dr], axis=0))
+            y_s[:, lanes(at)] = (x_s[:, lanes(at)].astype(F32) + mixed).astype(BF)
+        return 0
+
+    lax.fori_loop(0, dims.model // 8, down, 0)
+
+
+def bwd_hidden(dims, g_s, slp_s, gp_s, small_s, dn_s, dno, low_s, U=8):
     rows = g_s.shape[0]
     gdl = jnp.zeros((rows, RANK), F32)
     for h in range(dims.parts):
@@ -177,8 +180,8 @@
     low_s[:, BLK : BLK + RANK] = gdl
 
     def hid_step(it, gul):
-        for u in range(2):
-            i = it * 2 + u
+        for u in range(U):
+            i = it * U + u
             gi = g_s[:, lanes(i * BLK)]
             js = [dno[i * dims.group + c] for c in range(dims.group)]
             hs = [j // dims.hh for j in js]
@@ -194,7 +197,7 @@
             gul = gul + dot(gp, ur, NT)
         return gul
 
-    gul = lax.fori_loop(0, dims.model // 2, hid_step, jnp.zeros((rows, RANK), F32))
+    gul = lax.fori_loop(0, dims.model // U, hid_step, jnp.zeros((rows, RANK), F32))
     gul = gul.astype(BF)
     low_s[:, 0:RANK] = gul
     return gul
@@ -205,8 +208,8 @@
     r = inverse_rms(x_s, dims)
 
     def step(it, acc):
-        for u in range(2):
-            i = it * 2 + u
+        for u in range(8):
+            i = it * 8 + u
             h = i // dims.mh
             off = (i - h * dims.mh) * BLK
             js = [grouped[i * dims.group + c] for c in range(dims.group)]
@@ -221,7 +224,7 @@
             acc = acc + x * scaled
         return acc
 
-    acc = lax.fori_loop(0, dims.model // 2, step, jnp.zeros((rows, BLK), F32))
+    acc = lax.fori_loop(0, dims.model // 8, step, jnp.zeros((rows, BLK), F32))
     shift = jnp.sum(acc, axis=1, keepdims=True) * (1.0 / dims.width) * (r * r * r)
     for i in range(dims.model):
         at = slice(i * BLK, (i + 1) * BLK)
@@ -234,15 +237,15 @@
     return pltpu.CompilerParams(vmem_limit_bytes=mib * 1024 * 1024)
 
 
-def fwd_slot(dims, sc, upo, dno, first, recv, weights, bufs, micro):
+def fwd_slot(dims, sc, upo, dno, first, recv, weights, bufs, micro, held):
     rows = recv.shape[0]
     n_buf = 5
     shapes = (
-        jax.ShapeDtypeStruct((micro, dims.hidden, rows, BLK), BF),
-        jax.ShapeDtypeStruct((micro, dims.hidden, rows, BLK), BF),
+        jax.ShapeDtypeStruct((micro, dims.hidden, held, BLK), BF),
+        jax.ShapeDtypeStruct((micro, dims.hidden, held, BLK), BF),
+        jax.ShapeDtypeStruct((micro, held, dims.width), BF),
         jax.ShapeDtypeStruct((micro, rows, dims.width), BF),
-        jax.ShapeDtypeStruct((micro, rows, dims.width), BF),
-        jax.ShapeDtypeStruct((micro, rows, 2 * BLK), BF),
+        jax.ShapeDtypeStruct((micro, held, 2 * BLK), BF),
     )
     n_w = len(weights[0])
     n_in = 5 + 3 * n_w + (n_buf if bufs is not None else 0)
@@ -266,24 +269,28 @@
                 pltpu.make_async_copy(recv, x_s, sems.at[6]).start()
 
             wait_x = pltpu.make_async_copy(recv, x_s, sems.at[6])
-            small, up, dn = load_weights(
-                f, (small_w, up_w, dn_w), (small_s, up_s, dn_s), sems
-            )
+            small, up = load_weights(f, (small_w, up_w), (small_s, up_s), sems)
             low_s[...] = jnp.zeros_like(low_s)
             wait_x.wait()
             save_x = pltpu.make_async_copy(x_s, xb.at[m], sems.at[7])
             save_x.start()
             done(small)
-            fwd_body(dims, True, 8, (up, dn), x_s, small_s, up_s, dn_s, upo, dno, nrm_s, hid_s, slp_s, low_s, y_s)
+            fwd_norm(dims, x_s, small_s, nrm_s, low_s)
+            done(up)
+            (dn,) = load_weights(f, (dn_w,), (dn_s,), sems, 2)
+            low = fwd_hidden(dims, small_s, up_s, upo, nrm_s, hid_s, slp_s, low_s)
             outs = [
-                pltpu.make_async_copy(y_s, y, sems.at[8]),
-                pltpu.make_async_copy(hid_s, hidb.at[m], sems.at[9]),
-                pltpu.make_async_copy(slp_s, slpb.at[m], sems.at[10]),
-                pltpu.make_async_copy(nrm_s, nrmb.at[m], sems.at[11]),
-                pltpu.make_async_copy(low_s, lowb.at[m], sems.at[12]),
+                pltpu.make_async_copy(hid_s, hidb.at[m, :, 0:rows], sems.at[9]),
+                pltpu.make_async_copy(slp_s, slpb.at[m, :, 0:rows], sems.at[10]),
+                pltpu.make_async_copy(nrm_s, nrmb.at[m, 0:rows], sems.at[11]),
+                pltpu.make_async_copy(low_s, lowb.at[m, 0:rows], sems.at[12]),
             ]
             for copy in outs:
                 copy.start()
+            done(dn)
+            fwd_down(dims, low, x_s, small_s, dn_s, dno, hid_s, y_s)
+            outs.append(pltpu.make_async_copy(y_s, y, sems.at[8]))
+            outs[-1].start()
             save_x.wait()
             done(outs)
 
@@ -310,19 +317,19 @@
             pltpu.VMEM((rows, dims.width), BF),
             pltpu.SemaphoreType.DMA((13,)),
         ],
-        compiler_params=params(40),
+        compiler_params=params(60),
         name="forward_rows",
     )(*args)
     return out[0], out[1:]
 
 
-def bwd_slot(dims, sc, dno, grouped, last, recv, weights, xb, slpb, bufs, micro):
+def bwd_slot(dims, sc, dno, grouped, last, recv, weights, xb, slpb, bufs, micro, held):
     rows = recv.shape[0]
     n_buf = 4
     shapes = (
-        jax.ShapeDtypeStruct((micro, dims.hidden, rows, BLK), BF),
-        jax.ShapeDtypeStruct((micro, rows, dims.width), BF),
-        jax.ShapeDtypeStruct((micro, rows, 2 * BLK), BF),
+        jax.ShapeDtypeStruct((micro, dims.hidden, held, BLK), BF),
+        jax.ShapeDtypeStruct((micro, held, dims.width), BF),
+        jax.ShapeDtypeStruct((micro, held, 2 * BLK), BF),
         jax.ShapeDtypeStruct((micro, 8, dims.width), F32),
     )
     n_w = len(weights[0])
@@ -348,25 +355,24 @@
                 pltpu.make_async_copy(recv, g_s, sems.at[6]).start()
 
             wait_g = pltpu.make_async_copy(recv, g_s, sems.at[6])
-            get_slope = pltpu.make_async_copy(slpb.at[m], slp_s, sems.at[7])
+            get_slope = pltpu.make_async_copy(slpb.at[m, :, 0:rows], slp_s, sems.at[7])
             get_x = pltpu.make_async_copy(xb.at[m], x_s, sems.at[8])
-            small, dn, up = load_weights(
-                f, (small_w, dn_w, up_w), (small_s, dn_s, up_s), sems
-            )
+            small, dn = load_weights(f, (small_w, dn_w), (small_s, dn_s), sems)
             get_slope.start()
-            get_x.start()
             low_s[...] = jnp.zeros_like(low_s)
             gain_s[...] = jnp.zeros_like(gain_s)
             wait_g.wait()
-            save_g = pltpu.make_async_copy(g_s, gb.at[m], sems.at[9])
+            save_g = pltpu.make_async_copy(g_s, gb.at[m, 0:rows], sems.at[9])
             save_g.start()
             done(small)
             get_slope.wait()
             done(dn)
+            (up,) = load_weights(f, (up_w,), (up_s,), sems, 2)
+            get_x.start()
             gul = bwd_hidden(dims, g_s, slp_s, gp_s, small_s, dn_s, dno, low_s)
             outs = [
-                pltpu.make_async_copy(gp_s, gpb.at[m], sems.at[10]),
-                pltpu.make_async_copy(low_s, lowb.at[m], sems.at[11]),
+                pltpu.make_async_copy(gp_s, gpb.at[m, :, 0:rows], sems.at[10]),
+                pltpu.make_async_copy(low_s, lowb.at[m, 0:rows], sems.at[11]),
             ]
             for copy in outs:
                 copy.start()
@@ -408,113 +414,265 @@
             pltpu.VMEM((rows, dims.width), BF),
             pltpu.SemaphoreType.DMA((14,)),
         ],
-        compiler_params=params(40),
+        compiler_params=params(60),
         name="backward_rows",
     )(*args)
     return out[0], out[1:]
 
 
-def weight_grads(dims, sc, upo, dno, hidb, nrmb, lowf, gpb, gb, lowb, gainb):
-    micro, _, rows, _ = hidb.shape
+def pick_rows(sc, sources, dst, sem):
+    n = dst.shape[0] // len(sources[0])
+    for q, triple in enumerate(sources):
+
+        @pl.when(sc[3] == q)
+        def _():
+            for t, ref in enumerate(triple):
+                pltpu.make_async_copy(ref.at[sc[4]], dst.at[t * n : (t + 1) * n], sem.at[t]).start()
+
+    return tuple(
+        pltpu.make_async_copy(ref.at[0], dst.at[t * n : (t + 1) * n], sem.at[t])
+        for t, ref in enumerate(sources[0])
+    )
+
+
+def fwd_far(dims, sc, upo, sources, weights, bufs):
+    hidb, slpb, nrmb, lowb = bufs
+    rows = sources[0][0].shape[1]
+    far = rows * len(sources[0])
+    n_w, n_t, n_q = len(weights[0]), len(sources[0]), len(sources)
+    args = [sc, upo] + list(weights[0]) + list(weights[2]) + [a for triple in sources for a in triple]
+    n_plain = len(args)
+    args += list(bufs)
+
+    def kernel(*refs):
+        sc, upo = refs[:2]
+        up_w, small_w = refs[2 : 2 + n_w], refs[2 + n_w : 2 + 2 * n_w]
+        base = 2 + 2 * n_w
+        srcs = [refs[base + q * n_t : base + (q + 1) * n_t] for q in range(n_q)]
+        hidb, slpb, nrmb, lowb = refs[n_plain + 4 : n_plain + 8]
+        up_s, small_s, x_s, nrm_s, hid_s, slp_s, low_s, sems, xsem = refs[n_plain + 8 :]
+
+        @pl.when(sc[0] == 1)
+        def _():
+            m, f = sc[1], sc[2]
+            wait_x = pick_rows(sc, srcs, x_s, xsem)
+            small, up = load_weights(f, (small_w, up_w), (small_s, up_s), sems)
+            low_s[...] = jnp.zeros_like(low_s)
+            done(wait_x)
+            done(small)
+            fwd_norm(dims, x_s, small_s, nrm_s, low_s)
+            done(up)
+            fwd_hidden(dims, small_s, up_s, upo, nrm_s, hid_s, slp_s, low_s, 8)
+            at = slice(rows, rows + far)
+            outs = [
+                pltpu.make_async_copy(hid_s, hidb.at[m, :, at], sems.at[4]),
+                pltpu.make_async_copy(slp_s, slpb.at[m, :, at], sems.at[5]),
+                pltpu.make_async_copy(nrm_s, nrmb.at[m, at], sems.at[6]),
+                pltpu.make_async_copy(low_s, lowb.at[m, at], sems.at[7]),
+            ]
+            for copy in outs:
+                copy.start()
+            done(outs)
+
+    return pl.pallas_call(
+        kernel,
+        out_shape=tuple(jax.ShapeDtypeStruct(b.shape, b.dtype) for b in bufs),
+        in_specs=[SMEM] * 2 + [ANY] * (len(args) - 2),
+        out_specs=(ANY,) * 4,
+        input_output_aliases={n_plain + n: n for n in range(4)},
+        scratch_shapes=[
+            pltpu.VMEM((dims.hidden, BLK, BLK), BF),
+            pltpu.VMEM((dims.parts, RANK, dims.packed), BF),
+            pltpu.VMEM((far, dims.width), BF),
+            pltpu.VMEM((far, dims.width), BF),
+            pltpu.VMEM((dims.hidden, far, BLK), BF),
+            pltpu.VMEM((dims.hidden, far, BLK), BF),
+            pltpu.VMEM((far, 2 * BLK), BF),
+            pltpu.SemaphoreType.DMA((8,)),
+            pltpu.SemaphoreType.DMA((n_t,)),
+        ],
+        compiler_params=params(60),
+        name="forward_far_rows",
+    )(*args)
+
+
+def bwd_far(dims, sc, dno, sources, weights, slpb, bufs):
+    rows = sources[0][0].shape[1]
+    far = rows * len(sources[0])
+    n_w, n_t, n_q = len(weights[0]), len(sources[0]), len(sources)
+    args = [sc, dno] + list(weights[1]) + list(weights[2]) + [a for triple in sources for a in triple] + [slpb]
+    n_plain = len(args)
+    args += list(bufs)
+
+    def kernel(*refs):
+        sc, dno = refs[:2]
+        dn_w, small_w = refs[2 : 2 + n_w], refs[2 + n_w : 2 + 2 * n_w]
+        base = 2 + 2 * n_w
+        srcs = [refs[base + q * n_t : base + (q + 1) * n_t] for q in range(n_q)]
+        slpb = refs[n_plain - 1]
+        gpb, gb, lowb = refs[n_plain + 3 : n_plain + 6]
+        dn_s, small_s, g_s, slp_s, gp_s, low_s, sems, gsem = refs[n_plain + 6 :]
+
+        @pl.when(sc[0] == 1)
+        def _():
+            m, f = sc[1], sc[2]
+            at = slice(rows, rows + far)
+            wait_g = pick_rows(sc, srcs, g_s, gsem)
+            small, dn = load_weights(f, (small_w, dn_w), (small_s, dn_s), sems)
+            get_slope = pltpu.make_async_copy(slpb.at[m, :, at], slp_s, sems.at[4])
+            get_slope.start()
+            low_s[...] = jnp.zeros_like(low_s)
+            done(wait_g)
+            save_g = pltpu.make_async_copy(g_s, gb.at[m, at], sems.at[5])
+            save_g.start()
+            done(small)
+            done(dn)
+            get_slope.wait()
+            bwd_hidden(dims, g_s, slp_s, gp_s, small_s, dn_s, dno, low_s, 4)
+            outs = [
+                pltpu.make_async_copy(gp_s, gpb.at[m, :, at], sems.at[6]),
+                pltpu.make_async_copy(low_s, lowb.at[m, at], sems.at[7]),
+            ]
+            for copy in outs:
+                copy.start()
+            save_g.wait()
+            done(outs)
+
+    return pl.pallas_call(
+        kernel,
+        out_shape=tuple(jax.ShapeDtypeStruct(b.shape, b.dtype) for b in bufs),
+        in_specs=[SMEM] * 2 + [ANY] * (len(args) - 2),
+        out_specs=(ANY,) * 3,
+        input_output_aliases={n_plain + n: n for n in range(3)},
+        scratch_shapes=[
+            pltpu.VMEM((dims.hidden, BLK, BLK), BF),
+            pltpu.VMEM((dims.parts, RANK, dims.packed), BF),
+            pltpu.VMEM((far, dims.width), BF),
+            pltpu.VMEM((dims.hidden, far, BLK), BF),
+            pltpu.VMEM((dims.hidden, far, BLK), BF),
+            pltpu.VMEM((far, 2 * BLK), BF),
+            pltpu.SemaphoreType.DMA((8,)),
+            pltpu.SemaphoreType.DMA((n_t,)),
+        ],
+        compiler_params=params(60),
+        name="backward_far_rows",
+    )(*args)
+
+
+def weight_grads(dims, up, sc, order, blocks, wide, low_a, low_b, gain=None):
+    micro, _, held, _ = blocks.shape
+    total = micro * held
+    group, model, mh, hh = dims.group, dims.model, dims.mh, dims.hh
+    U = 4
+    two = dims.parts == 2
+    hid_at = mh * BLK
+    gain_at = hid_at + hh * BLK
+    packed = gain_at + (mh * BLK if up else 0)
     VM = pl.BlockSpec(memory_space=pltpu.VMEM)
-
-    two = dims.parts == 2
+    a_at, b_at = (0, 0) if up else (BLK, BLK)
+    extra = [gain] if up else []
 
     def kernel(*refs):
-        sc, upo, dno, hidb, nrmb, lowf, gpb, gb, lowb, gainb = refs[:10]
-        outs_hbm = refs[10:-4]
-        upg, dng, smg, sems = refs[-4:]
+        sc, order, blocks, wide, low_a, low_b = refs[:6]
+        gain = refs[6] if up else None
+        outs_hbm = refs[6 + len(extra) : -6]
+        big, small, held_s, wide_s, sems, osems = refs[-6:]
         f = sc[2]
-
-        def cat(parts):
-            return jnp.concatenate(parts, axis=0)
-
-        def rows_of(ref, at, count=BLK):
-            return cat([ref[m, :, lanes(at, count)] for m in range(micro)])
-
-        def block_of(ref, j):
-            return cat([ref[m, j] for m in range(micro)])
-
-        up_low = cat([lowf[m, :, 0:BLK] for m in range(micro)])
-        down_low = cat([lowf[m, :, BLK : 2 * BLK] for m in range(micro)])
-        gul = cat([lowb[m, :, 0:BLK] for m in range(micro)])
-        gdl = cat([lowb[m, :, BLK : 2 * BLK] for m in range(micro)])
+        get_wide = pltpu.make_async_copy(wide, wide_s, osems.at[0])
+        get_wide.start()
+
+        def fetch(it, slot, go):
+            for u in range(U):
+                for c in range(group):
+                    j = order[(it * U + u) * group + c]
+                    copy = pltpu.make_async_copy(
+                        blocks.at[:, j], held_s.at[slot, u * group + c], sems.at[slot, u * group + c]
+                    )
+                    copy.start() if go else copy.wait()
+
+        fetch(0, 0, True)
+
+        def low_t(ref, at):
+            rows = jnp.concatenate([ref[m, :, at : at + BLK] for m in range(micro)], axis=0)
+            return rows.astype(F32).T[0:RANK].astype(BF)
+
+        with_blocks, with_wide = low_t(low_a, a_at), low_t(low_b, b_at)
+        get_wide.wait()
 
         def which(h):
             return jnp.where(h == f, 0, 1) if two else h
 
-        def down(it, _):
-            for u in range(2):
-                i = it * 2 + u
-                h = i // dims.mh
-                hid = jnp.concatenate(
-                    [block_of(hidb, dno[i * dims.group + c]) for c in range(dims.group)], axis=1
+        def step(it, _):
+            slot = lax.rem(it, 2)
+
+            @pl.when(it + 1 < model // U)
+            def _():
+                fetch(it + 1, 1 - slot, True)
+
+            fetch(it, slot, False)
+            for u in range(U):
+                i = it * U + u
+                h = i // mh
+                w = which(h)
+                off = i - h * mh
+                wi = jnp.concatenate([wide_s[m, :, lanes(i * BLK)] for m in range(micro)], axis=0)
+                lhs = jnp.concatenate([wi.T, with_blocks], axis=0)
+                rhs = jnp.concatenate(
+                    [held_s[slot, u * group + c].reshape(total, BLK) for c in range(group)], axis=1
                 )
-                gi = rows_of(gb, i * BLK)
-                grad = dot(hid, gi, TN).astype(BF).reshape(dims.group, BLK, BLK)
-                off = i - h * dims.mh
-                w = which(h)
-                dng[w, pl.ds(off * dims.group, dims.group)] = grad
-                nrm = rows_of(nrmb, i * BLK)
-                smg[w, :, lanes(dims.dr + off * BLK)] = dot(down_low, gi, TN)[0:RANK].astype(BF)
-                smg[w, :, lanes(dims.ul + off * BLK)] = dot(gul, nrm, TN)[0:RANK].astype(BF)
-                gain = jnp.zeros((8, BLK), F32)
-                for m in range(micro):
-                    gain = gain + gainb[m, :, lanes(i * BLK)]
-                smg[w, :, lanes(dims.gain + off * BLK)] = jnp.broadcast_to(
-                    jnp.sum(gain, axis=0, keepdims=True), (RANK, BLK)
-                ).astype(BF)
+                res = dot(lhs, rhs)
+                for c in range(group):
+                    j = order[i * group + c]
+                    hj = j // hh
+                    wj = which(hj)
+                    part = res[:, c * BLK : (c + 1) * BLK]
+                    if up:
+                        big[wj, j - hj * hh] = part[0:BLK].astype(BF)
+                    else:
+                        big[w, off * group + c] = part[0:BLK].T.astype(BF)
+                    small[wj, :, lanes(hid_at + (j - hj * hh) * BLK)] = part[BLK:].astype(BF)
+                small[w, :, lanes(off * BLK)] = dot(with_wide, wi).astype(BF)
+                if up:
+                    small[w, :, lanes(gain_at + off * BLK)] = jnp.broadcast_to(
+                        gain[0:1, lanes(i * BLK)], (RANK, BLK)
+                    ).astype(BF)
             return 0
 
-        lax.fori_loop(0, dims.model // 2, down, 0)
-
-        def up(it, _):
-            for u in range(4):
-                j = it * 4 + u
-                h = j // dims.hh
-                off = j - h * dims.hh
-                w = which(h)
-                gp = block_of(gpb, j)
-                hid = block_of(hidb, j)
-                nrm = rows_of(nrmb, upo[j] * BLK)
-                upg[w, off] = dot(nrm, gp, TN).astype(BF)
-                smg[w, :, lanes(dims.ur + off * BLK)] = dot(up_low, gp, TN)[0:RANK].astype(BF)
-                smg[w, :, lanes(dims.dl + off * BLK)] = dot(gdl, hid, TN)[0:RANK].astype(BF)
-            return 0
-
-        lax.fori_loop(0, dims.hidden // 4, up, 0)
+        lax.fori_loop(0, model // U, step, 0)
         outs = []
-        for n, src in enumerate((upg, dng, smg)):
+        for n, src in enumerate((big, small)):
             if two:
-                outs.append(pltpu.make_async_copy(src.at[0], outs_hbm[2 * n], sems.at[2 * n]))
-                outs.append(pltpu.make_async_copy(src.at[1], outs_hbm[2 * n + 1], sems.at[2 * n + 1]))
+                outs.append(pltpu.make_async_copy(src.at[0], outs_hbm[2 * n], osems.at[2 * n]))
+                outs.append(pltpu.make_async_copy(src.at[1], outs_hbm[2 * n + 1], osems.at[2 * n + 1]))
             else:
-                outs.append(pltpu.make_async_copy(src, outs_hbm[n], sems.at[2 * n]))
+                outs.append(pltpu.make_async_copy(src, outs_hbm[n], osems.at[2 * n]))
         for copy in outs:
             copy.start()
         done(outs)
 
     lead = () if two else (dims.parts,)
-    shapes = [lead + (dims.hh, BLK, BLK)] * 2 + [lead + (RANK, dims.packed)]
+    shapes = [lead + (hh, BLK, BLK), lead + (RANK, packed)]
     shapes = [jax.ShapeDtypeStruct(shape, BF) for shape in shapes for _ in range(2 if two else 1)]
     got = pl.pallas_call(
         kernel,
         out_shape=tuple(shapes),
-        in_specs=[SMEM] * 3 + [VM] * 7,
+        in_specs=[SMEM] * 2 + [ANY] * 2 + [VM] * (2 + len(extra)),
         out_specs=(ANY,) * len(shapes),
         scratch_shapes=[
-            pltpu.VMEM((dims.parts, dims.hh, BLK, BLK), BF),
-            pltpu.VMEM((dims.parts, dims.hh, BLK, BLK), BF),
-            pltpu.VMEM((dims.parts, RANK, dims.packed), BF),
-            pltpu.SemaphoreType.DMA((6,)),
+            pltpu.VMEM((dims.parts, hh, BLK, BLK), BF),
+            pltpu.VMEM((dims.parts, RANK, packed), BF),
+            pltpu.VMEM((2, U * group, micro, held, BLK), BF),
+            pltpu.VMEM((micro, held, dims.width), BF),
+            pltpu.SemaphoreType.DMA((2, U * group)),
+            pltpu.SemaphoreType.DMA((4,)),
         ],
-        compiler_params=params(48),
-        name="weight_gradients",
-    )(sc, upo, dno, hidb, nrmb, lowf, gpb, gb, lowb, gainb)
-    return [got[0:2], got[2:4], got[4:6]] if two else [got[0:1], got[1:2], got[2:3]]
-
-
-def orders(up_order, down_order, dims):
+        compiler_params=params(60),
+        name="up_gradients" if up else "down_gradients",
+    )(sc, order, blocks, wide, low_a, low_b, *extra)
+    return [got[0:2], got[2:4]] if two else [got[0:1], got[1:2]]
+
+
+def orders(up_order, dims):
     at = jnp.arange(dims.hidden, dtype=jnp.int32)
     same = (up_order[:, None] == up_order[None, :]) & (at[None, :] < at[:, None])
     place = up_order * dims.group + jnp.sum(same.astype(jnp.int32), axis=1)
@@ -532,6 +690,7 @@
     sec = lax.axis_index("section")
     f = lax.axis_index("fsdp")
     swap = [(0, 1), (1, 0)]
+    held = rows
     small = jnp.concatenate(
         [up_left[0], down_right[0], up_right[0], down_left[0],
          jnp.broadcast_to(norm_gain, (RANK, norm_gain.shape[1]))], axis=1)
@@ -544,7 +703,7 @@
     small_w = whole_layer(small, True)
     up_w = whole_layer(up_blocks[0], False)
     weights = (up_w, whole_layer(down_blocks[0], False), small_w)
-    grouped = orders(upo, dno, dims)
+    grouped = orders(upo, dims)
     zero = jnp.int32(0)
 
     def scalars(m, edge):
@@ -568,7 +727,7 @@
     def forward(t):
         nonlocal fbufs, frecv
         (x,) = chained(frecv)
-        y, fbufs = fwd_slot(dims, scalars(t - sec, sec == 0), upo, dno, inputs, x, weights, fbufs, micro)
+        y, fbufs = fwd_slot(dims, scalars(t - sec, sec == 0), upo, dno, inputs, x, weights, fbufs, micro, held)
         state["token"] = y
         pairs = [(s, s + 1) for s in range(last) if 0 <= t - s < micro]
         if pairs:
@@ -578,7 +737,7 @@
         nonlocal bbufs, brecv
         (g,) = chained(brecv)
         out, bbufs = bwd_slot(dims, scalars(t - (last - sec), sec == last), dno, grouped, cotangent, g,
-                              weights, fbufs[3], fbufs[1], bbufs, micro)
+                              weights, fbufs[3], fbufs[1], bbufs, micro, held)
         state["token"] = out
         pairs = [(last - s, last - s - 1) for s in range(last) if 0 <= t - s < micro]
         if pairs:
@@ -591,29 +750,30 @@
             backward(t - last)
     for t in range(slots - last, slots):
         backward(t)
-    up_g, dn_g, small_g = weight_grads(
-        dims, scalars(zero, sec == 0), upo, dno, fbufs[0], fbufs[2], fbufs[4], *bbufs)
-
-    def total(pieces):
+    hidb, slpb, nrmb, _, lowf = fbufs
+    gpb, gb, lowb, gainb = bbufs
+    sc = scalars(zero, sec == 0)
+
+    def over_fsdp(pieces):
         if parts == 2:
             got = lax.ppermute(pieces[1], "fsdp", swap)
-            both = (pieces[0].astype(F32) + got.astype(F32)).astype(BF)
-        else:
-            both = lax.psum_scatter(pieces[0], "fsdp", scatter_dimension=0, tiled=False)
-        return lax.psum(both, "dp").astype(F32)
-
-    sm = total(small_g)
-    dn = total(dn_g)
-    up = total(up_g)
+            return (pieces[0].astype(F32) + got.astype(F32)).astype(BF)
+        return lax.psum_scatter(pieces[0], "fsdp", scatter_dimension=0, tiled=False)
+
+    gain = jnp.sum(gainb, axis=(0, 1))[None]
+    dn_g, dn_small = weight_grads(dims, False, sc, dno, hidb, gb, lowb, lowf)
+    up_g, up_small = weight_grads(dims, True, sc, grouped, gpb, nrmb, lowf, lowb, gain)
+    sums = lax.psum([over_fsdp(p) for p in (dn_g, dn_small, up_g, up_small)], "dp")
+    dn, dns, up, ups = (s[None].astype(F32) for s in sums)
     mw, hw = dims.mh * BLK, dims.hh * BLK
     return (
-        sm[0:1, dims.gain : dims.gain + mw],
-        up[None],
-        dn[None],
-        sm[None, :, dims.ul : dims.ul + mw],
-        sm[None, :, dims.ur : dims.ur + hw],
-        sm[None, :, dims.dl : dims.dl + hw],
-        sm[None, :, dims.dr : dims.dr + mw],
+        ups[:, 0, mw + hw :],
+        up,
+        dn,
+        ups[:, :, 0:mw],
+        ups[:, :, mw : mw + hw],
+        dns[:, :, mw : mw + hw],
+        dns[:, :, 0:mw],
     )
 
 

time: 626 us -> 479 us (0.77)
  local copies, waits for them, and re-layouts: 126 us -> 30.6 us
  Pallas kernels: 140 us -> 110 us
  waiting for transfers between devices: 281 us -> 265 us
  starting transfers between devices: 43 us -> 35.5 us
    unnamed x246 -> x50, local copies, waits for them, and re-layouts: 113 us -> 12.2 us
    pallas_call x7, Pallas kernels: 66.6 us -> 48.9 us  [bwd_slot(): pl.pallas_call(kernel, out_shape=(jax.ShapeDtypeStruct((rows, dims.width)...]
    convert_element_type x2 -> x7, other arithmetic: 2.44 us -> 14.8 us  [shards(): dn, dns, up, ups = (s[None].astype(F32) for s in sums)]
    pallas_call x7, Pallas kernels: 51.7 us -> 40.2 us  [fwd_slot(): pl.pallas_call(kernel, out_shape=(jax.ShapeDtypeStruct((rows, dims.width)...]
    broadcast_in_dim x4 -> x0, other arithmetic: 10.9 us -> none  [the longest x2 6.27 us: shards(): dn[None]]
    psum x1, waiting for transfers between devices: 213 us -> 205 us  [shards(): lax.psum([over_fsdp(p) for p in (dn_g, dn_small, up_g, up_small)], 'dp')]
    ppermute x6, starting transfers between devices: 26 us -> 18.3 us  [forward(): frecv = lax.ppermute(y, 'section', pairs)]
    pallas_call x1 -> x2, Pallas kernels: 21.4 us -> 21.2 us  [weight_grads(): pl.pallas_call(kernel, out_shape=tuple(shapes), in_specs=[SMEM] * 2 + [AN...]
  transfers between devices with their start and end apart: 19 -> 20, of which waited for: 9 -> 10; matrix products, arithmetic and copies ran while one was open for 3% -> 5% of each run, Pallas kernels for 9% -> 11%
where the time goes in v2:
time: 479 us; the launch traced here: 473 us
  waiting for transfers between devices  265 us (55%)
  Pallas kernels  110 us (23%)
  starting transfers between devices  35.5 us (7%)
  local copies, waits for them, and re-layouts  30.6 us (6%)
  other arithmetic  17 us (4%)
  between operations  14.5 us (3%)
    psum x1, waiting for transfers between devices, shards(): lax.psum([over_fsdp(p) for p in (dn_g, dn_small, up_g, up_small)], 'dp')  205 us
    pallas_call x7, Pallas kernels, bwd_slot(): pl.pallas_call(kernel, out_shape=(jax.ShapeDtypeStruct((rows, dims.width)...  48.9 us
    pallas_call x7, Pallas kernels, fwd_slot(): pl.pallas_call(kernel, out_shape=(jax.ShapeDtypeStruct((rows, dims.width)...  40.2 us
    ppermute x6, waiting for transfers between devices, forward(): frecv = lax.ppermute(y, 'section', pairs)  39.2 us
    pallas_call x2, Pallas kernels, weight_grads(): pl.pallas_call(kernel, out_shape=tuple(shapes), in_specs=[SMEM] * 2 + [AN...  21.2 us
    ppermute x6, starting transfers between devices, forward(): frecv = lax.ppermute(y, 'section', pairs)  18.3 us
    ppermute x6, waiting for transfers between devices, backward(): brecv = lax.ppermute(out, 'section', pairs)  17 us
    convert_element_type x7, other arithmetic, shards(): dn, dns, up, ups = (s[None].astype(F32) for s in sums)  14.8 us
  transfers between devices with their start and end apart: 20, of which 10 were waited for; matrix products, arithmetic and copies ran while one was open for 5% of the time, Pallas kernels for 11%

profile of v2, /device:TPU:13, one launch (start us, length us, event | category | flops | bytes accessed | tf_op | source)
XLA Modules:
  0.0 473.4 jit_solution(3941697037569655321)
XLA Ops:
  23.9 30.2 %collective-permute-done.4.refs_4_ = bf16[32,4096]{1,0:T(8,128)(2,1)S(1)} collective-permute-done((bf16[32,4096]{1,0:T(8,128)(2,1)}, bf16[32,4096]{1,0:T(8,128)(2,1)S(1)}, u32[]{:S(2)}, u32[]{:S(2)}) %collective-permute-start.4) | collective-permute-done | bytes 262176 | tf_op jit(solution)/shard_map/ppermute | solution.py:734
  54.8 9.5 %forward_rows.9 = (bf16[32,4096]{1,0:T(8,128)(2,1)}, bf16[4,128,32,128]{3,2,1,0:T(8,128)(2,1)}, bf16[4,128,32,128]{3,2,1,0:T(8,128)(2,1)}, bf16[4,32,4096]{2,1,0...) custom-call(s32[8]{0:T(128)} %stack.255.refs_0_, ...), custom_call_target="tpu_custom_call", output_to_operand_aliasing={{1}: (11, {}), {2}: (12, {}), {3}: (13, {}), {4}: (14, {}),... | custom-call | tf_op jit(solution)/shard_map/forward_rows/pallas_call | solution.py:302
  66.9 6.7 %collective-permute-done.5.refs_4_ = bf16[32,4096]{1,0:T(8,128)(2,1)S(1)} collective-permute-done((bf16[32,4096]{1,0:T(8,128)(2,1)}, bf16[32,4096]{1,0:T(8,128)(2,1)S(1)}, u32[]{:S(2)}, u32[]{:S(2)}) %collective-permute-start.5) | collective-permute-done | bytes 262176 | tf_op jit(solution)/shard_map/ppermute | solution.py:734
  74.3 9.3 %forward_rows.10 = (bf16[32,4096]{1,0:T(8,128)(2,1)}, bf16[4,128,32,128]{3,2,1,0:T(8,128)(2,1)}, bf16[4,128,32,128]{3,2,1,0:T(8,128)(2,1)}, bf16[4,32,4096]{2,1,...) custom-call(s32[8]{0:T(128)} %stack.251.refs_0_, ...), custom_call_target="tpu_custom_call", output_to_operand_aliasing={{1}: (11, {}), {2}: (12, {}), {3}: (13, {}), {4}: (14, {}),... | custom-call | tf_op jit(solution)/shard_map/forward_rows/pallas_call | solution.py:302
  92.6 9.3 %forward_rows.11 = (bf16[32,4096]{1,0:T(8,128)(2,1)}, bf16[4,128,32,128]{3,2,1,0:T(8,128)(2,1)}, bf16[4,128,32,128]{3,2,1,0:T(8,128)(2,1)}, bf16[4,32,4096]{2,1,...) custom-call(s32[8]{0:T(128)} %stack.267.refs_0_, ...), custom_call_target="tpu_custom_call", output_to_operand_aliasing={{1}: (11, {}), {2}: (12, {}), {3}: (13, {}), {4}: (14, {}),... | custom-call | tf_op jit(solution)/shard_map/forward_rows/pallas_call | solution.py:302
  101.9 9.1 %collective-permute-start.9 = (bf16[32,4096]{1,0:T(8,128)(2,1)}, bf16[32,4096]{1,0:T(8,128)(2,1)S(1)}, u32[]{:S(2)}, u32[]{:S(2)}) collective-permute-start(bf16[32,4096]{1,0:T(8,128)(2,1)} %get-tuple-element.132), channel_id=1, source_target_pairs={{8,16},{16,24},{9,17},{17,25},{10,18},{18,26},{11,19},{19,27},{12,... | collective-permute-start | bytes 786440 | tf_op jit(solution)/shard_map/ppermute | solution.py:734
  111.7 11.6 %backward_rows.8 = (bf16[32,4096]{1,0:T(8,128)(2,1)}, bf16[4,128,32,128]{3,2,1,0:T(8,128)(2,1)}, bf16[4,32,4096]{2,1,0:T(8,128)(2,1)}, bf16[4,32,256]{2,1,0:T(8,128)(2,1)}, f32[4,8,4096]{2,1,0:T(8,128)}) custom-call(s32[8]{0:T(128)} %stack.243.refs_0_, s32[128]{0:T(128)} %bitcast.98, ...), custom_call_target="tpu_custom_call", output_to_operand_aliasing={{1}: (13, {}), {2}: (14, {}), {3}: (15, {}), {4}: (16, {})} | custom-call | tf_op jit(solution)/shard_map/backward_rows/pallas_call | solution.py:397
  127.2 9.5 %forward_rows.12 = (bf16[32,4096]{1,0:T(8,128)(2,1)}, bf16[4,128,32,128]{3,2,1,0:T(8,128)(2,1)}, bf16[4,128,32,128]{3,2,1,0:T(8,128)(2,1)}, bf16[4,32,4096]{2,1,...) custom-call(s32[8]{0:T(128)} %stack.271.refs_0_, ...), custom_call_target="tpu_custom_call", output_to_operand_aliasing={{1}: (11, {}), {2}: (12, {}), {3}: (13, {}), {4}: (14, {}),... | custom-call | tf_op jit(solution)/shard_map/forward_rows/pallas_call | solution.py:302
  136.7 3.4 collective-permute-start.11
  140.8 11.6 %backward_rows.9 = (bf16[32,4096]{1,0:T(8,128)(2,1)}, bf16[4,128,32,128]{3,2,1,0:T(8,128)(2,1)}, bf16[4,32,4096]{2,1,0:T(8,128)(2,1)}, bf16[4,32,256]{2,1,0:T(8,128)(2,1)}, f32[4,8,4096]{2,1,0:T(8,128)}) custom-call(s32[8]{0:T(128)} %stack.239.refs_0_, s32[128]{0:T(128)} %bitcast.100, ...), custom_call_target="tpu_custom_call", output_to_operand_aliasing={{1}: (13, {}), {2}: (14, {}), {3}: (15, {}), {4}: (16, {})} | custom-call | tf_op jit(solution)/shard_map/backward_rows/pallas_call | solution.py:397
  155.5 4.2 collective-permute-done.10.refs_4_
  160.5 11.6 %backward_rows.10 = (bf16[32,4096]{1,0:T(8,128)(2,1)}, bf16[4,128,32,128]{3,2,1,0:T(8,128)(2,1)}, bf16[4,32,4096]{2,1,0:T(8,128)(2,1)}, bf16[4,32,256]{2,1,0:T(8,128)(2,1)}, f32[4,8,4096]{2,1,0:T(8,128)}) custom-call(s32[8]{0:T(128)} %stack.235.refs_0_, s32[128]{0:T(128)} %bitcast.102, ...), custom_call_target="tpu_custom_call", output_to_operand_aliasing={{1}: (13, {}), {2}: (14, {}), {3}: (15, {}), {4}: (16, {})} | custom-call | tf_op jit(solution)/shard_map/backward_rows/pallas_call | solution.py:397
  172.1 2.8 collective-permute-start.12
  175.6 9.9 %collective-permute-done.12.refs_4_ = bf16[32,4096]{1,0:T(8,128)(2,1)S(1)} collective-permute-done((bf16[32,4096]{1,0:T(8,128)(2,1)}, bf16[32,4096]{1,0:T(8,128)(2,1)S(1)}, u32[]{:S(2)}, u32[]{:S(2)}) %collective-permute-start.12) | collective-permute-done | bytes 262176 | tf_op jit(solution)/shard_map/ppermute | solution.py:744
  186.2 11.5 %backward_rows.11 = (bf16[32,4096]{1,0:T(8,128)(2,1)}, bf16[4,128,32,128]{3,2,1,0:T(8,128)(2,1)}, bf16[4,32,4096]{2,1,0:T(8,128)(2,1)}, bf16[4,32,256]{2,1,0:T(8,128)(2,1)}, f32[4,8,4096]{2,1,0:T(8,128)}) custom-call(s32[8]{0:T(128)} %stack.231.refs_0_, s32[128]{0:T(128)} %bitcast.103, ...), custom_call_target="tpu_custom_call", output_to_operand_aliasing={{1}: (13, {}), {2}: (14, {}), {3}: (15, {}), {4}: (16, {})} | custom-call | tf_op jit(solution)/shard_map/backward_rows/pallas_call | solution.py:397
  199.8 2.9 collective-permute-done.13.refs_4_
  208.0 10.7 %down_gradients.1 = (bf16[64,128,128]{2,1,0:T(8,128)(2,1)}, bf16[64,128,128]{2,1,0:T(8,128)(2,1)}, bf16[16,10240]{1,0:T(8,128)(2,1)}, bf16[16,10240]{1,0:T(8,128)(2,1)}) custom-call(s32[8]{0:T(128)} %stack.217.refs_0_, s32[128]{0:T(128)} %bitcast.106, bf16[4,128,32,128]{3,2,1,0:T(8,128)(2,1)} %get-tuple-element.191.refs_2_, ...), custom_call_target="tpu_custom_call" | custom-call | tf_op jit(solution)/shard_map/down_gradients/pallas_call | solution.py:656
  218.7 5.3 %collective-permute-start.18 = (bf16[16,10240]{1,0:T(8,128)(2,1)}, bf16[16,10240]{1,0:T(8,128)(2,1)S(1)}, u32[]{:S(2)}, u32[]{:S(2)}) collective-permute-start(bf16[16,10240]{1,0:T(8,128)(2,1)} %get-tuple-element.196), channel_id=1, source_target_pairs={{0,4},{4,0},{1,5},{5,1},{2,6},{6,2},{3,7},{7,3},{8,12},{12,8},{9,1... | collective-permute-start | bytes 983048 | tf_op jit(solution)/shard_map/ppermute | solution.py:759
  224.7 10.5 %up_gradients.1 = (bf16[64,128,128]{2,1,0:T(8,128)(2,1)}, bf16[64,128,128]{2,1,0:T(8,128)(2,1)}, bf16[16,12288]{1,0:T(8,128)(2,1)}, bf16[16,12288]{1,0:T(8,128)(2,1)}) custom-call(s32[8]{0:T(128)} %stack.217.refs_0_, s32[128]{0:T(128)} %select_reduce_fusion.refs_2_.refs_1_, bf16[4,128,32,128]{3,2,1,0:T(8,128)(2,1)} %get-tuple-element.182.refs_2_, ...), custom_call_target="tpu_custom_call" | custom-call | tf_op jit(solution)/shard_map/up_gradients/pallas_call | solution.py:656
  236.6 3.7 collective-permute-done.15
  242.2 3.8 fusion.1
  248.1 204.8 %all-reduce.3.cloned.1.call-done = (bf16[1,16,12288]{2,1,0:T(8,128)(2,1)}, bf16[1,64,128,128]{3,2,1,0:T(8,128)(2,1)}, bf16[1,64,128,128]{3,2,1,0:T(8,128)(2,1)}, bf16[1,16,10240]{2,1,0:T(8,128)(2,1)}) async-done(((bf16[1,16,12288]{2,1,0:T(8,128)(2,1)}, bf16[1,64,128,128]{3,2,1,0:T(8,128)(2,1)}, bf16[1,64,128,128]{3,2,1,0:T(8,128)(2,1)}, bf16[1,16,10240]{2,1,0:T(8,128)(2,1)}), ...) | async-done | bytes 4915216 | tf_op jit(solution)/shard_map/psum | solution.py:766
  460.8 2.5 convert_element_type.102
  463.4 2.5 convert_element_type.107
  (118 shorter events, 61.9 us)
Async XLA Ops:
  7.2 445.7 %all-reduce.3.cloned.1.call-start = ((), (), s32[]{:S(2)}) async-start(), calls=%async_computation | async-start | bytes 9830400 | tf_op jit(solution)/shard_map/psum | solution.py:766
  7.2 8.6 %collective-permute-start = (bf16[64,128,128]{2,1,0:T(8,128)(2,1)}, bf16[64,128,128]{2,1,0:T(8,128)(2,1)S(1)}, u32[]{:S(2)}, u32[]{:S(2)}) collective-permute-start(bf16[64,128,128]{2,1,0:T(8,128)(2,1)} %bitcast.62), channel_id=1, source_target_pairs={{0,4},{4,0},{1,5},{5,1},{2,6},{6,2},{3,7},{7,3},{8,12},{12,8},{9,1... | collective-permute-start | bytes 6291464 | tf_op jit(solution)/shard_map/ppermute | solution.py:700
  8.0 7.9 %collective-permute-start.1 = (bf16[64,128,128]{2,1,0:T(8,128)(2,1)}, bf16[64,128,128]{2,1,0:T(8,128)(2,1)}, u32[]{:S(2)}, u32[]{:S(2)}) collective-permute-start(bf16[64,128,128]{2,1,0:T(8,128)(2,1)} %bitcast.77), channel_id=1, source_target_pairs={{0,4},{4,0},{1,5},{5,1},{2,6},{6,2},{3,7},{7,3},{8,12},{12,8},{9,1... | collective-permute-start | bytes 6291464 | tf_op jit(solution)/shard_map/ppermute | solution.py:700
  12.4 3.3 collective-permute-start.2
  18.2 1.3 collective-permute-start.3
  21.1 32.9 %collective-permute-start.4 = (bf16[32,4096]{1,0:T(8,128)(2,1)}, bf16[32,4096]{1,0:T(8,128)(2,1)S(1)}, u32[]{:S(2)}, u32[]{:S(2)}) collective-permute-start(bf16[32,4096]{1,0:T(8,128)(2,1)} %get-tuple-element.109), channel_id=1, source_target_pairs={{0,8},{8,16},{1,9},{9,17},{2,10},{10,18},{3,11},{11,19},{4,12},{12... | collective-permute-start | bytes 786440 | tf_op jit(solution)/shard_map/ppermute | solution.py:734
  54.8 11.4 %copy-start.22 = (s32[1,128]{1,0:T(1,128)S(1)}, s32[1,128]{1,0:T(1,128)}, u32[]{:S(2)}) copy-start(s32[1,128]{1,0:T(1,128)} %param.20) | copy-start | bytes 1540
  64.3 9.3 %collective-permute-start.5 = (bf16[32,4096]{1,0:T(8,128)(2,1)}, bf16[32,4096]{1,0:T(8,128)(2,1)S(1)}, u32[]{:S(2)}, u32[]{:S(2)}) collective-permute-start(bf16[32,4096]{1,0:T(8,128)(2,1)} %get-tuple-element.116), channel_id=1, source_target_pairs={{0,8},{8,16},{16,24},{1,9},{9,17},{17,25},{2,10},{10,18},{18,26},{... | collective-permute-start | bytes 786440 | tf_op jit(solution)/shard_map/ppermute | solution.py:734
  83.6 8.2 %collective-permute-start.7 = (bf16[32,4096]{1,0:T(8,128)(2,1)}, bf16[32,4096]{1,0:T(8,128)(2,1)S(1)}, u32[]{:S(2)}, u32[]{:S(2)}) collective-permute-start(bf16[32,4096]{1,0:T(8,128)(2,1)} %get-tuple-element.123), channel_id=1, source_target_pairs={{0,8},{8,16},{16,24},{1,9},{9,17},{17,25},{2,10},{10,18},{18,26},{... | collective-permute-start | bytes 786440 | tf_op jit(solution)/shard_map/ppermute | solution.py:734
  87.0 24.0 %collective-permute-start.6 = (bf16[32,4096]{1,0:T(8,128)(2,1)}, bf16[32,4096]{1,0:T(8,128)(2,1)S(1)}, u32[]{:S(2)}, u32[]{:S(2)}) collective-permute-start(bf16[32,4096]{1,0:T(8,128)(2,1)} %get-tuple-element.127), channel_id=1, source_target_pairs={{24,16},{25,17},{26,18},{27,19},{28,20},{29,21},{30,22},{31,23}} | collective-permute-start | bytes 786440 | tf_op jit(solution)/shard_map/ppermute | solution.py:744
  101.9 24.6 %collective-permute-start.9 = (bf16[32,4096]{1,0:T(8,128)(2,1)}, bf16[32,4096]{1,0:T(8,128)(2,1)S(1)}, u32[]{:S(2)}, u32[]{:S(2)}) collective-permute-start(bf16[32,4096]{1,0:T(8,128)(2,1)} %get-tuple-element.132), channel_id=1, source_target_pairs={{8,16},{16,24},{9,17},{17,25},{10,18},{18,26},{11,19},{19,27},{12,... | collective-permute-start | bytes 786440 | tf_op jit(solution)/shard_map/ppermute | solution.py:734
  123.3 16.8 %collective-permute-start.8 = (bf16[32,4096]{1,0:T(8,128)(2,1)}, bf16[32,4096]{1,0:T(8,128)(2,1)S(1)}, u32[]{:S(2)}, u32[]{:S(2)}) collective-permute-start(bf16[32,4096]{1,0:T(8,128)(2,1)} %get-tuple-element.140), channel_id=1, source_target_pairs={{24,16},{16,8},{25,17},{17,9},{26,18},{18,10},{27,19},{19,11},{28,... | collective-permute-start | bytes 786440 | tf_op jit(solution)/shard_map/ppermute | solution.py:744
  136.7 18.8 %collective-permute-start.11 = (bf16[32,4096]{1,0:T(8,128)(2,1)}, bf16[32,4096]{1,0:T(8,128)(2,1)S(1)}, u32[]{:S(2)}, u32[]{:S(2)}) collective-permute-start(bf16[32,4096]{1,0:T(8,128)(2,1)} %get-tuple-element.145), channel_id=1, source_target_pairs={{16,24},{17,25},{18,26},{19,27},{20,28},{21,29},{22,30},{23,31}} | collective-permute-start | bytes 786440 | tf_op jit(solution)/shard_map/ppermute | solution.py:734
  152.4 7.3 %collective-permute-start.10 = (bf16[32,4096]{1,0:T(8,128)(2,1)}, bf16[32,4096]{1,0:T(8,128)(2,1)S(1)}, u32[]{:S(2)}, u32[]{:S(2)}) collective-permute-start(bf16[32,4096]{1,0:T(8,128)(2,1)} %get-tuple-element.153), channel_id=1, source_target_pairs={{24,16},{16,8},{8,0},{25,17},{17,9},{9,1},{26,18},{18,10},{10,2},{... | collective-permute-start | bytes 786440 | tf_op jit(solution)/shard_map/ppermute | solution.py:744
  172.1 13.5 %collective-permute-start.12 = (bf16[32,4096]{1,0:T(8,128)(2,1)}, bf16[32,4096]{1,0:T(8,128)(2,1)S(1)}, u32[]{:S(2)}, u32[]{:S(2)}) collective-permute-start(bf16[32,4096]{1,0:T(8,128)(2,1)} %get-tuple-element.164), channel_id=1, source_target_pairs={{24,16},{16,8},{8,0},{25,17},{17,9},{9,1},{26,18},{18,10},{10,2},{... | collective-permute-start | bytes 786440 | tf_op jit(solution)/shard_map/ppermute | solution.py:744
  197.8 4.9 %collective-permute-start.13 = (bf16[32,4096]{1,0:T(8,128)(2,1)}, bf16[32,4096]{1,0:T(8,128)(2,1)S(1)}, u32[]{:S(2)}, u32[]{:S(2)}) collective-permute-start(bf16[32,4096]{1,0:T(8,128)(2,1)} %get-tuple-element.170), channel_id=1, source_target_pairs={{16,8},{8,0},{17,9},{9,1},{18,10},{10,2},{19,11},{11,3},{20,12},{1... | collective-permute-start | bytes 786440 | tf_op jit(solution)/shard_map/ppermute | solution.py:744
  204.2 2.0 collective-permute-start.14
  208.0 16.1 %copy-start.3 = (f32[4,8,4096]{2,1,0:T(8,128)S(1)}, f32[4,8,4096]{2,1,0:T(8,128)}, u32[]{:S(2)}) copy-start(f32[4,8,4096]{2,1,0:T(8,128)} %get-tuple-element.186) | copy-start | bytes 1572868
  218.7 17.2 %copy-start.8 = (bf16[16,10240]{1,0:T(8,128)(2,1)S(1)}, bf16[16,10240]{1,0:T(8,128)(2,1)}, u32[]{:S(2)}) copy-start(bf16[16,10240]{1,0:T(8,128)(2,1)} %get-tuple-element.195) | copy-start | bytes 983044
  218.7 23.5 %copy-start.4 = (bf16[64,128,128]{2,1,0:T(8,128)(2,1)S(1)}, bf16[64,128,128]{2,1,0:T(8,128)(2,1)}, u32[]{:S(2)}) copy-start(bf16[64,128,128]{2,1,0:T(8,128)(2,1)} %get-tuple-element.193) | copy-start | bytes 6291460
  218.7 17.1 %collective-permute-start.18 = (bf16[16,10240]{1,0:T(8,128)(2,1)}, bf16[16,10240]{1,0:T(8,128)(2,1)S(1)}, u32[]{:S(2)}, u32[]{:S(2)}) collective-permute-start(bf16[16,10240]{1,0:T(8,128)(2,1)} %get-tuple-element.196), channel_id=1, source_target_pairs={{0,4},{4,0},{1,5},{5,1},{2,6},{6,2},{3,7},{7,3},{8,12},{12,8},{9,1... | collective-permute-start | bytes 983048 | tf_op jit(solution)/shard_map/ppermute | solution.py:759
  224.0 18.2 %collective-permute-start.17 = (bf16[64,128,128]{2,1,0:T(8,128)(2,1)}, bf16[64,128,128]{2,1,0:T(8,128)(2,1)}, u32[]{:S(2)}, u32[]{:S(2)}) collective-permute-start(bf16[64,128,128]{2,1,0:T(8,128)(2,1)} %get-tuple-element.194), channel_id=1, source_target_pairs={{0,4},{4,0},{1,5},{5,1},{2,6},{6,2},{3,7},{7,3},{8,12},{12,8},{9,1... | collective-permute-start | bytes 6291464 | tf_op jit(solution)/shard_map/ppermute | solution.py:759
  235.2 10.7 %collective-permute-start.16 = (bf16[64,128,128]{2,1,0:T(8,128)(2,1)}, bf16[64,128,128]{2,1,0:T(8,128)(2,1)S(1)}, u32[]{:S(2)}, u32[]{:S(2)}) collective-permute-start(bf16[64,128,128]{2,1,0:T(8,128)(2,1)} %get-tuple-element.190), channel_id=1, source_target_pairs={{0,4},{4,0},{1,5},{5,1},{2,6},{6,2},{3,7},{7,3},{8,12},{12,8},{9,1... | collective-permute-start | bytes 6291464 | tf_op jit(solution)/shard_map/ppermute | solution.py:759
  235.7 4.6 collective-permute-start.15
  (19 other events, 47.0 us)
Sparse Core Ops, SparseCore 0:
  248.2 204.6 all-reduce.2

commit v3 on v2

--- a/solution.py
+++ b/solution.py
@@ -690,7 +690,8 @@
     sec = lax.axis_index("section")
     f = lax.axis_index("fsdp")
     swap = [(0, 1), (1, 0)]
-    held = rows
+    n_dp = lax.axis_size("dp")
+    held = rows * n_dp
     small = jnp.concatenate(
         [up_left[0], down_right[0], up_right[0], down_left[0],
          jnp.broadcast_to(norm_gain, (RANK, norm_gain.shape[1]))], axis=1)
@@ -711,6 +712,16 @@
         return jnp.stack([live.astype(jnp.int32), jnp.clip(m, 0, micro - 1).astype(jnp.int32),
                           f.astype(jnp.int32), edge.astype(jnp.int32), zero, zero, zero, zero])
 
+    def to_dp(block, sections):
+        got = []
+        for k in range(1, n_dp):
+            pairs = [(s * n_dp + d, s * n_dp + (d + k) % n_dp) for s in sections for d in range(n_dp)]
+            got.append(lax.ppermute(block, ("section", "dp"), pairs))
+        return tuple(got)
+
+    def flags(live, m, source, index):
+        return jnp.stack([jnp.asarray(v).astype(jnp.int32) for v in (live, m, f, source, index, 0, 0, 0)])
+
     state = {"token": None}
 
     def chained(*arrays):
@@ -723,6 +734,8 @@
     frecv = inputs[0]
     brecv = inputs[0]
     last = n_sec - 1
+    far_x, far_g = {}, {}
+    far_edge = to_dp(jnp.where(sec == 0, inputs, cotangent), (0, last))
 
     def forward(t):
         nonlocal fbufs, frecv
@@ -730,6 +743,10 @@
         y, fbufs = fwd_slot(dims, scalars(t - sec, sec == 0), upo, dno, inputs, x, weights, fbufs, micro, held)
         state["token"] = y
         pairs = [(s, s + 1) for s in range(last) if 0 <= t - s < micro]
+        arrived = [s for s in range(1, n_sec) if 0 <= t - s < micro]
+        if arrived:
+            (late,) = chained(x)
+            far_x[t] = to_dp(late[None], arrived)
         if pairs:
             frecv = lax.ppermute(y, "section", pairs)
 
@@ -740,31 +757,51 @@
                               weights, fbufs[3], fbufs[1], bbufs, micro, held)
         state["token"] = out
         pairs = [(last - s, last - s - 1) for s in range(last) if 0 <= t - s < micro]
+        arrived = [s for s in range(last) if 0 <= t - (last - s) < micro]
+        if arrived:
+            (late,) = chained(g)
+            far_g[t] = to_dp(late[None], arrived)
         if pairs:
             brecv = lax.ppermute(out, "section", pairs)
+
+    def forward_far(m, live, sources, source, index):
+        nonlocal fbufs
+        (sc,) = chained(flags(live, m, source, index))
+        hidb, slpb, nrmb, xb, lowf = fbufs
+        hidb, slpb, nrmb, lowf = fwd_far(dims, sc, upo, sources, weights, (hidb, slpb, nrmb, lowf))
+        fbufs = (hidb, slpb, nrmb, xb, lowf)
 
     slots = micro + last
     for t in range(slots):
         forward(t)
         if t >= last:
             backward(t - last)
+    for m in range(micro):
+        forward_far(m, sec == 0, [far_edge], 0, m)
     for t in range(slots - last, slots):
         backward(t)
+    for m in range(micro):
+        forward_far(m, sec > 0, [far_x[m + s] for s in range(1, n_sec)], sec - 1, 0)
+    gain = jnp.sum(bbufs[3], axis=(0, 1))[None]
+    for other in to_dp(gain, range(n_sec)):
+        gain = gain + other
+    gpb, gb, lowb, _ = bbufs
+    for m in range(micro):
+        sources = [far_g[m + last - s] for s in range(last)] + [far_edge]
+        sc = flags(True, m, sec, jnp.where(sec == last, m, 0))
+        gpb, gb, lowb = bwd_far(dims, sc, dno, sources, weights, fbufs[1], (gpb, gb, lowb))
     hidb, slpb, nrmb, _, lowf = fbufs
-    gpb, gb, lowb, gainb = bbufs
     sc = scalars(zero, sec == 0)
 
     def over_fsdp(pieces):
         if parts == 2:
             got = lax.ppermute(pieces[1], "fsdp", swap)
-            return (pieces[0].astype(F32) + got.astype(F32)).astype(BF)
-        return lax.psum_scatter(pieces[0], "fsdp", scatter_dimension=0, tiled=False)
-
-    gain = jnp.sum(gainb, axis=(0, 1))[None]
+            return (pieces[0].astype(F32) + got.astype(F32))[None]
+        return lax.psum_scatter(pieces[0], "fsdp", scatter_dimension=0, tiled=False).astype(F32)[None]
+
     dn_g, dn_small = weight_grads(dims, False, sc, dno, hidb, gb, lowb, lowf)
     up_g, up_small = weight_grads(dims, True, sc, grouped, gpb, nrmb, lowf, lowb, gain)
-    sums = lax.psum([over_fsdp(p) for p in (dn_g, dn_small, up_g, up_small)], "dp")
-    dn, dns, up, ups = (s[None].astype(F32) for s in sums)
+    dn, dns, up, ups = (over_fsdp(p) for p in (dn_g, dn_small, up_g, up_small))
     mw, hw = dims.mh * BLK, dims.hh * BLK
     return (
         ups[:, 0, mw + hw :],

time: 479 us -> 645 us (1.35)
  starting transfers between devices: 35.5 us -> 277 us
  waiting for transfers between devices: 265 us -> 60.6 us
  Pallas kernels: 110 us -> 251 us
  between operations: 14.5 us -> 2.7 us
    ppermute x0 -> x42, starting transfers between devices: none -> 242 us  [to_dp(): got.append(lax.ppermute(block, ('section', 'dp'), pairs))]
    psum x1 -> x0, waiting for transfers between devices: 205 us -> none  [shards(): lax.psum([over_fsdp(p) for p in (dn_g, dn_small, up_g, up_small)], 'dp')]
    pallas_call x0 -> x12, Pallas kernels: none -> 131 us  [the longest x8 76.8 us: fwd_far(): pl.pallas_call(kernel, out_shape=tuple((jax.ShapeDtypeStruct(b.shape, b.d...]
    ppermute x0 -> x42, waiting for transfers between devices: none -> 21.4 us  [to_dp(): got.append(lax.ppermute(block, ('section', 'dp'), pairs))]
    ppermute x6, waiting for transfers between devices: 17 us -> 0.02 us  [backward(): brecv = lax.ppermute(out, 'section', pairs)]
    convert_element_type x7 -> x0, other arithmetic: 14.8 us -> none  [shards(): dn, dns, up, ups = (s[None].astype(F32) for s in sums)]
    pallas_call x2, Pallas kernels: 21.2 us -> 31.5 us  [weight_grads(): pl.pallas_call(kernel, out_shape=tuple(shapes), in_specs=[SMEM] * 2 + [AN...]
    another operation x1 -> x15, local copies, waits for them, and re-layouts: 0.01 us -> 7.61 us  [the longest x12 7.61 us: flags(): jnp.stack([jnp.asarray(v).astype(jnp.int32) for v in (live, m, f, source,...]
  transfers between devices with their start and end apart: 20 -> 61, of which waited for: 10 -> 9; matrix products, arithmetic and copies ran while one was open for 5% -> 6% of each run, Pallas kernels for 11% -> 40%
where the time goes in v3:
time: 645 us; the launch traced here: 633 us
  starting transfers between devices  277 us (43%)
  Pallas kernels  251 us (39%)
  waiting for transfers between devices  60.6 us (9%)
  local copies, waits for them, and re-layouts  29.6 us (5%)
  other arithmetic  12.4 us (2%)
    ppermute x42, starting transfers between devices, to_dp(): got.append(lax.ppermute(block, ('section', 'dp'), pairs))  242 us
    pallas_call x8, Pallas kernels, fwd_far(): pl.pallas_call(kernel, out_shape=tuple((jax.ShapeDtypeStruct(b.shape, b.d...  76.8 us
    pallas_call x4, Pallas kernels, bwd_far(): pl.pallas_call(kernel, out_shape=tuple((jax.ShapeDtypeStruct(b.shape, b.d...  53.8 us
    pallas_call x7, Pallas kernels, bwd_slot(): pl.pallas_call(kernel, out_shape=(jax.ShapeDtypeStruct((rows, dims.width)...  49.3 us
    pallas_call x7, Pallas kernels, fwd_slot(): pl.pallas_call(kernel, out_shape=(jax.ShapeDtypeStruct((rows, dims.width)...  39.9 us
    ppermute x6, waiting for transfers between devices, forward(): frecv = lax.ppermute(y, 'section', pairs)  35.6 us
    pallas_call x2, Pallas kernels, weight_grads(): pl.pallas_call(kernel, out_shape=tuple(shapes), in_specs=[SMEM] * 2 + [AN...  31.5 us
    ppermute x42, waiting for transfers between devices, to_dp(): got.append(lax.ppermute(block, ('section', 'dp'), pairs))  21.4 us
  transfers between devices with their start and end apart: 61, of which 9 were waited for; matrix products, arithmetic and copies ran while one was open for 6% of the time, Pallas kernels for 40%

profile of v3, /device:TPU:13, one launch (start us, length us, event | category | flops | bytes accessed | tf_op | source)
XLA Modules:
  0.0 633.4 jit_solution(12029486193027259237)
XLA Ops:
  20.7 26.0 %collective-permute-done.4.refs_4_ = bf16[32,4096]{1,0:T(8,128)(2,1)} collective-permute-done((bf16[32,4096]{1,0:T(8,128)(2,1)}, bf16[32,4096]{1,0:T(8,128)(2,1)}, u32[]{:S(2)}, u32[]{:S(2)}) %collective-permute-start.4) | collective-permute-done | bytes 262176 | tf_op jit(solution)/shard_map/ppermute | solution.py:751
  46.7 9.5 %forward_rows.9 = (bf16[32,4096]{1,0:T(8,128)(2,1)}, bf16[4,128,128,128]{3,2,1,0:T(8,128)(2,1)}, bf16[4,128,128,128]{3,2,1,0:T(8,128)(2,1)}, bf16[4,128,4096]{2,...) custom-call(s32[8]{0:T(128)} %stack.337.refs_0_, ...), custom_call_target="tpu_custom_call", output_to_operand_aliasing={{1}: (11, {}), {2}: (12, {}), {3}: (13, {}), {4}: (14, {}),... | custom-call | tf_op jit(solution)/shard_map/forward_rows/pallas_call | solution.py:302
  65.7 9.3 %forward_rows.10 = (bf16[32,4096]{1,0:T(8,128)(2,1)}, bf16[4,128,128,128]{3,2,1,0:T(8,128)(2,1)}, bf16[4,128,128,128]{3,2,1,0:T(8,128)(2,1)}, bf16[4,128,4096]{2...) custom-call(s32[8]{0:T(128)} %stack.333.refs_0_, ...), custom_call_target="tpu_custom_call", output_to_operand_aliasing={{1}: (11, {}), {2}: (12, {}), {3}: (13, {}), {4}: (14, {}),... | custom-call | tf_op jit(solution)/shard_map/forward_rows/pallas_call | solution.py:302
  85.9 9.3 %forward_rows.11 = (bf16[32,4096]{1,0:T(8,128)(2,1)}, bf16[4,128,128,128]{3,2,1,0:T(8,128)(2,1)}, bf16[4,128,128,128]{3,2,1,0:T(8,128)(2,1)}, bf16[4,128,4096]{2...) custom-call(s32[8]{0:T(128)} %stack.349.refs_0_, ...), custom_call_target="tpu_custom_call", output_to_operand_aliasing={{1}: (11, {}), {2}: (12, {}), {3}: (13, {}), {4}: (14, {}),... | custom-call | tf_op jit(solution)/shard_map/forward_rows/pallas_call | solution.py:302
  104.5 11.5 %backward_rows.8 = (bf16[32,4096]{1,0:T(8,128)(2,1)}, bf16[4,128,128,128]{3,2,1,0:T(8,128)(2,1)}, bf16[4,128,4096]{2,1,0:T(8,128)(2,1)}, bf16[4,128,256]{2,1,0:T(8,128)(2,1)}, f32[4,8,4096]{2,1,0:T(8,128)}) custom-call(s32[8]{0:T(128)} %stack.325.refs_0_, s32[128]{0:T(128)} %bitcast.143, ...), custom_call_target="tpu_custom_call", output_to_operand_aliasing={{1}: (13, {}), {2}: (14, {}), {3}: (15, {}), {4}: (16, {})} | custom-call | tf_op jit(solution)/shard_map/backward_rows/pallas_call | solution.py:397
  132.4 9.3 %forward_rows.12 = (bf16[32,4096]{1,0:T(8,128)(2,1)}, bf16[4,128,128,128]{3,2,1,0:T(8,128)(2,1)}, bf16[4,128,128,128]{3,2,1,0:T(8,128)(2,1)}, bf16[4,128,4096]{2...) custom-call(s32[8]{0:T(128)} %stack.353.refs_0_, ...), custom_call_target="tpu_custom_call", output_to_operand_aliasing={{1}: (11, {}), {2}: (12, {}), {3}: (13, {}), {4}: (14, {}),... | custom-call | tf_op jit(solution)/shard_map/forward_rows/pallas_call | solution.py:302
  143.8 11.7 %backward_rows.9 = (bf16[32,4096]{1,0:T(8,128)(2,1)}, bf16[4,128,128,128]{3,2,1,0:T(8,128)(2,1)}, bf16[4,128,4096]{2,1,0:T(8,128)(2,1)}, bf16[4,128,256]{2,1,0:T(8,128)(2,1)}, f32[4,8,4096]{2,1,0:T(8,128)}) custom-call(s32[8]{0:T(128)} %stack.321.refs_0_, s32[128]{0:T(128)} %bitcast.145, ...), custom_call_target="tpu_custom_call", output_to_operand_aliasing={{1}: (13, {}), {2}: (14, {}), {3}: (15, {}), {4}: (16, {})} | custom-call | tf_op jit(solution)/shard_map/backward_rows/pallas_call | solution.py:397
  158.8 11.7 %collective-permute-start.37 = (bf16[1,32,4096]{2,1,0:T(8,128)(2,1)}, bf16[1,32,4096]{2,1,0:T(8,128)(2,1)S(1)}, u32[]{:S(2)}, u32[]{:S(2)}) collective-permute-start(bf16[1,32,4096]{2,1,0:T(8,128)(2,1)} %bitcast.52), channel_id=1, source_target_pairs={{8,10},{9,11},{10,8},{11,9},{16,18},{17,19},{18,16},{19,17},{24,26... | collective-permute-start | bytes 786440 | tf_op jit(solution)/shard_map/ppermute | solution.py:719
  196.2 11.5 %backward_rows.10 = (bf16[32,4096]{1,0:T(8,128)(2,1)}, bf16[4,128,128,128]{3,2,1,0:T(8,128)(2,1)}, bf16[4,128,4096]{2,1,0:T(8,128)(2,1)}, bf16[4,128,256]{2,1,0:T(8,128)(2,1)}, f32[4,8,4096]{2,1,0:T(8,128)}) custom-call(s32[8]{0:T(128)} %stack.317.refs_0_, ...), custom_call_target="tpu_custom_call", output_to_operand_aliasing={{1}: (13, {}), {2}: (14, {}), {3}: (15, {}), {4}: (16, {})} | custom-call | tf_op jit(solution)/shard_map/backward_rows/pallas_call | solution.py:397
  244.0 11.9 %backward_rows.11 = (bf16[32,4096]{1,0:T(8,128)(2,1)}, bf16[4,128,128,128]{3,2,1,0:T(8,128)(2,1)}, bf16[4,128,4096]{2,1,0:T(8,128)(2,1)}, bf16[4,128,256]{2,1,0:T(8,128)(2,1)}, f32[4,8,4096]{2,1,0:T(8,128)}) custom-call(s32[8]{0:T(128)} %stack.313.refs_0_, ...), custom_call_target="tpu_custom_call", output_to_operand_aliasing={{1}: (13, {}), {2}: (14, {}), {3}: (15, {}), {4}: (16, {})} | custom-call | tf_op jit(solution)/shard_map/backward_rows/pallas_call | solution.py:397
  269.2 12.3 %collective-permute-done.49.refs_10_.refs_13_ = bf16[1,32,4096]{2,1,0:T(8,128)(2,1)S(1)} collective-permute-done((bf16[1,32,4096]{2,1,0:T(8,128)(2,1)}, bf16[1,32,4096]{2,1,0:T(8,128)(2,1)S(1)}, u32[]{:S(2)}, u32[]{:S(2)}) %collective-permute-start.49) | collective-permute-done | bytes 262176 | tf_op jit(solution)/shard_map/ppermute | solution.py:719
  282.9 59.9 %collective-permute-start.45 = (bf16[1,32,4096]{2,1,0:T(8,128)(2,1)S(1)}, bf16[1,32,4096]{2,1,0:T(8,128)(2,1)S(1)}, u32[]{:S(2)}, u32[]{:S(2)}) collective-permute-start(bf16[1,32,4096]{2,1,0:T(8,128)(2,1)S(1)} %bitcast.122), channel_id=1, source_target_pairs={{0,1},{1,2},{2,3},{3,0},{8,9},{9,10},{10,11},{11,8},{16,17},{17,18... | collective-permute-start | bytes 786440 | tf_op jit(solution)/shard_map/ppermute | solution.py:719
  344.3 16.8 %collective-permute-start.46 = (bf16[1,32,4096]{2,1,0:T(8,128)(2,1)S(1)}, bf16[1,32,4096]{2,1,0:T(8,128)(2,1)S(1)}, u32[]{:S(2)}, u32[]{:S(2)}) collective-permute-start(bf16[1,32,4096]{2,1,0:T(8,128)(2,1)S(1)} %bitcast.123), channel_id=1, source_target_pairs={{0,2},{1,3},{2,0},{3,1},{8,10},{9,11},{10,8},{11,9},{16,18},{17,19... | collective-permute-start | bytes 786440 | tf_op jit(solution)/shard_map/ppermute | solution.py:719
  405.0 28.1 %collective-permute-start.54 = (f32[1,4096]{1,0:T(1,128)S(1)}, f32[1,4096]{1,0:T(1,128)S(1)}, u32[]{:S(2)}, u32[]{:S(2)}) collective-permute-start(f32[1,4096]{1,0:T(1,128)S(1)} %bitcast.172), channel_id=1, source_target_pairs={{0,1},{1,2},{2,3},{3,0},{8,9},{9,10},{10,11},{11,8},{16,17},{17,18... | collective-permute-start | bytes 49160 | tf_op jit(solution)/shard_map/ppermute | solution.py:719
  452.5 18.4 %forward_far_rows.12 = (bf16[4,128,128,128]{3,2,1,0:T(8,128)(2,1)}, bf16[4,128,128,128]{3,2,1,0:T(8,128)(2,1)}, bf16[4,128,4096]{2,1,0:T(8,128)(2,1)}, bf16[4,128,256]{2,1,0:T(8,128)(2,1)}) custom-call(s32[8]{0:T(128)} %stack.372.refs_0_, s32[128]{0:T(128)} %bitcast.167, ...), custom_call_target="tpu_custom_call", output_to_operand_aliasing={{0}: (15, {}), {1}: (16, {}), {2}: (17, {}), {3}: (18, {})} | custom-call | tf_op jit(solution)/shard_map/forward_far_rows/pallas_call | solution.py:477
  471.0 18.4 %forward_far_rows.13 = (bf16[4,128,128,128]{3,2,1,0:T(8,128)(2,1)}, bf16[4,128,128,128]{3,2,1,0:T(8,128)(2,1)}, bf16[4,128,4096]{2,1,0:T(8,128)(2,1)}, bf16[4,128,256]{2,1,0:T(8,128)(2,1)}) custom-call(s32[8]{0:T(128)} %stack.371.refs_0_, s32[128]{0:T(128)} %bitcast.168, ...), custom_call_target="tpu_custom_call", output_to_operand_aliasing={{0}: (15, {}), {1}: (16, {}), {2}: (17, {}), {3}: (18, {})} | custom-call | tf_op jit(solution)/shard_map/forward_far_rows/pallas_call | solution.py:477
  489.4 18.4 %forward_far_rows.14 = (bf16[4,128,128,128]{3,2,1,0:T(8,128)(2,1)}, bf16[4,128,128,128]{3,2,1,0:T(8,128)(2,1)}, bf16[4,128,4096]{2,1,0:T(8,128)(2,1)}, bf16[4,128,256]{2,1,0:T(8,128)(2,1)}) custom-call(s32[8]{0:T(128)} %stack.370.refs_0_, s32[128]{0:T(128)} %bitcast.169, ...), custom_call_target="tpu_custom_call", output_to_operand_aliasing={{0}: (15, {}), {1}: (16, {}), {2}: (17, {}), {3}: (18, {})} | custom-call | tf_op jit(solution)/shard_map/forward_far_rows/pallas_call | solution.py:477
  507.9 18.4 %forward_far_rows.15 = (bf16[4,128,128,128]{3,2,1,0:T(8,128)(2,1)}, bf16[4,128,128,128]{3,2,1,0:T(8,128)(2,1)}, bf16[4,128,4096]{2,1,0:T(8,128)(2,1)}, bf16[4,128,256]{2,1,0:T(8,128)(2,1)}) custom-call(s32[8]{0:T(128)} %stack.369.refs_0_, s32[128]{0:T(128)} %bitcast.170, ...), custom_call_target="tpu_custom_call", output_to_operand_aliasing={{0}: (15, {}), {1}: (16, {}), {2}: (17, {}), {3}: (18, {})} | custom-call | tf_op jit(solution)/shard_map/forward_far_rows/pallas_call | solution.py:477
  526.3 13.4 %backward_far_rows.4 = (bf16[4,128,128,128]{3,2,1,0:T(8,128)(2,1)}, bf16[4,128,4096]{2,1,0:T(8,128)(2,1)}, bf16[4,128,256]{2,1,0:T(8,128)(2,1)}) custom-call(s32[8]{0:T(128)} %stack.377.refs_0_, s32[128]{0:T(128)} %bitcast.151, bf16[64,128,128]{2,1,0:T(8,128)(2,1)} %bitcast.118, ...), custom_call_target="tpu_custom_call", output_to_operand_aliasing={{0}: (19, {}), {1}: (20, {}), {2}: (21, {})} | custom-call | tf_op jit(solution)/shard_map/backward_far_rows/pallas_call | solution.py:541
  539.8 13.7 %backward_far_rows.5 = (bf16[4,128,128,128]{3,2,1,0:T(8,128)(2,1)}, bf16[4,128,4096]{2,1,0:T(8,128)(2,1)}, bf16[4,128,256]{2,1,0:T(8,128)(2,1)}) custom-call(s32[8]{0:T(128)} %stack.376.refs_0_, s32[128]{0:T(128)} %bitcast.152, bf16[64,128,128]{2,1,0:T(8,128)(2,1)} %bitcast.119, ...), custom_call_target="tpu_custom_call", output_to_operand_aliasing={{0}: (19, {}), {1}: (20, {}), {2}: (21, {})} | custom-call | tf_op jit(solution)/shard_map/backward_far_rows/pallas_call | solution.py:541
  553.4 13.4 %backward_far_rows.6 = (bf16[4,128,128,128]{3,2,1,0:T(8,128)(2,1)}, bf16[4,128,4096]{2,1,0:T(8,128)(2,1)}, bf16[4,128,256]{2,1,0:T(8,128)(2,1)}) custom-call(s32[8]{0:T(128)} %stack.374.refs_0_, s32[128]{0:T(128)} %bitcast.153, bf16[64,128,128]{2,1,0:T(8,128)(2,1)} %bitcast.120, ...), custom_call_target="tpu_custom_call", output_to_operand_aliasing={{0}: (19, {}), {1}: (20, {}), {2}: (21, {})} | custom-call | tf_op jit(solution)/shard_map/backward_far_rows/pallas_call | solution.py:541
  567.6 13.3 %backward_far_rows.7 = (bf16[4,128,128,128]{3,2,1,0:T(8,128)(2,1)}, bf16[4,128,4096]{2,1,0:T(8,128)(2,1)}, bf16[4,128,256]{2,1,0:T(8,128)(2,1)}) custom-call(s32[8]{0:T(128)} %stack.303.refs_0_, s32[128]{0:T(128)} %bitcast.154, bf16[64,128,128]{2,1,0:T(8,128)(2,1)} %bitcast.121, ...), custom_call_target="tpu_custom_call", output_to_operand_aliasing={{0}: (19, {}), {1}: (20, {}), {2}: (21, {})} | custom-call | tf_op jit(solution)/shard_map/backward_far_rows/pallas_call | solution.py:541
  580.9 15.8 %down_gradients.1 = (bf16[64,128,128]{2,1,0:T(8,128)(2,1)}, bf16[64,128,128]{2,1,0:T(8,128)(2,1)}, bf16[16,10240]{1,0:T(8,128)(2,1)}, bf16[16,10240]{1,0:T(8,128)(2,1)}) custom-call(s32[8]{0:T(128)} %stack.300.refs_0_, s32[128]{0:T(128)} %bitcast.155, bf16[4,128,128,128]{3,2,1,0:T(8,128)(2,1)} %get-tuple-element.325.refs_2_, ...), custom_call_target="tpu_custom_call" | custom-call | tf_op jit(solution)/shard_map/down_gradients/pallas_call | solution.py:656
  603.5 15.7 %up_gradients.1 = (bf16[64,128,128]{2,1,0:T(8,128)(2,1)}, bf16[64,128,128]{2,1,0:T(8,128)(2,1)}, bf16[16,12288]{1,0:T(8,128)(2,1)}, bf16[16,12288]{1,0:T(8,128)(2,1)}) custom-call(s32[8]{0:T(128)} %stack.300.refs_0_, s32[128]{0:T(128)} %select_reduce_fusion.refs_2_.refs_1_, bf16[4,128,128,128]{3,2,1,0:T(8,128)(2,1)} %get-tuple-element.316.refs_2_, ...), custom_call_target="tpu_custom_call" | custom-call | tf_op jit(solution)/shard_map/up_gradients/pallas_call | solution.py:656
  (278 shorter events, 232.7 us)
Async XLA Ops:
  15.2 100.8 %collective-permute-start.13 = (bf16[4,32,4096]{2,1,0:T(8,128)(2,1)}, bf16[4,32,4096]{2,1,0:T(8,128)(2,1)S(1)}, u32[]{:S(2)}, u32[]{:S(2)}) collective-permute-start(bf16[4,32,4096]{2,1,0:T(8,128)(2,1)} %broadcast_select_fusion), channel_id=1, source_target_pairs={{0,1},{1,2},{2,3},{3,0},{24,25},{25,26},{26,27},{27,24},{4,5},{5,6... | collective-permute-start | bytes 3145736 | tf_op jit(solution)/shard_map/ppermute | solution.py:719
  18.6 99.4 %collective-permute-start.14 = (bf16[4,32,4096]{2,1,0:T(8,128)(2,1)}, bf16[4,32,4096]{2,1,0:T(8,128)(2,1)S(1)}, u32[]{:S(2)}, u32[]{:S(2)}) collective-permute-start(bf16[4,32,4096]{2,1,0:T(8,128)(2,1)} %broadcast_select_fusion), channel_id=1, source_target_pairs={{0,2},{1,3},{2,0},{3,1},{24,26},{25,27},{26,24},{27,25},{4,6},{5,7... | collective-permute-start | bytes 3145736 | tf_op jit(solution)/shard_map/ppermute | solution.py:719
  19.4 100.0 %collective-permute-start.15 = (bf16[4,32,4096]{2,1,0:T(8,128)(2,1)}, bf16[4,32,4096]{2,1,0:T(8,128)(2,1)S(1)}, u32[]{:S(2)}, u32[]{:S(2)}) collective-permute-start(bf16[4,32,4096]{2,1,0:T(8,128)(2,1)} %broadcast_select_fusion), channel_id=1, source_target_pairs={{0,3},{1,0},{2,1},{3,2},{24,27},{25,24},{26,25},{27,26},{4,7},{5,4... | collective-permute-start | bytes 3145736 | tf_op jit(solution)/shard_map/ppermute | solution.py:719
  127.6 42.8 %collective-permute-start.41 = (bf16[1,32,4096]{2,1,0:T(8,128)(2,1)}, bf16[1,32,4096]{2,1,0:T(8,128)(2,1)}, u32[]{:S(2)}, u32[]{:S(2)}) collective-permute-start(bf16[1,32,4096]{2,1,0:T(8,128)(2,1)} %bitcast.53), channel_id=1, source_target_pairs={{8,11},{9,8},{10,9},{11,10},{16,19},{17,16},{18,17},{19,18},{12,15... | collective-permute-start | bytes 786440 | tf_op jit(solution)/shard_map/ppermute | solution.py:719
  158.8 49.0 %collective-permute-start.37 = (bf16[1,32,4096]{2,1,0:T(8,128)(2,1)}, bf16[1,32,4096]{2,1,0:T(8,128)(2,1)S(1)}, u32[]{:S(2)}, u32[]{:S(2)}) collective-permute-start(bf16[1,32,4096]{2,1,0:T(8,128)(2,1)} %bitcast.52), channel_id=1, source_target_pairs={{8,10},{9,11},{10,8},{11,9},{16,18},{17,19},{18,16},{19,17},{24,26... | collective-permute-start | bytes 786440 | tf_op jit(solution)/shard_map/ppermute | solution.py:719
  170.4 40.4 %collective-permute-start.38 = (bf16[1,32,4096]{2,1,0:T(8,128)(2,1)}, bf16[1,32,4096]{2,1,0:T(8,128)(2,1)S(1)}, u32[]{:S(2)}, u32[]{:S(2)}) collective-permute-start(bf16[1,32,4096]{2,1,0:T(8,128)(2,1)} %bitcast.52), channel_id=1, source_target_pairs={{8,11},{9,8},{10,9},{11,10},{16,19},{17,16},{18,17},{19,18},{24,27... | collective-permute-start | bytes 786440 | tf_op jit(solution)/shard_map/ppermute | solution.py:719
  212.8 43.1 %collective-permute-start.52 = (bf16[1,32,4096]{2,1,0:T(8,128)(2,1)}, bf16[1,32,4096]{2,1,0:T(8,128)(2,1)S(1)}, u32[]{:S(2)}, u32[]{:S(2)}) collective-permute-start(bf16[1,32,4096]{2,1,0:T(8,128)(2,1)} %bitcast.59), channel_id=1, source_target_pairs={{16,18},{17,19},{18,16},{19,17},{20,22},{21,23},{22,20},{23,21}} | collective-permute-start | bytes 786440 | tf_op jit(solution)/shard_map/ppermute | solution.py:719
  215.9 43.1 %collective-permute-start.53 = (bf16[1,32,4096]{2,1,0:T(8,128)(2,1)}, bf16[1,32,4096]{2,1,0:T(8,128)(2,1)}, u32[]{:S(2)}, u32[]{:S(2)}) collective-permute-start(bf16[1,32,4096]{2,1,0:T(8,128)(2,1)} %bitcast.59), channel_id=1, source_target_pairs={{16,19},{17,16},{18,17},{19,18},{20,23},{21,20},{22,21},{23,22}} | collective-permute-start | bytes 786440 | tf_op jit(solution)/shard_map/ppermute | solution.py:719
  219.1 43.0 %collective-permute-start.30 = (bf16[1,32,4096]{2,1,0:T(8,128)(2,1)}, bf16[1,32,4096]{2,1,0:T(8,128)(2,1)S(1)}, u32[]{:S(2)}, u32[]{:S(2)}) collective-permute-start(bf16[1,32,4096]{2,1,0:T(8,128)(2,1)} %bitcast.50), channel_id=1, source_target_pairs={{16,17},{17,18},{18,19},{19,16},{24,25},{25,26},{26,27},{27,24},{2... | collective-permute-start | bytes 786440 | tf_op jit(solution)/shard_map/ppermute | solution.py:719
  221.3 43.4 %collective-permute-start.31 = (bf16[1,32,4096]{2,1,0:T(8,128)(2,1)}, bf16[1,32,4096]{2,1,0:T(8,128)(2,1)S(1)}, u32[]{:S(2)}, u32[]{:S(2)}) collective-permute-start(bf16[1,32,4096]{2,1,0:T(8,128)(2,1)} %bitcast.50), channel_id=1, source_target_pairs={{16,18},{17,19},{18,16},{19,17},{24,26},{25,27},{26,24},{27,25},{2... | collective-permute-start | bytes 786440 | tf_op jit(solution)/shard_map/ppermute | solution.py:719
  230.6 37.2 %collective-permute-start.32 = (bf16[1,32,4096]{2,1,0:T(8,128)(2,1)}, bf16[1,32,4096]{2,1,0:T(8,128)(2,1)S(1)}, u32[]{:S(2)}, u32[]{:S(2)}) collective-permute-start(bf16[1,32,4096]{2,1,0:T(8,128)(2,1)} %bitcast.50), channel_id=1, source_target_pairs={{16,19},{17,16},{18,17},{19,18},{24,27},{25,24},{26,25},{27,26},{2... | collective-permute-start | bytes 786440 | tf_op jit(solution)/shard_map/ppermute | solution.py:719
  264.7 79.6 %collective-permute-start.50 = (bf16[1,32,4096]{2,1,0:T(8,128)(2,1)}, bf16[1,32,4096]{2,1,0:T(8,128)(2,1)S(1)}, u32[]{:S(2)}, u32[]{:S(2)}) collective-permute-start(bf16[1,32,4096]{2,1,0:T(8,128)(2,1)} %bitcast.58), channel_id=1, source_target_pairs={{8,11},{9,8},{10,9},{11,10},{16,19},{17,16},{18,17},{19,18},{12,15... | collective-permute-start | bytes 786440 | tf_op jit(solution)/shard_map/ppermute | solution.py:719
  267.9 93.3 %collective-permute-start.33 = (bf16[1,32,4096]{2,1,0:T(8,128)(2,1)S(1)}, bf16[1,32,4096]{2,1,0:T(8,128)(2,1)S(1)}, u32[]{:S(2)}, u32[]{:S(2)}) collective-permute-start(bf16[1,32,4096]{2,1,0:T(8,128)(2,1)S(1)} %bitcast.128), channel_id=1, source_target_pairs={{24,25},{25,26},{26,27},{27,24},{28,29},{29,30},{30,31},{31,28}} | collective-permute-start | bytes 786440 | tf_op jit(solution)/shard_map/ppermute | solution.py:719
  268.6 93.3 %collective-permute-start.34 = (bf16[1,32,4096]{2,1,0:T(8,128)(2,1)S(1)}, bf16[1,32,4096]{2,1,0:T(8,128)(2,1)S(1)}, u32[]{:S(2)}, u32[]{:S(2)}) collective-permute-start(bf16[1,32,4096]{2,1,0:T(8,128)(2,1)S(1)} %bitcast.129), channel_id=1, source_target_pairs={{24,26},{25,27},{26,24},{27,25},{28,30},{29,31},{30,28},{31,29}} | collective-permute-start | bytes 786440 | tf_op jit(solution)/shard_map/ppermute | solution.py:719
  281.5 88.2 %collective-permute-start.35 = (bf16[1,32,4096]{2,1,0:T(8,128)(2,1)S(1)}, bf16[1,32,4096]{2,1,0:T(8,128)(2,1)}, u32[]{:S(2)}, u32[]{:S(2)}) collective-permute-start(bf16[1,32,4096]{2,1,0:T(8,128)(2,1)S(1)} %bitcast.130), channel_id=1, source_target_pairs={{24,27},{25,24},{26,25},{27,26},{28,31},{29,28},{30,29},{31,30}} | collective-permute-start | bytes 786440 | tf_op jit(solution)/shard_map/ppermute | solution.py:719
  282.9 93.3 %collective-permute-start.45 = (bf16[1,32,4096]{2,1,0:T(8,128)(2,1)S(1)}, bf16[1,32,4096]{2,1,0:T(8,128)(2,1)S(1)}, u32[]{:S(2)}, u32[]{:S(2)}) collective-permute-start(bf16[1,32,4096]{2,1,0:T(8,128)(2,1)S(1)} %bitcast.122), channel_id=1, source_target_pairs={{0,1},{1,2},{2,3},{3,0},{8,9},{9,10},{10,11},{11,8},{16,17},{17,18... | collective-permute-start | bytes 786440 | tf_op jit(solution)/shard_map/ppermute | solution.py:719
  344.3 38.3 %collective-permute-start.46 = (bf16[1,32,4096]{2,1,0:T(8,128)(2,1)S(1)}, bf16[1,32,4096]{2,1,0:T(8,128)(2,1)S(1)}, u32[]{:S(2)}, u32[]{:S(2)}) collective-permute-start(bf16[1,32,4096]{2,1,0:T(8,128)(2,1)S(1)} %bitcast.123), channel_id=1, source_target_pairs={{0,2},{1,3},{2,0},{3,1},{8,10},{9,11},{10,8},{11,9},{16,18},{17,19... | collective-permute-start | bytes 786440 | tf_op jit(solution)/shard_map/ppermute | solution.py:719
  392.1 41.1 %collective-permute-start.23 = (bf16[1,32,4096]{2,1,0:T(8,128)(2,1)S(1)}, bf16[1,32,4096]{2,1,0:T(8,128)(2,1)S(1)}, u32[]{:S(2)}, u32[]{:S(2)}) collective-permute-start(bf16[1,32,4096]{2,1,0:T(8,128)(2,1)S(1)} %bitcast.136), channel_id=1, source_target_pairs={{0,3},{1,0},{2,1},{3,2},{8,11},{9,8},{10,9},{11,10},{4,7},{5,4},{6... | collective-permute-start | bytes 786440 | tf_op jit(solution)/shard_map/ppermute | solution.py:719
  401.0 39.5 %collective-permute-start.18 = (bf16[1,32,4096]{2,1,0:T(8,128)(2,1)}, bf16[1,32,4096]{2,1,0:T(8,128)(2,1)S(1)}, u32[]{:S(2)}, u32[]{:S(2)}) collective-permute-start(bf16[1,32,4096]{2,1,0:T(8,128)(2,1)} %bitcast.131), channel_id=1, source_target_pairs={{0,1},{1,2},{2,3},{3,0},{4,5},{5,6},{6,7},{7,4}} | collective-permute-start | bytes 786440 | tf_op jit(solution)/shard_map/ppermute | solution.py:719
  402.5 164.3 %collective-permute-start.19 = (bf16[1,32,4096]{2,1,0:T(8,128)(2,1)}, bf16[1,32,4096]{2,1,0:T(8,128)(2,1)S(1)}, u32[]{:S(2)}, u32[]{:S(2)}) collective-permute-start(bf16[1,32,4096]{2,1,0:T(8,128)(2,1)} %bitcast.132), channel_id=1, source_target_pairs={{0,2},{1,3},{2,0},{3,1},{4,6},{5,7},{6,4},{7,5}} | collective-permute-start | bytes 786440 | tf_op jit(solution)/shard_map/ppermute | solution.py:719
  403.2 163.6 %collective-permute-start.20 = (bf16[1,32,4096]{2,1,0:T(8,128)(2,1)}, bf16[1,32,4096]{2,1,0:T(8,128)(2,1)S(1)}, u32[]{:S(2)}, u32[]{:S(2)}) collective-permute-start(bf16[1,32,4096]{2,1,0:T(8,128)(2,1)} %bitcast.133), channel_id=1, source_target_pairs={{0,3},{1,0},{2,1},{3,2},{4,7},{5,4},{6,5},{7,6}} | collective-permute-start | bytes 786440 | tf_op jit(solution)/shard_map/ppermute | solution.py:719
  405.0 197.5 %collective-permute-start.54 = (f32[1,4096]{1,0:T(1,128)S(1)}, f32[1,4096]{1,0:T(1,128)S(1)}, u32[]{:S(2)}, u32[]{:S(2)}) collective-permute-start(f32[1,4096]{1,0:T(1,128)S(1)} %bitcast.172), channel_id=1, source_target_pairs={{0,1},{1,2},{2,3},{3,0},{8,9},{9,10},{10,11},{11,8},{16,17},{17,18... | collective-permute-start | bytes 49160 | tf_op jit(solution)/shard_map/ppermute | solution.py:719
  433.1 169.3 %collective-permute-start.55 = (f32[1,4096]{1,0:T(1,128)S(1)}, f32[1,4096]{1,0:T(1,128)S(1)}, u32[]{:S(2)}, u32[]{:S(2)}) collective-permute-start(f32[1,4096]{1,0:T(1,128)S(1)} %bitcast.173), channel_id=1, source_target_pairs={{0,2},{1,3},{2,0},{3,1},{8,10},{9,11},{10,8},{11,9},{16,18},{17,19... | collective-permute-start | bytes 49160 | tf_op jit(solution)/shard_map/ppermute | solution.py:719
  440.5 162.0 %collective-permute-start.56 = (f32[1,4096]{1,0:T(1,128)S(1)}, f32[1,4096]{1,0:T(1,128)S(1)}, u32[]{:S(2)}, u32[]{:S(2)}) collective-permute-start(f32[1,4096]{1,0:T(1,128)S(1)} %bitcast.174), channel_id=1, source_target_pairs={{0,3},{1,0},{2,1},{3,2},{8,11},{9,8},{10,9},{11,10},{16,19},{17,16... | collective-permute-start | bytes 49160 | tf_op jit(solution)/shard_map/ppermute | solution.py:719
  (87 other events, 2336.0 us)

commit v4 on v2

--- a/solution.py
+++ b/solution.py
@@ -420,22 +420,22 @@
     return out[0], out[1:]
 
 
-def pick_rows(sc, sources, dst, sem):
-    n = dst.shape[0] // len(sources[0])
-    for q, triple in enumerate(sources):
-
-        @pl.when(sc[3] == q)
+def pick_rows(sc, sources, dst, sem, count):
+    n = dst.shape[0] // (len(sources[0]) * count)
+    places = [(q, t, (q * len(sources[0]) + t) * n) for q in range(count) for t in range(len(sources[0]))]
+    for number, triple in enumerate(sources):
+
+        @pl.when(sc[3] == number)
         def _():
-            for t, ref in enumerate(triple):
-                pltpu.make_async_copy(ref.at[sc[4]], dst.at[t * n : (t + 1) * n], sem.at[t]).start()
+            for q, t, at in places:
+                pltpu.make_async_copy(triple[t].at[sc[4] + q], dst.at[at : at + n], sem.at[q, t]).start()
 
     return tuple(
-        pltpu.make_async_copy(ref.at[0], dst.at[t * n : (t + 1) * n], sem.at[t])
-        for t, ref in enumerate(sources[0])
+        pltpu.make_async_copy(sources[0][t].at[0], dst.at[at : at + n], sem.at[q, t]) for q, t, at in places
     )
 
 
-def fwd_far(dims, sc, upo, sources, weights, bufs):
+def fwd_far(dims, sc, upo, sources, weights, bufs, count):
     hidb, slpb, nrmb, lowb = bufs
     rows = sources[0][0].shape[1]
     far = rows * len(sources[0])
@@ -450,53 +450,58 @@
         base = 2 + 2 * n_w
         srcs = [refs[base + q * n_t : base + (q + 1) * n_t] for q in range(n_q)]
         hidb, slpb, nrmb, lowb = refs[n_plain + 4 : n_plain + 8]
-        up_s, small_s, x_s, nrm_s, hid_s, slp_s, low_s, sems, xsem = refs[n_plain + 8 :]
+        up_s, small_s, x_s, nrm_s, hid_s, slp_s, low_s, sems, xsem, osems = refs[n_plain + 9 :]
 
         @pl.when(sc[0] == 1)
         def _():
             m, f = sc[1], sc[2]
-            wait_x = pick_rows(sc, srcs, x_s, xsem)
+            wait_x = pick_rows(sc, srcs, x_s, xsem, count)
             small, up = load_weights(f, (small_w, up_w), (small_s, up_s), sems)
             low_s[...] = jnp.zeros_like(low_s)
             done(wait_x)
             done(small)
             fwd_norm(dims, x_s, small_s, nrm_s, low_s)
             done(up)
-            fwd_hidden(dims, small_s, up_s, upo, nrm_s, hid_s, slp_s, low_s, 8)
+            fwd_hidden(dims, small_s, up_s, upo, nrm_s, hid_s, slp_s, low_s, 4)
             at = slice(rows, rows + far)
-            outs = [
-                pltpu.make_async_copy(hid_s, hidb.at[m, :, at], sems.at[4]),
-                pltpu.make_async_copy(slp_s, slpb.at[m, :, at], sems.at[5]),
-                pltpu.make_async_copy(nrm_s, nrmb.at[m, at], sems.at[6]),
-                pltpu.make_async_copy(low_s, lowb.at[m, at], sems.at[7]),
-            ]
+            outs = []
+            for q in range(count):
+                mine = slice(q * far, (q + 1) * far)
+                outs += [
+                    pltpu.make_async_copy(hid_s.at[:, mine], hidb.at[m + q, :, at], osems.at[q, 0]),
+                    pltpu.make_async_copy(slp_s.at[:, mine], slpb.at[m + q, :, at], osems.at[q, 1]),
+                    pltpu.make_async_copy(nrm_s.at[mine], nrmb.at[m + q, at], osems.at[q, 2]),
+                    pltpu.make_async_copy(low_s.at[mine], lowb.at[m + q, at], osems.at[q, 3]),
+                ]
             for copy in outs:
                 copy.start()
             done(outs)
 
     return pl.pallas_call(
         kernel,
-        out_shape=tuple(jax.ShapeDtypeStruct(b.shape, b.dtype) for b in bufs),
+        out_shape=tuple(jax.ShapeDtypeStruct(b.shape, b.dtype) for b in bufs)
+        + (jax.ShapeDtypeStruct((8, BLK), F32),),
         in_specs=[SMEM] * 2 + [ANY] * (len(args) - 2),
-        out_specs=(ANY,) * 4,
+        out_specs=(ANY,) * 5,
         input_output_aliases={n_plain + n: n for n in range(4)},
         scratch_shapes=[
             pltpu.VMEM((dims.hidden, BLK, BLK), BF),
             pltpu.VMEM((dims.parts, RANK, dims.packed), BF),
-            pltpu.VMEM((far, dims.width), BF),
-            pltpu.VMEM((far, dims.width), BF),
-            pltpu.VMEM((dims.hidden, far, BLK), BF),
-            pltpu.VMEM((dims.hidden, far, BLK), BF),
-            pltpu.VMEM((far, 2 * BLK), BF),
+            pltpu.VMEM((count * far, dims.width), BF),
+            pltpu.VMEM((count * far, dims.width), BF),
+            pltpu.VMEM((dims.hidden, count * far, BLK), BF),
+            pltpu.VMEM((dims.hidden, count * far, BLK), BF),
+            pltpu.VMEM((count * far, 2 * BLK), BF),
             pltpu.SemaphoreType.DMA((8,)),
-            pltpu.SemaphoreType.DMA((n_t,)),
+            pltpu.SemaphoreType.DMA((count, n_t)),
+            pltpu.SemaphoreType.DMA((count, 4)),
         ],
         compiler_params=params(60),
         name="forward_far_rows",
     )(*args)
 
 
-def bwd_far(dims, sc, dno, sources, weights, slpb, bufs):
+def bwd_far(dims, sc, dno, sources, weights, slpb, bufs, count):
     rows = sources[0][0].shape[1]
     far = rows * len(sources[0])
     n_w, n_t, n_q = len(weights[0]), len(sources[0]), len(sources)
@@ -511,48 +516,60 @@
         srcs = [refs[base + q * n_t : base + (q + 1) * n_t] for q in range(n_q)]
         slpb = refs[n_plain - 1]
         gpb, gb, lowb = refs[n_plain + 3 : n_plain + 6]
-        dn_s, small_s, g_s, slp_s, gp_s, low_s, sems, gsem = refs[n_plain + 6 :]
+        dn_s, small_s, g_s, slp_s, gp_s, low_s, sems, gsem, osems = refs[n_plain + 7 :]
 
         @pl.when(sc[0] == 1)
         def _():
             m, f = sc[1], sc[2]
             at = slice(rows, rows + far)
-            wait_g = pick_rows(sc, srcs, g_s, gsem)
+            wait_g = pick_rows(sc, srcs, g_s, gsem, count)
             small, dn = load_weights(f, (small_w, dn_w), (small_s, dn_s), sems)
-            get_slope = pltpu.make_async_copy(slpb.at[m, :, at], slp_s, sems.at[4])
-            get_slope.start()
+            mine = [slice(q * far, (q + 1) * far) for q in range(count)]
+            get_slope = [
+                pltpu.make_async_copy(slpb.at[m + q, :, at], slp_s.at[:, mine[q]], osems.at[q, 0])
+                for q in range(count)
+            ]
+            for copy in get_slope:
+                copy.start()
             low_s[...] = jnp.zeros_like(low_s)
             done(wait_g)
-            save_g = pltpu.make_async_copy(g_s, gb.at[m, at], sems.at[5])
-            save_g.start()
+            save_g = [
+                pltpu.make_async_copy(g_s.at[mine[q]], gb.at[m + q, at], osems.at[q, 1]) for q in range(count)
+            ]
+            for copy in save_g:
+                copy.start()
             done(small)
             done(dn)
-            get_slope.wait()
-            bwd_hidden(dims, g_s, slp_s, gp_s, small_s, dn_s, dno, low_s, 4)
-            outs = [
-                pltpu.make_async_copy(gp_s, gpb.at[m, :, at], sems.at[6]),
-                pltpu.make_async_copy(low_s, lowb.at[m, at], sems.at[7]),
-            ]
+            done(get_slope)
+            bwd_hidden(dims, g_s, slp_s, gp_s, small_s, dn_s, dno, low_s, 2)
+            outs = []
+            for q in range(count):
+                outs += [
+                    pltpu.make_async_copy(gp_s.at[:, mine[q]], gpb.at[m + q, :, at], osems.at[q, 2]),
+                    pltpu.make_async_copy(low_s.at[mine[q]], lowb.at[m + q, at], osems.at[q, 3]),
+                ]
             for copy in outs:
                 copy.start()
-            save_g.wait()
+            done(save_g)
             done(outs)
 
     return pl.pallas_call(
         kernel,
-        out_shape=tuple(jax.ShapeDtypeStruct(b.shape, b.dtype) for b in bufs),
+        out_shape=tuple(jax.ShapeDtypeStruct(b.shape, b.dtype) for b in bufs)
+        + (jax.ShapeDtypeStruct((8, BLK), F32),),
         in_specs=[SMEM] * 2 + [ANY] * (len(args) - 2),
-        out_specs=(ANY,) * 3,
+        out_specs=(ANY,) * 4,
         input_output_aliases={n_plain + n: n for n in range(3)},
         scratch_shapes=[
             pltpu.VMEM((dims.hidden, BLK, BLK), BF),
             pltpu.VMEM((dims.parts, RANK, dims.packed), BF),
-            pltpu.VMEM((far, dims.width), BF),
-            pltpu.VMEM((dims.hidden, far, BLK), BF),
-            pltpu.VMEM((dims.hidden, far, BLK), BF),
-            pltpu.VMEM((far, 2 * BLK), BF),
+            pltpu.VMEM((count * far, dims.width), BF),
+            pltpu.VMEM((dims.hidden, count * far, BLK), BF),
+            pltpu.VMEM((dims.hidden, count * far, BLK), BF),
+            pltpu.VMEM((count * far, 2 * BLK), BF),
             pltpu.SemaphoreType.DMA((8,)),
-            pltpu.SemaphoreType.DMA((n_t,)),
+            pltpu.SemaphoreType.DMA((count, n_t)),
+            pltpu.SemaphoreType.DMA((count, 4)),
         ],
         compiler_params=params(60),
         name="backward_far_rows",
@@ -690,7 +707,8 @@
     sec = lax.axis_index("section")
     f = lax.axis_index("fsdp")
     swap = [(0, 1), (1, 0)]
-    held = rows
+    n_dp = lax.axis_size("dp")
+    held = rows * n_dp
     small = jnp.concatenate(
         [up_left[0], down_right[0], up_right[0], down_left[0],
          jnp.broadcast_to(norm_gain, (RANK, norm_gain.shape[1]))], axis=1)
@@ -711,18 +729,49 @@
         return jnp.stack([live.astype(jnp.int32), jnp.clip(m, 0, micro - 1).astype(jnp.int32),
                           f.astype(jnp.int32), edge.astype(jnp.int32), zero, zero, zero, zero])
 
-    state = {"token": None}
+    def shifted(block, sections, k):
+        pairs = [(s * n_dp + d, s * n_dp + (d + k) % n_dp) for s in sections for d in range(n_dp)]
+        return lax.ppermute(block, ("section", "dp"), pairs)
+
+    def to_dp(block, sections):
+        return tuple(shifted(block, sections, k) for k in range(1, n_dp))
+
+    def flags(live, m, source, index):
+        return jnp.stack([jnp.asarray(v).astype(jnp.int32) for v in (live, m, f, source, index, 0, 0, 0)])
+
+    state = {"token": None, "due": []}
 
     def chained(*arrays):
-        if state["token"] is None:
+        due = tuple(v for n, v in state["due"] if n <= 0)
+        state["due"] = [(n - 1, v) for n, v in state["due"] if n > 0]
+        if state["token"] is not None:
+            due = due + (state["token"],)
+        if not due:
             return arrays
-        out = lax.optimization_barrier(arrays + (state["token"],))
-        return out[:-1]
+        out = lax.optimization_barrier(arrays + due)
+        return out[: len(arrays)]
+
+    shifts = [1] + list(range(n_dp - 1, 1, -1))
+    queue = []
+
+    def send_one(hold):
+        if queue:
+            store, k, payload, sections = queue.pop(0)
+            block, _ = lax.optimization_barrier((payload(), state["token"]))
+            store[k] = shifted(block, sections, k)
+            state["due"].append((hold, store[k]))
+
+    def enqueue(payload, sections):
+        store = {}
+        queue.extend((store, k, payload, sections) for k in shifts)
+        return store
 
     fbufs, bbufs = None, None
     frecv = inputs[0]
     brecv = inputs[0]
     last = n_sec - 1
+    edge = jnp.where(sec == 0, inputs, cotangent)
+    far_edge = enqueue(lambda: edge, (0, last))
 
     def forward(t):
         nonlocal fbufs, frecv
@@ -743,28 +792,88 @@
         if pairs:
             brecv = lax.ppermute(out, "section", pairs)
 
+    def forward_far(m, live, sources, source, index):
+        nonlocal fbufs
+        (sc,) = chained(flags(live, m, source, index))
+        hidb, slpb, nrmb, xb, lowf = fbufs
+        hidb, slpb, nrmb, lowf, state["token"] = fwd_far(dims, sc, upo, sources, weights, (hidb, slpb, nrmb, lowf), half)
+        fbufs = (hidb, slpb, nrmb, xb, lowf)
+
     slots = micro + last
+    half = micro // 2
+    early, late = slice(0, half), slice(half, micro)
+    inner, outer = list(range(1, n_sec)), list(range(last))
+
+    def triple(store):
+        return tuple(store[k] for k in range(1, n_dp))
+
     for t in range(slots):
+        if t == slots - 1:
+            forward_far(0, sec == 0, [triple(far_edge)], 0, 0)
         forward(t)
+        if t < last:
+            send_one(3)
+        if t == slots - 1:
+            x_late = enqueue(lambda: fbufs[3][late], inner)
+        if t > last + 1:
+            send_one(1)
         if t >= last:
             backward(t - last)
+        if t == last + 1:
+            x_early = enqueue(lambda: fbufs[3][early], inner)
+        if t > last:
+            send_one(1)
+        if t == slots - 1:
+            send_one(1)
+
     for t in range(slots - last, slots):
         backward(t)
+        if t == slots - 3:
+            g_early = enqueue(lambda: bbufs[1][early, 0:rows], outer)
+        if t == slots - 1:
+            g_late = enqueue(lambda: bbufs[1][late, 0:rows], outer)
+        hold = 2 if t == slots - 1 else 1
+        send_one(hold)
+        if t != slots - 2:
+            send_one(hold)
+    gpb, gb, lowb, gain_rows = bbufs
+
+    def far_forward(m, hold):
+        if m < half:
+            forward_far(m, sec > 0, [triple(x_early)], 0, m)
+        else:
+            forward_far(m, True, [triple(x_late), triple(far_edge)],
+                        jnp.where(sec == 0, 1, 0), jnp.where(sec == 0, m, m - half))
+        send_one(hold)
+
+    def far_backward(m):
+        nonlocal gpb, gb, lowb
+        sources = [triple(g_early if m < half else g_late), triple(far_edge)]
+        (sc,) = chained(flags(True, m, jnp.where(sec == last, 1, 0), jnp.where(sec == last, m, m % half)))
+        gpb, gb, lowb, state["token"] = bwd_far(dims, sc, dno, sources, weights, fbufs[1], (gpb, gb, lowb), half)
+        send_one(1)
+
+    far_forward(0, 2)
+    far_forward(half, 1)
+    far_backward(0)
+    while queue:
+        send_one(2)
+    gain = jnp.sum(gain_rows, axis=(0, 1))[None]
+    for other in to_dp(gain, range(n_sec)):
+        gain = gain + other
+    far_backward(half)
     hidb, slpb, nrmb, _, lowf = fbufs
-    gpb, gb, lowb, gainb = bbufs
     sc = scalars(zero, sec == 0)
 
     def over_fsdp(pieces):
         if parts == 2:
             got = lax.ppermute(pieces[1], "fsdp", swap)
-            return (pieces[0].astype(F32) + got.astype(F32)).astype(BF)
-        return lax.psum_scatter(pieces[0], "fsdp", scatter_dimension=0, tiled=False)
-
-    gain = jnp.sum(gainb, axis=(0, 1))[None]
+            return (pieces[0].astype(F32) + got.astype(F32))[None]
+        return lax.psum_scatter(pieces[0], "fsdp", scatter_dimension=0, tiled=False).astype(F32)[None]
+
     dn_g, dn_small = weight_grads(dims, False, sc, dno, hidb, gb, lowb, lowf)
     up_g, up_small = weight_grads(dims, True, sc, grouped, gpb, nrmb, lowf, lowb, gain)
-    sums = lax.psum([over_fsdp(p) for p in (dn_g, dn_small, up_g, up_small)], "dp")
-    dn, dns, up, ups = (s[None].astype(F32) for s in sums)
+    dn, dns, up, ups = (over_fsdp(p) for p in (dn_g, dn_small, up_g, up_small))
     mw, hw = dims.mh * BLK, dims.hh * BLK
     return (
         ups[:, 0, mw + hw :],

time: 479 us -> 466 us (0.973)
  waiting for transfers between devices: 265 us -> 91.4 us
  Pallas kernels: 110 us -> 226 us
  starting transfers between devices: 35.5 us -> 95.2 us
  between operations: 14.5 us -> 1.52 us
  local copies, waits for them, and re-layouts: 30.6 us -> 38.5 us
  other arithmetic: 17 us -> 10.2 us
    psum x1 -> x0, waiting for transfers between devices: 205 us -> none  [shards(): lax.psum([over_fsdp(p) for p in (dn_g, dn_small, up_g, up_small)], 'dp')]
    pallas_call x0 -> x5, Pallas kernels: none -> 105 us  [the longest x3 67 us: fwd_far(): pl.pallas_call(kernel, out_shape=tuple((jax.ShapeDtypeStruct(b.shape, b.d...]
    ppermute x0 -> x18, starting transfers between devices: none -> 57.8 us  [shifted(): return lax.ppermute(block, ('section', 'dp'), pairs)]
    ppermute x0 -> x18, waiting for transfers between devices: none -> 43.3 us  [shifted(): return lax.ppermute(block, ('section', 'dp'), pairs)]
    convert_element_type x7 -> x0, other arithmetic: 14.8 us -> none  [shards(): dn, dns, up, ups = (s[None].astype(F32) for s in sums)]
    pallas_call x2, Pallas kernels: 21.2 us -> 31.6 us  [weight_grads(): pl.pallas_call(kernel, out_shape=tuple(shapes), in_specs=[SMEM] * 2 + [AN...]
    ppermute x6, waiting for transfers between devices: 17 us -> 7.67 us  [backward(): brecv = lax.ppermute(out, 'section', pairs)]
    broadcast_in_dim x0 -> x4, other arithmetic: none -> 6.8 us  [over_fsdp(): return (pieces[0].astype(F32) + got.astype(F32))[None]]
  transfers between devices with their start and end apart: 20 -> 37, of which waited for: 10 -> 12; matrix products, arithmetic and copies ran while one was open for 5% -> 8% of each run, Pallas kernels for 11% -> 46%
where the time goes in v4:
time: 466 us; the launch traced here: 463 us
  Pallas kernels  226 us (48%)
  starting transfers between devices  95.2 us (20%)
  waiting for transfers between devices  91.4 us (20%)
  local copies, waits for them, and re-layouts  38.5 us (8%)
  other arithmetic  10.2 us (2%)
    pallas_call x3, Pallas kernels, fwd_far(): pl.pallas_call(kernel, out_shape=tuple((jax.ShapeDtypeStruct(b.shape, b.d...  67 us
    ppermute x18, starting transfers between devices, shifted(): return lax.ppermute(block, ('section', 'dp'), pairs)  57.8 us
    pallas_call x7, Pallas kernels, bwd_slot(): pl.pallas_call(kernel, out_shape=(jax.ShapeDtypeStruct((rows, dims.width)...  49.1 us
    ppermute x18, waiting for transfers between devices, shifted(): return lax.ppermute(block, ('section', 'dp'), pairs)  43.3 us
    pallas_call x7, Pallas kernels, fwd_slot(): pl.pallas_call(kernel, out_shape=(jax.ShapeDtypeStruct((rows, dims.width)...  40.1 us
    pallas_call x2, Pallas kernels, bwd_far(): pl.pallas_call(kernel, out_shape=tuple((jax.ShapeDtypeStruct(b.shape, b.d...  38.4 us
    ppermute x6, waiting for transfers between devices, forward(): frecv = lax.ppermute(y, 'section', pairs)  37.1 us
    pallas_call x2, Pallas kernels, weight_grads(): pl.pallas_call(kernel, out_shape=tuple(shapes), in_specs=[SMEM] * 2 + [AN...  31.6 us
  transfers between devices with their start and end apart: 37, of which 12 were waited for; matrix products, arithmetic and copies ran while one was open for 8% of the time, Pallas kernels for 46%

profile of v4, /device:TPU:13, one launch (start us, length us, event | category | flops | bytes accessed | tf_op | source)
XLA Modules:
  0.0 463.0 jit_solution(4070980910710555901)
XLA Ops:
  19.1 28.3 %collective-permute-done.5.refs_4_ = bf16[32,4096]{1,0:T(8,128)(2,1)S(1)} collective-permute-done((bf16[32,4096]{1,0:T(8,128)(2,1)}, bf16[32,4096]{1,0:T(8,128)(2,1)S(1)}, u32[]{:S(2)}, u32[]{:S(2)}) %collective-permute-start.5) | collective-permute-done | bytes 262176 | tf_op jit(solution)/shard_map/ppermute | solution.py:783
  48.1 9.4 %forward_rows.9 = (bf16[32,4096]{1,0:T(8,128)(2,1)}, bf16[4,128,128,128]{3,2,1,0:T(8,128)(2,1)}, bf16[4,128,128,128]{3,2,1,0:T(8,128)(2,1)}, bf16[4,128,4096]{2,...) custom-call(s32[8]{0:T(128)} %stack.303.refs_0_, ...), custom_call_target="tpu_custom_call", output_to_operand_aliasing={{1}: (11, {}), {2}: (12, {}), {3}: (13, {}), {4}: (14, {}),... | custom-call | tf_op jit(solution)/shard_map/forward_rows/pallas_call | solution.py:302
  62.7 6.7 %collective-permute-done.6.refs_4_ = bf16[32,4096]{1,0:T(8,128)(2,1)S(1)} collective-permute-done((bf16[32,4096]{1,0:T(8,128)(2,1)}, bf16[32,4096]{1,0:T(8,128)(2,1)S(1)}, u32[]{:S(2)}, u32[]{:S(2)}) %collective-permute-start.6) | collective-permute-done | bytes 262176 | tf_op jit(solution)/shard_map/ppermute | solution.py:783
  70.0 9.3 %forward_rows.10 = (bf16[32,4096]{1,0:T(8,128)(2,1)}, bf16[4,128,128,128]{3,2,1,0:T(8,128)(2,1)}, bf16[4,128,128,128]{3,2,1,0:T(8,128)(2,1)}, bf16[4,128,4096]{2...) custom-call(s32[8]{0:T(128)} %stack.299.refs_0_, ...), custom_call_target="tpu_custom_call", output_to_operand_aliasing={{1}: (11, {}), {2}: (12, {}), {3}: (13, {}), {4}: (14, {}),... | custom-call | tf_op jit(solution)/shard_map/forward_rows/pallas_call | solution.py:302
  88.3 9.3 %forward_rows.11 = (bf16[32,4096]{1,0:T(8,128)(2,1)}, bf16[4,128,128,128]{3,2,1,0:T(8,128)(2,1)}, bf16[4,128,128,128]{3,2,1,0:T(8,128)(2,1)}, bf16[4,128,4096]{2...) custom-call(s32[8]{0:T(128)} %stack.311.refs_0_, ...), custom_call_target="tpu_custom_call", output_to_operand_aliasing={{1}: (11, {}), {2}: (12, {}), {3}: (13, {}), {4}: (14, {}),... | custom-call | tf_op jit(solution)/shard_map/forward_rows/pallas_call | solution.py:302
  99.4 11.7 %backward_rows.8 = (bf16[32,4096]{1,0:T(8,128)(2,1)}, bf16[4,128,128,128]{3,2,1,0:T(8,128)(2,1)}, bf16[4,128,4096]{2,1,0:T(8,128)(2,1)}, bf16[4,128,256]{2,1,0:T(8,128)(2,1)}, f32[4,8,4096]{2,1,0:T(8,128)}) custom-call(s32[8]{0:T(128)} %stack.287.refs_0_, s32[128]{0:T(128)} %bitcast.108, ...), custom_call_target="tpu_custom_call", output_to_operand_aliasing={{1}: (13, {}), {2}: (14, {}), {3}: (15, {}), {4}: (16, {})} | custom-call | tf_op jit(solution)/shard_map/backward_rows/pallas_call | solution.py:397
  114.3 13.7 %collective-permute-start.13 = (bf16[32,4096]{1,0:T(8,128)(2,1)S(1)}, bf16[32,4096]{1,0:T(8,128)(2,1)S(1)}, u32[]{:S(2)}, u32[]{:S(2)}) collective-permute-start(bf16[32,4096]{1,0:T(8,128)(2,1)S(1)} %copy-done.38), channel_id=1, source_target_pairs={{8,16},{16,24},{9,17},{17,25},{10,18},{18,26},{11,19},{19,27},{12,... | collective-permute-start | bytes 786440 | tf_op jit(solution)/shard_map/ppermute | solution.py:783
  132.0 9.5 %forward_rows.12 = (bf16[32,4096]{1,0:T(8,128)(2,1)}, bf16[4,128,128,128]{3,2,1,0:T(8,128)(2,1)}, bf16[4,128,128,128]{3,2,1,0:T(8,128)(2,1)}, bf16[4,128,4096]{2...) custom-call(s32[8]{0:T(128)} %stack.315.refs_0_, ...), custom_call_target="tpu_custom_call", output_to_operand_aliasing={{1}: (11, {}), {2}: (12, {}), {3}: (13, {}), {4}: (14, {}),... | custom-call | tf_op jit(solution)/shard_map/forward_rows/pallas_call | solution.py:302
  147.1 11.7 %backward_rows.9 = (bf16[32,4096]{1,0:T(8,128)(2,1)}, bf16[4,128,128,128]{3,2,1,0:T(8,128)(2,1)}, bf16[4,128,4096]{2,1,0:T(8,128)(2,1)}, bf16[4,128,256]{2,1,0:T(8,128)(2,1)}, f32[4,8,4096]{2,1,0:T(8,128)}) custom-call(s32[8]{0:T(128)} %stack.283.refs_0_, s32[128]{0:T(128)} %bitcast.110, ...), custom_call_target="tpu_custom_call", output_to_operand_aliasing={{1}: (13, {}), {2}: (14, {}), {3}: (15, {}), {4}: (16, {})} | custom-call | tf_op jit(solution)/shard_map/backward_rows/pallas_call | solution.py:397
  158.8 5.5 %collective-permute-start.16 = (bf16[2,32,4096]{2,1,0:T(8,128)(2,1)S(1)}, bf16[2,32,4096]{2,1,0:T(8,128)(2,1)S(1)}, u32[]{:S(2)}, u32[]{:S(2)}) collective-permute-start(bf16[2,32,4096]{2,1,0:T(8,128)(2,1)S(1)} %slice.45), channel_id=1, source_target_pairs={{8,10},{9,11},{10,8},{11,9},{16,18},{17,19},{18,16},{19,17},{24,26... | collective-permute-start | bytes 1572872 | tf_op jit(solution)/shard_map/ppermute | solution.py:734
  172.7 13.6 %collective-permute-done.16.refs_7_ = bf16[2,32,4096]{2,1,0:T(8,128)(2,1)S(1)} collective-permute-done((bf16[2,32,4096]{2,1,0:T(8,128)(2,1)S(1)}, bf16[2,32,4096]{2,1,0:T(8,128)(2,1)S(1)}, u32[]{:S(2)}, u32[]{:S(2)}) %collective-permute-start.16) | collective-permute-done | bytes 524320 | tf_op jit(solution)/shard_map/ppermute | solution.py:734
  192.4 11.6 %backward_rows.10 = (bf16[32,4096]{1,0:T(8,128)(2,1)}, bf16[4,128,128,128]{3,2,1,0:T(8,128)(2,1)}, bf16[4,128,4096]{2,1,0:T(8,128)(2,1)}, bf16[4,128,256]{2,1,0:T(8,128)(2,1)}, f32[4,8,4096]{2,1,0:T(8,128)}) custom-call(s32[8]{0:T(128)} %stack.279.refs_0_, ...), custom_call_target="tpu_custom_call", output_to_operand_aliasing={{1}: (13, {}), {2}: (14, {}), {3}: (15, {}), {4}: (16, {})} | custom-call | tf_op jit(solution)/shard_map/backward_rows/pallas_call | solution.py:397
  214.4 7.7 %collective-permute-done.18.refs_4_ = bf16[32,4096]{1,0:T(8,128)(2,1)S(1)} collective-permute-done((bf16[32,4096]{1,0:T(8,128)(2,1)}, bf16[32,4096]{1,0:T(8,128)(2,1)S(1)}, u32[]{:S(2)}, u32[]{:S(2)}) %collective-permute-start.18) | collective-permute-done | bytes 262176 | tf_op jit(solution)/shard_map/ppermute | solution.py:793
  222.8 11.6 %backward_rows.11 = (bf16[32,4096]{1,0:T(8,128)(2,1)}, bf16[4,128,128,128]{3,2,1,0:T(8,128)(2,1)}, bf16[4,128,4096]{2,1,0:T(8,128)(2,1)}, bf16[4,128,256]{2,1,0:T(8,128)(2,1)}, f32[4,8,4096]{2,1,0:T(8,128)}) custom-call(s32[8]{0:T(128)} %stack.275.refs_0_, ...), custom_call_target="tpu_custom_call", output_to_operand_aliasing={{1}: (13, {}), {2}: (14, {}), {3}: (15, {}), {4}: (16, {})} | custom-call | tf_op jit(solution)/shard_map/backward_rows/pallas_call | solution.py:397
  249.5 5.0 %collective-permute-start.26 = (bf16[2,32,4096]{2,1,0:T(8,128)(2,1)S(1)}, bf16[2,32,4096]{2,1,0:T(8,128)(2,1)S(1)}, u32[]{:S(2)}, u32[]{:S(2)}) collective-permute-start(bf16[2,32,4096]{2,1,0:T(8,128)(2,1)S(1)} %slice.49), channel_id=1, source_target_pairs={{0,2},{1,3},{2,0},{3,1},{8,10},{9,11},{10,8},{11,9},{16,18},{17,19... | collective-permute-start | bytes 1572872 | tf_op jit(solution)/shard_map/ppermute | solution.py:734
  255.8 24.7 %collective-permute-done.24.refs_6_ = bf16[2,32,4096]{2,1,0:T(8,128)(2,1)S(1)} collective-permute-done((bf16[2,32,4096]{2,1,0:T(8,128)(2,1)S(1)}, bf16[2,32,4096]{2,1,0:T(8,128)(2,1)S(1)}, u32[]{:S(2)}, u32[]{:S(2)}) %collective-permute-start.24) | collective-permute-done | bytes 524320 | tf_op jit(solution)/shard_map/ppermute | solution.py:734
  291.8 33.3 %forward_far_rows.4 = (bf16[4,128,128,128]{3,2,1,0:T(8,128)(2,1)}, bf16[4,128,128,128]{3,2,1,0:T(8,128)(2,1)}, bf16[4,128,4096]{2,1,0:T(8,128)(2,1)}, bf16[4,128,256]{2,1,0:T(8,128)(2,1)}, f32[8,128]{1,0:T(8,128)}) custom-call(s32[8]{0:T(128)} %stack.323.refs_0_, ...), custom_call_target="tpu_custom_call", output_to_operand_aliasing={{0}: (9, {}), {1}: (10, {}), {2}: (11, {}), {3}: (12, {})} | custom-call | tf_op jit(solution)/shard_map/forward_far_rows/pallas_call | solution.py:480
  325.2 5.0 %collective-permute-start.27 = (bf16[2,32,4096]{2,1,0:T(8,128)(2,1)S(1)}, bf16[2,32,4096]{2,1,0:T(8,128)(2,1)S(1)}, u32[]{:S(2)}, u32[]{:S(2)}) collective-permute-start(bf16[2,32,4096]{2,1,0:T(8,128)(2,1)S(1)} %slice.48), channel_id=1, source_target_pairs={{0,2},{1,3},{2,0},{3,1},{8,10},{9,11},{10,8},{11,9},{16,18},{17,19... | collective-permute-start | bytes 1572872 | tf_op jit(solution)/shard_map/ppermute | solution.py:734
  330.3 7.0 %collective-permute-start.32 = (f32[1,4096]{1,0:T(1,128)S(1)}, f32[1,4096]{1,0:T(1,128)S(1)}, u32[]{:S(2)}, u32[]{:S(2)}) collective-permute-start(f32[1,4096]{1,0:T(1,128)S(1)} %bitcast.119), channel_id=1, source_target_pairs={{0,3},{1,0},{2,1},{3,2},{8,11},{9,8},{10,9},{11,10},{16,19},{17,16... | collective-permute-start | bytes 49160 | tf_op jit(solution)/shard_map/ppermute | solution.py:734
  342.2 32.8 %forward_far_rows.5 = (bf16[4,128,128,128]{3,2,1,0:T(8,128)(2,1)}, bf16[4,128,128,128]{3,2,1,0:T(8,128)(2,1)}, bf16[4,128,4096]{2,1,0:T(8,128)(2,1)}, bf16[4,128,256]{2,1,0:T(8,128)(2,1)}, f32[8,128]{1,0:T(8,128)}) custom-call(s32[8]{0:T(128)} %stack.326.refs_0_, ...), custom_call_target="tpu_custom_call", output_to_operand_aliasing={{0}: (12, {}), {1}: (13, {}), {2}: (14, {}), {3}: (15, {})} | custom-call | tf_op jit(solution)/shard_map/forward_far_rows/pallas_call | solution.py:480
  375.0 19.2 %backward_far_rows.2 = (bf16[4,128,128,128]{3,2,1,0:T(8,128)(2,1)}, bf16[4,128,4096]{2,1,0:T(8,128)(2,1)}, bf16[4,128,256]{2,1,0:T(8,128)(2,1)}, f32[8,128]{1,0:T(8,128)}) custom-call(s32[8]{0:T(128)} %stack.327.refs_0_, s32[128]{0:T(128)} %bitcast.116, ...), custom_call_target="tpu_custom_call", output_to_operand_aliasing={{0}: (13, {}), {1}: (14, {}), {2}: (15, {})} | custom-call | tf_op jit(solution)/shard_map/backward_far_rows/pallas_call | solution.py:556
  395.1 19.2 %backward_far_rows.3 = (bf16[4,128,128,128]{3,2,1,0:T(8,128)(2,1)}, bf16[4,128,4096]{2,1,0:T(8,128)(2,1)}, bf16[4,128,256]{2,1,0:T(8,128)(2,1)}, f32[8,128]{1,0:T(8,128)}) custom-call(s32[8]{0:T(128)} %stack.261.refs_0_, s32[128]{0:T(128)} %bitcast.117, ...), custom_call_target="tpu_custom_call", output_to_operand_aliasing={{0}: (13, {}), {1}: (14, {}), {2}: (15, {})} | custom-call | tf_op jit(solution)/shard_map/backward_far_rows/pallas_call | solution.py:556
  414.2 15.8 %down_gradients.1 = (bf16[64,128,128]{2,1,0:T(8,128)(2,1)}, bf16[64,128,128]{2,1,0:T(8,128)(2,1)}, bf16[16,10240]{1,0:T(8,128)(2,1)}, bf16[16,10240]{1,0:T(8,128)(2,1)}) custom-call(s32[8]{0:T(128)} %stack.258.refs_0_, s32[128]{0:T(128)} %bitcast.118, bf16[4,128,128,128]{3,2,1,0:T(8,128)(2,1)} %get-tuple-element.269.refs_2_, ...), custom_call_target="tpu_custom_call" | custom-call | tf_op jit(solution)/shard_map/down_gradients/pallas_call | solution.py:673
  433.5 15.8 %up_gradients.1 = (bf16[64,128,128]{2,1,0:T(8,128)(2,1)}, bf16[64,128,128]{2,1,0:T(8,128)(2,1)}, bf16[16,12288]{1,0:T(8,128)(2,1)}, bf16[16,12288]{1,0:T(8,128)(2,1)}) custom-call(s32[8]{0:T(128)} %stack.258.refs_0_, s32[128]{0:T(128)} %select_reduce_fusion.refs_2_.refs_1_, bf16[4,128,128,128]{3,2,1,0:T(8,128)(2,1)} %get-tuple-element.260.refs_2_, ...), custom_call_target="tpu_custom_call" | custom-call | tf_op jit(solution)/shard_map/up_gradients/pallas_call | solution.py:673
  (199 shorter events, 124.3 us)
Async XLA Ops:
  14.6 32.8 %collective-permute-start.5 = (bf16[32,4096]{1,0:T(8,128)(2,1)}, bf16[32,4096]{1,0:T(8,128)(2,1)S(1)}, u32[]{:S(2)}, u32[]{:S(2)}) collective-permute-start(bf16[32,4096]{1,0:T(8,128)(2,1)} %get-tuple-element.149), channel_id=1, source_target_pairs={{0,8},{8,16},{1,9},{9,17},{2,10},{10,18},{3,11},{11,19},{4,12},{12... | collective-permute-start | bytes 786440 | tf_op jit(solution)/shard_map/ppermute | solution.py:783
  17.0 64.9 %collective-permute-start.3 = (bf16[4,32,4096]{2,1,0:T(8,128)(2,1)}, bf16[4,32,4096]{2,1,0:T(8,128)(2,1)S(1)}, u32[]{:S(2)}, u32[]{:S(2)}) collective-permute-start(bf16[4,32,4096]{2,1,0:T(8,128)(2,1)} %broadcast_select_fusion), channel_id=1, source_target_pairs={{0,1},{1,2},{2,3},{3,0},{24,25},{25,26},{26,27},{27,24},{4,5},{5,6... | collective-permute-start | bytes 3145736 | tf_op jit(solution)/shard_map/ppermute | solution.py:734
  18.4 69.2 %collective-permute-start.10 = (bf16[4,32,4096]{2,1,0:T(8,128)(2,1)}, bf16[4,32,4096]{2,1,0:T(8,128)(2,1)S(1)}, u32[]{:S(2)}, u32[]{:S(2)}) collective-permute-start(bf16[4,32,4096]{2,1,0:T(8,128)(2,1)} %broadcast_select_fusion), channel_id=1, source_target_pairs={{0,3},{1,0},{2,1},{3,2},{24,27},{25,24},{26,25},{27,26},{4,7},{5,4... | collective-permute-start | bytes 3145736 | tf_op jit(solution)/shard_map/ppermute | solution.py:734
  57.5 41.1 %collective-permute-start.8 = (bf16[4,32,4096]{2,1,0:T(8,128)(2,1)}, bf16[4,32,4096]{2,1,0:T(8,128)(2,1)}, u32[]{:S(2)}, u32[]{:S(2)}) collective-permute-start(bf16[4,32,4096]{2,1,0:T(8,128)(2,1)} %broadcast_select_fusion), channel_id=1, source_target_pairs={{0,2},{1,3},{2,0},{3,1},{24,26},{25,27},{26,24},{27,25},{4,6},{5,7... | collective-permute-start | bytes 3145736 | tf_op jit(solution)/shard_map/ppermute | solution.py:734
  111.1 35.4 %collective-permute-start.12 = (bf16[2,32,4096]{2,1,0:T(8,128)(2,1)S(1)}, bf16[2,32,4096]{2,1,0:T(8,128)(2,1)S(1)}, u32[]{:S(2)}, u32[]{:S(2)}) collective-permute-start(bf16[2,32,4096]{2,1,0:T(8,128)(2,1)S(1)} %slice.44), channel_id=1, source_target_pairs={{8,9},{9,10},{10,11},{11,8},{16,17},{17,18},{18,19},{19,16},{24,25... | collective-permute-start | bytes 1572872 | tf_op jit(solution)/shard_map/ppermute | solution.py:734
  128.0 18.4 %collective-permute-start.11 = (bf16[32,4096]{1,0:T(8,128)(2,1)}, bf16[32,4096]{1,0:T(8,128)(2,1)S(1)}, u32[]{:S(2)}, u32[]{:S(2)}) collective-permute-start(bf16[32,4096]{1,0:T(8,128)(2,1)} %get-tuple-element.182), channel_id=1, source_target_pairs={{24,16},{16,8},{25,17},{17,9},{26,18},{18,10},{27,19},{19,11},{28,... | collective-permute-start | bytes 786440 | tf_op jit(solution)/shard_map/ppermute | solution.py:793
  142.6 29.2 %collective-permute-start.17 = (bf16[2,32,4096]{2,1,0:T(8,128)(2,1)S(1)}, bf16[2,32,4096]{2,1,0:T(8,128)(2,1)S(1)}, u32[]{:S(2)}, u32[]{:S(2)}) collective-permute-start(bf16[2,32,4096]{2,1,0:T(8,128)(2,1)S(1)} %slice.45), channel_id=1, source_target_pairs={{8,11},{9,8},{10,9},{11,10},{16,19},{17,16},{18,17},{19,18},{24,27... | collective-permute-start | bytes 1572872 | tf_op jit(solution)/shard_map/ppermute | solution.py:734
  158.8 27.4 %collective-permute-start.16 = (bf16[2,32,4096]{2,1,0:T(8,128)(2,1)S(1)}, bf16[2,32,4096]{2,1,0:T(8,128)(2,1)S(1)}, u32[]{:S(2)}, u32[]{:S(2)}) collective-permute-start(bf16[2,32,4096]{2,1,0:T(8,128)(2,1)S(1)} %slice.45), channel_id=1, source_target_pairs={{8,10},{9,11},{10,8},{11,9},{16,18},{17,19},{18,16},{19,17},{24,26... | collective-permute-start | bytes 1572872 | tf_op jit(solution)/shard_map/ppermute | solution.py:734
  169.8 21.9 %collective-permute-start.14 = (bf16[32,4096]{1,0:T(8,128)(2,1)}, bf16[32,4096]{1,0:T(8,128)(2,1)S(1)}, u32[]{:S(2)}, u32[]{:S(2)}) collective-permute-start(bf16[32,4096]{1,0:T(8,128)(2,1)} %get-tuple-element.196), channel_id=1, source_target_pairs={{24,16},{16,8},{8,0},{25,17},{17,9},{9,1},{26,18},{18,10},{10,2},{... | collective-permute-start | bytes 786440 | tf_op jit(solution)/shard_map/ppermute | solution.py:793
  188.1 33.9 %collective-permute-start.19 = (bf16[2,32,4096]{2,1,0:T(8,128)(2,1)S(1)}, bf16[2,32,4096]{2,1,0:T(8,128)(2,1)S(1)}, u32[]{:S(2)}, u32[]{:S(2)}) collective-permute-start(bf16[2,32,4096]{2,1,0:T(8,128)(2,1)S(1)} %slice.46), channel_id=1, source_target_pairs={{8,9},{9,10},{10,11},{11,8},{16,17},{17,18},{18,19},{19,16},{24,25... | collective-permute-start | bytes 1572872 | tf_op jit(solution)/shard_map/ppermute | solution.py:734
  204.0 18.1 %collective-permute-start.18 = (bf16[32,4096]{1,0:T(8,128)(2,1)}, bf16[32,4096]{1,0:T(8,128)(2,1)S(1)}, u32[]{:S(2)}, u32[]{:S(2)}) collective-permute-start(bf16[32,4096]{1,0:T(8,128)(2,1)} %get-tuple-element.216), channel_id=1, source_target_pairs={{24,16},{16,8},{8,0},{25,17},{17,9},{9,1},{26,18},{18,10},{10,2},{... | collective-permute-start | bytes 786440 | tf_op jit(solution)/shard_map/ppermute | solution.py:793
  205.9 37.6 %collective-permute-start.21 = (bf16[2,32,4096]{2,1,0:T(8,128)(2,1)S(1)}, bf16[2,32,4096]{2,1,0:T(8,128)(2,1)S(1)}, u32[]{:S(2)}, u32[]{:S(2)}) collective-permute-start(bf16[2,32,4096]{2,1,0:T(8,128)(2,1)S(1)} %slice.46), channel_id=1, source_target_pairs={{8,11},{9,8},{10,9},{11,10},{16,19},{17,16},{18,17},{19,18},{24,27... | collective-permute-start | bytes 1572872 | tf_op jit(solution)/shard_map/ppermute | solution.py:734
  209.7 37.1 %collective-permute-start.22 = (bf16[2,32,4096]{2,1,0:T(8,128)(2,1)S(1)}, bf16[2,32,4096]{2,1,0:T(8,128)(2,1)S(1)}, u32[]{:S(2)}, u32[]{:S(2)}) collective-permute-start(bf16[2,32,4096]{2,1,0:T(8,128)(2,1)S(1)} %slice.46), channel_id=1, source_target_pairs={{8,10},{9,11},{10,8},{11,9},{16,18},{17,19},{18,16},{19,17},{24,26... | collective-permute-start | bytes 1572872 | tf_op jit(solution)/shard_map/ppermute | solution.py:734
  236.7 43.8 %collective-permute-start.24 = (bf16[2,32,4096]{2,1,0:T(8,128)(2,1)S(1)}, bf16[2,32,4096]{2,1,0:T(8,128)(2,1)S(1)}, u32[]{:S(2)}, u32[]{:S(2)}) collective-permute-start(bf16[2,32,4096]{2,1,0:T(8,128)(2,1)S(1)} %slice.47), channel_id=1, source_target_pairs={{0,1},{1,2},{2,3},{3,0},{8,9},{9,10},{10,11},{11,8},{16,17},{17,18... | collective-permute-start | bytes 1572872 | tf_op jit(solution)/shard_map/ppermute | solution.py:734
  240.0 40.5 %collective-permute-start.25 = (bf16[2,32,4096]{2,1,0:T(8,128)(2,1)S(1)}, bf16[2,32,4096]{2,1,0:T(8,128)(2,1)S(1)}, u32[]{:S(2)}, u32[]{:S(2)}) collective-permute-start(bf16[2,32,4096]{2,1,0:T(8,128)(2,1)S(1)} %slice.47), channel_id=1, source_target_pairs={{0,3},{1,0},{2,1},{3,2},{8,11},{9,8},{10,9},{11,10},{16,19},{17,16... | collective-permute-start | bytes 1572872 | tf_op jit(solution)/shard_map/ppermute | solution.py:734
  249.5 42.3 %collective-permute-start.26 = (bf16[2,32,4096]{2,1,0:T(8,128)(2,1)S(1)}, bf16[2,32,4096]{2,1,0:T(8,128)(2,1)S(1)}, u32[]{:S(2)}, u32[]{:S(2)}) collective-permute-start(bf16[2,32,4096]{2,1,0:T(8,128)(2,1)S(1)} %slice.49), channel_id=1, source_target_pairs={{0,2},{1,3},{2,0},{3,1},{8,10},{9,11},{10,8},{11,9},{16,18},{17,19... | collective-permute-start | bytes 1572872 | tf_op jit(solution)/shard_map/ppermute | solution.py:734
  254.5 26.0 %collective-permute-start.23 = (bf16[32,4096]{1,0:T(8,128)(2,1)}, bf16[32,4096]{1,0:T(8,128)(2,1)S(1)}, u32[]{:S(2)}, u32[]{:S(2)}) collective-permute-start(bf16[32,4096]{1,0:T(8,128)(2,1)} %get-tuple-element.230), channel_id=1, source_target_pairs={{8,0},{9,1},{10,2},{11,3},{12,4},{13,5},{14,6},{15,7}} | collective-permute-start | bytes 786440 | tf_op jit(solution)/shard_map/ppermute | solution.py:793
  283.5 56.1 %collective-permute-start.28 = (bf16[2,32,4096]{2,1,0:T(8,128)(2,1)S(1)}, bf16[2,32,4096]{2,1,0:T(8,128)(2,1)S(1)}, u32[]{:S(2)}, u32[]{:S(2)}) collective-permute-start(bf16[2,32,4096]{2,1,0:T(8,128)(2,1)S(1)} %slice.48), channel_id=1, source_target_pairs={{0,1},{1,2},{2,3},{3,0},{8,9},{9,10},{10,11},{11,8},{16,17},{17,18... | collective-permute-start | bytes 1572872 | tf_op jit(solution)/shard_map/ppermute | solution.py:734
  288.2 86.8 %collective-permute-start.29 = (bf16[2,32,4096]{2,1,0:T(8,128)(2,1)S(1)}, bf16[2,32,4096]{2,1,0:T(8,128)(2,1)S(1)}, u32[]{:S(2)}, u32[]{:S(2)}) collective-permute-start(bf16[2,32,4096]{2,1,0:T(8,128)(2,1)S(1)} %slice.48), channel_id=1, source_target_pairs={{0,3},{1,0},{2,1},{3,2},{8,11},{9,8},{10,9},{11,10},{16,19},{17,16... | collective-permute-start | bytes 1572872 | tf_op jit(solution)/shard_map/ppermute | solution.py:734
  325.2 69.1 %collective-permute-start.27 = (bf16[2,32,4096]{2,1,0:T(8,128)(2,1)S(1)}, bf16[2,32,4096]{2,1,0:T(8,128)(2,1)S(1)}, u32[]{:S(2)}, u32[]{:S(2)}) collective-permute-start(bf16[2,32,4096]{2,1,0:T(8,128)(2,1)S(1)} %slice.48), channel_id=1, source_target_pairs={{0,2},{1,3},{2,0},{3,1},{8,10},{9,11},{10,8},{11,9},{16,18},{17,19... | collective-permute-start | bytes 1572872 | tf_op jit(solution)/shard_map/ppermute | solution.py:734
  330.3 102.6 %collective-permute-start.32 = (f32[1,4096]{1,0:T(1,128)S(1)}, f32[1,4096]{1,0:T(1,128)S(1)}, u32[]{:S(2)}, u32[]{:S(2)}) collective-permute-start(f32[1,4096]{1,0:T(1,128)S(1)} %bitcast.119), channel_id=1, source_target_pairs={{0,3},{1,0},{2,1},{3,2},{8,11},{9,8},{10,9},{11,10},{16,19},{17,16... | collective-permute-start | bytes 49160 | tf_op jit(solution)/shard_map/ppermute | solution.py:734
  337.2 95.7 %collective-permute-start.31 = (f32[1,4096]{1,0:T(1,128)S(1)}, f32[1,4096]{1,0:T(1,128)S(1)}, u32[]{:S(2)}, u32[]{:S(2)}) collective-permute-start(f32[1,4096]{1,0:T(1,128)S(1)} %bitcast.120), channel_id=1, source_target_pairs={{0,2},{1,3},{2,0},{3,1},{8,10},{9,11},{10,8},{11,9},{16,18},{17,19... | collective-permute-start | bytes 49160 | tf_op jit(solution)/shard_map/ppermute | solution.py:734
  339.6 93.3 %collective-permute-start.30 = (f32[1,4096]{1,0:T(1,128)S(1)}, f32[1,4096]{1,0:T(1,128)S(1)}, u32[]{:S(2)}, u32[]{:S(2)}) collective-permute-start(f32[1,4096]{1,0:T(1,128)S(1)} %bitcast.121), channel_id=1, source_target_pairs={{0,1},{1,2},{2,3},{3,0},{8,9},{9,10},{10,11},{11,8},{16,17},{17,18... | collective-permute-start | bytes 49160 | tf_op jit(solution)/shard_map/ppermute | solution.py:734
  430.1 19.9 %collective-permute-start.36 = (bf16[16,10240]{1,0:T(8,128)(2,1)}, bf16[16,10240]{1,0:T(8,128)(2,1)S(1)}, u32[]{:S(2)}, u32[]{:S(2)}) collective-permute-start(bf16[16,10240]{1,0:T(8,128)(2,1)} %get-tuple-element.274), channel_id=1, source_target_pairs={{0,4},{4,0},{1,5},{5,1},{2,6},{6,2},{3,7},{7,3},{8,12},{12,8},{9,1... | collective-permute-start | bytes 983048 | tf_op jit(solution)/shard_map/ppermute | solution.py:870
  (52 other events, 406.7 us)

commit v5 on v4

--- a/solution.py
+++ b/solution.py
@@ -836,15 +836,9 @@
         send_one(hold)
         if t != slots - 2:
             send_one(hold)
+        else:
+            forward_far(0, sec > 0, [triple(x_early)], 0, 0)
     gpb, gb, lowb, gain_rows = bbufs
-
-    def far_forward(m, hold):
-        if m < half:
-            forward_far(m, sec > 0, [triple(x_early)], 0, m)
-        else:
-            forward_far(m, True, [triple(x_late), triple(far_edge)],
-                        jnp.where(sec == 0, 1, 0), jnp.where(sec == 0, m, m - half))
-        send_one(hold)
 
     def far_backward(m):
         nonlocal gpb, gb, lowb
@@ -853,8 +847,8 @@
         gpb, gb, lowb, state["token"] = bwd_far(dims, sc, dno, sources, weights, fbufs[1], (gpb, gb, lowb), half)
         send_one(1)
 
-    far_forward(0, 2)
-    far_forward(half, 1)
+    forward_far(half, True, [triple(x_late), triple(far_edge)], jnp.where(sec == 0, 1, 0), jnp.where(sec == 0, half, 0))
+    send_one(1)
     far_backward(0)
     while queue:
         send_one(2)

time: 466 us -> 453 us (0.972)
  starting transfers between devices: 95.2 us -> 88.4 us
  waiting for transfers between devices: 91.4 us -> 86.7 us
    ppermute x18, starting transfers between devices: 57.8 us -> 50.9 us  [shifted(): return lax.ppermute(block, ('section', 'dp'), pairs)]
  transfers between devices with their start and end apart: 37 -> 37, of which waited for: 12 -> 12; matrix products, arithmetic and copies ran while one was open for 8% -> 8% of each run, Pallas kernels for 46% -> 47%
where the time goes in v5:
time: 453 us; the launch traced here: 452 us
  Pallas kernels  226 us (50%)
  starting transfers between devices  88.4 us (20%)
  waiting for transfers between devices  86.7 us (19%)
  local copies, waits for them, and re-layouts  38.6 us (9%)
  other arithmetic  10.2 us (2%)
    pallas_call x3, Pallas kernels, fwd_far(): pl.pallas_call(kernel, out_shape=tuple((jax.ShapeDtypeStruct(b.shape, b.d...  67.2 us
    ppermute x18, starting transfers between devices, shifted(): return lax.ppermute(block, ('section', 'dp'), pairs)  50.9 us
    pallas_call x7, Pallas kernels, bwd_slot(): pl.pallas_call(kernel, out_shape=(jax.ShapeDtypeStruct((rows, dims.width)...  48.9 us
    pallas_call x7, Pallas kernels, fwd_slot(): pl.pallas_call(kernel, out_shape=(jax.ShapeDtypeStruct((rows, dims.width)...  40.1 us
    ppermute x18, waiting for transfers between devices, shifted(): return lax.ppermute(block, ('section', 'dp'), pairs)  38.7 us
    pallas_call x2, Pallas kernels, bwd_far(): pl.pallas_call(kernel, out_shape=tuple((jax.ShapeDtypeStruct(b.shape, b.d...  38.4 us
    ppermute x6, waiting for transfers between devices, forward(): frecv = lax.ppermute(y, 'section', pairs)  37.2 us
    pallas_call x2, Pallas kernels, weight_grads(): pl.pallas_call(kernel, out_shape=tuple(shapes), in_specs=[SMEM] * 2 + [AN...  31.6 us
  transfers between devices with their start and end apart: 37, of which 12 were waited for; matrix products, arithmetic and copies ran while one was open for 8% of the time, Pallas kernels for 47%

profile of v5, /device:TPU:13, one launch (start us, length us, event | category | flops | bytes accessed | tf_op | source)
XLA Modules:
  0.0 451.5 jit_solution(6258353524861297976)
XLA Ops:
  19.1 28.3 %collective-permute-done.5.refs_4_ = bf16[32,4096]{1,0:T(8,128)(2,1)S(1)} collective-permute-done((bf16[32,4096]{1,0:T(8,128)(2,1)}, bf16[32,4096]{1,0:T(8,128)(2,1)S(1)}, u32[]{:S(2)}, u32[]{:S(2)}) %collective-permute-start.5) | collective-permute-done | bytes 262176 | tf_op jit(solution)/shard_map/ppermute | solution.py:783
  48.2 9.5 %forward_rows.9 = (bf16[32,4096]{1,0:T(8,128)(2,1)}, bf16[4,128,128,128]{3,2,1,0:T(8,128)(2,1)}, bf16[4,128,128,128]{3,2,1,0:T(8,128)(2,1)}, bf16[4,128,4096]{2,...) custom-call(s32[8]{0:T(128)} %stack.303.refs_0_, ...), custom_call_target="tpu_custom_call", output_to_operand_aliasing={{1}: (11, {}), {2}: (12, {}), {3}: (13, {}), {4}: (14, {}),... | custom-call | tf_op jit(solution)/shard_map/forward_rows/pallas_call | solution.py:302
  62.7 6.7 %collective-permute-done.6.refs_4_ = bf16[32,4096]{1,0:T(8,128)(2,1)S(1)} collective-permute-done((bf16[32,4096]{1,0:T(8,128)(2,1)}, bf16[32,4096]{1,0:T(8,128)(2,1)S(1)}, u32[]{:S(2)}, u32[]{:S(2)}) %collective-permute-start.6) | collective-permute-done | bytes 262176 | tf_op jit(solution)/shard_map/ppermute | solution.py:783
  70.1 9.3 %forward_rows.10 = (bf16[32,4096]{1,0:T(8,128)(2,1)}, bf16[4,128,128,128]{3,2,1,0:T(8,128)(2,1)}, bf16[4,128,128,128]{3,2,1,0:T(8,128)(2,1)}, bf16[4,128,4096]{2...) custom-call(s32[8]{0:T(128)} %stack.299.refs_0_, ...), custom_call_target="tpu_custom_call", output_to_operand_aliasing={{1}: (11, {}), {2}: (12, {}), {3}: (13, {}), {4}: (14, {}),... | custom-call | tf_op jit(solution)/shard_map/forward_rows/pallas_call | solution.py:302
  88.4 9.3 %forward_rows.11 = (bf16[32,4096]{1,0:T(8,128)(2,1)}, bf16[4,128,128,128]{3,2,1,0:T(8,128)(2,1)}, bf16[4,128,128,128]{3,2,1,0:T(8,128)(2,1)}, bf16[4,128,4096]{2...) custom-call(s32[8]{0:T(128)} %stack.311.refs_0_, ...), custom_call_target="tpu_custom_call", output_to_operand_aliasing={{1}: (11, {}), {2}: (12, {}), {3}: (13, {}), {4}: (14, {}),... | custom-call | tf_op jit(solution)/shard_map/forward_rows/pallas_call | solution.py:302
  99.5 11.7 %backward_rows.8 = (bf16[32,4096]{1,0:T(8,128)(2,1)}, bf16[4,128,128,128]{3,2,1,0:T(8,128)(2,1)}, bf16[4,128,4096]{2,1,0:T(8,128)(2,1)}, bf16[4,128,256]{2,1,0:T(8,128)(2,1)}, f32[4,8,4096]{2,1,0:T(8,128)}) custom-call(s32[8]{0:T(128)} %stack.287.refs_0_, s32[128]{0:T(128)} %bitcast.108, ...), custom_call_target="tpu_custom_call", output_to_operand_aliasing={{1}: (13, {}), {2}: (14, {}), {3}: (15, {}), {4}: (16, {})} | custom-call | tf_op jit(solution)/shard_map/backward_rows/pallas_call | solution.py:397
  114.5 13.5 %collective-permute-start.13 = (bf16[32,4096]{1,0:T(8,128)(2,1)S(1)}, bf16[32,4096]{1,0:T(8,128)(2,1)S(1)}, u32[]{:S(2)}, u32[]{:S(2)}) collective-permute-start(bf16[32,4096]{1,0:T(8,128)(2,1)S(1)} %copy-done.38), channel_id=1, source_target_pairs={{8,16},{16,24},{9,17},{17,25},{10,18},{18,26},{11,19},{19,27},{12,... | collective-permute-start | bytes 786440 | tf_op jit(solution)/shard_map/ppermute | solution.py:783
  132.0 9.5 %forward_rows.12 = (bf16[32,4096]{1,0:T(8,128)(2,1)}, bf16[4,128,128,128]{3,2,1,0:T(8,128)(2,1)}, bf16[4,128,128,128]{3,2,1,0:T(8,128)(2,1)}, bf16[4,128,4096]{2...) custom-call(s32[8]{0:T(128)} %stack.315.refs_0_, ...), custom_call_target="tpu_custom_call", output_to_operand_aliasing={{1}: (11, {}), {2}: (12, {}), {3}: (13, {}), {4}: (14, {}),... | custom-call | tf_op jit(solution)/shard_map/forward_rows/pallas_call | solution.py:302
  147.2 11.7 %backward_rows.9 = (bf16[32,4096]{1,0:T(8,128)(2,1)}, bf16[4,128,128,128]{3,2,1,0:T(8,128)(2,1)}, bf16[4,128,4096]{2,1,0:T(8,128)(2,1)}, bf16[4,128,256]{2,1,0:T(8,128)(2,1)}, f32[4,8,4096]{2,1,0:T(8,128)}) custom-call(s32[8]{0:T(128)} %stack.283.refs_0_, s32[128]{0:T(128)} %bitcast.110, ...), custom_call_target="tpu_custom_call", output_to_operand_aliasing={{1}: (13, {}), {2}: (14, {}), {3}: (15, {}), {4}: (16, {})} | custom-call | tf_op jit(solution)/shard_map/backward_rows/pallas_call | solution.py:397
  158.9 5.5 %collective-permute-start.16 = (bf16[2,32,4096]{2,1,0:T(8,128)(2,1)S(1)}, bf16[2,32,4096]{2,1,0:T(8,128)(2,1)S(1)}, u32[]{:S(2)}, u32[]{:S(2)}) collective-permute-start(bf16[2,32,4096]{2,1,0:T(8,128)(2,1)S(1)} %slice.45), channel_id=1, source_target_pairs={{8,10},{9,11},{10,8},{11,9},{16,18},{17,19},{18,16},{19,17},{24,26... | collective-permute-start | bytes 1572872 | tf_op jit(solution)/shard_map/ppermute | solution.py:734
  172.7 13.6 %collective-permute-done.16.refs_7_ = bf16[2,32,4096]{2,1,0:T(8,128)(2,1)S(1)} collective-permute-done((bf16[2,32,4096]{2,1,0:T(8,128)(2,1)S(1)}, bf16[2,32,4096]{2,1,0:T(8,128)(2,1)S(1)}, u32[]{:S(2)}, u32[]{:S(2)}) %collective-permute-start.16) | collective-permute-done | bytes 524320 | tf_op jit(solution)/shard_map/ppermute | solution.py:734
  192.5 11.5 %backward_rows.10 = (bf16[32,4096]{1,0:T(8,128)(2,1)}, bf16[4,128,128,128]{3,2,1,0:T(8,128)(2,1)}, bf16[4,128,4096]{2,1,0:T(8,128)(2,1)}, bf16[4,128,256]{2,1,0:T(8,128)(2,1)}, f32[4,8,4096]{2,1,0:T(8,128)}) custom-call(s32[8]{0:T(128)} %stack.279.refs_0_, ...), custom_call_target="tpu_custom_call", output_to_operand_aliasing={{1}: (13, {}), {2}: (14, {}), {3}: (15, {}), {4}: (16, {})} | custom-call | tf_op jit(solution)/shard_map/backward_rows/pallas_call | solution.py:397
  205.9 5.9 %collective-permute-start.22 = (bf16[2,32,4096]{2,1,0:T(8,128)(2,1)S(1)}, bf16[2,32,4096]{2,1,0:T(8,128)(2,1)S(1)}, u32[]{:S(2)}, u32[]{:S(2)}) collective-permute-start(bf16[2,32,4096]{2,1,0:T(8,128)(2,1)S(1)} %slice.46), channel_id=1, source_target_pairs={{8,10},{9,11},{10,8},{11,9},{16,18},{17,19},{18,16},{19,17},{24,26... | collective-permute-start | bytes 1572872 | tf_op jit(solution)/shard_map/ppermute | solution.py:734
  214.4 7.7 %collective-permute-done.18.refs_4_ = bf16[32,4096]{1,0:T(8,128)(2,1)S(1)} collective-permute-done((bf16[32,4096]{1,0:T(8,128)(2,1)}, bf16[32,4096]{1,0:T(8,128)(2,1)S(1)}, u32[]{:S(2)}, u32[]{:S(2)}) %collective-permute-start.18) | collective-permute-done | bytes 262176 | tf_op jit(solution)/shard_map/ppermute | solution.py:793
  222.8 11.6 %backward_rows.11 = (bf16[32,4096]{1,0:T(8,128)(2,1)}, bf16[4,128,128,128]{3,2,1,0:T(8,128)(2,1)}, bf16[4,128,4096]{2,1,0:T(8,128)(2,1)}, bf16[4,128,256]{2,1,0:T(8,128)(2,1)}, f32[4,8,4096]{2,1,0:T(8,128)}) custom-call(s32[8]{0:T(128)} %stack.275.refs_0_, ...), custom_call_target="tpu_custom_call", output_to_operand_aliasing={{1}: (13, {}), {2}: (14, {}), {3}: (15, {}), {4}: (16, {})} | custom-call | tf_op jit(solution)/shard_map/backward_rows/pallas_call | solution.py:397
  243.5 11.1 %collective-permute-done.22.refs_7_ = bf16[2,32,4096]{2,1,0:T(8,128)(2,1)S(1)} collective-permute-done((bf16[2,32,4096]{2,1,0:T(8,128)(2,1)S(1)}, bf16[2,32,4096]{2,1,0:T(8,128)(2,1)S(1)}, u32[]{:S(2)}, u32[]{:S(2)}) %collective-permute-start.22) | collective-permute-done | bytes 524320 | tf_op jit(solution)/shard_map/ppermute | solution.py:734
  257.4 5.5 %collective-permute-start.24 = (bf16[2,32,4096]{2,1,0:T(8,128)(2,1)S(1)}, bf16[2,32,4096]{2,1,0:T(8,128)(2,1)S(1)}, u32[]{:S(2)}, u32[]{:S(2)}) collective-permute-start(bf16[2,32,4096]{2,1,0:T(8,128)(2,1)S(1)} %slice.47), channel_id=1, source_target_pairs={{0,2},{1,3},{2,0},{3,1},{8,10},{9,11},{10,8},{11,9},{16,18},{17,19... | collective-permute-start | bytes 1572872 | tf_op jit(solution)/shard_map/ppermute | solution.py:734
  264.9 13.7 %collective-permute-done.26.refs_8_ = bf16[2,32,4096]{2,1,0:T(8,128)(2,1)S(1)} collective-permute-done((bf16[2,32,4096]{2,1,0:T(8,128)(2,1)S(1)}, bf16[2,32,4096]{2,1,0:T(8,128)(2,1)S(1)}, u32[]{:S(2)}, u32[]{:S(2)}) %collective-permute-start.26) | collective-permute-done | bytes 524320 | tf_op jit(solution)/shard_map/ppermute | solution.py:734
  278.8 33.4 %forward_far_rows.4 = (bf16[4,128,128,128]{3,2,1,0:T(8,128)(2,1)}, bf16[4,128,128,128]{3,2,1,0:T(8,128)(2,1)}, bf16[4,128,4096]{2,1,0:T(8,128)(2,1)}, bf16[4,128,256]{2,1,0:T(8,128)(2,1)}, f32[8,128]{1,0:T(8,128)}) custom-call(s32[8]{0:T(128)} %stack.323.refs_0_, ...), custom_call_target="tpu_custom_call", output_to_operand_aliasing={{0}: (9, {}), {1}: (10, {}), {2}: (11, {}), {3}: (12, {})} | custom-call | tf_op jit(solution)/shard_map/forward_far_rows/pallas_call | solution.py:480
  321.8 32.9 %forward_far_rows.5 = (bf16[4,128,128,128]{3,2,1,0:T(8,128)(2,1)}, bf16[4,128,128,128]{3,2,1,0:T(8,128)(2,1)}, bf16[4,128,4096]{2,1,0:T(8,128)(2,1)}, bf16[4,128,256]{2,1,0:T(8,128)(2,1)}, f32[8,128]{1,0:T(8,128)}) custom-call(s32[8]{0:T(128)} %stack.326.refs_0_, ...), custom_call_target="tpu_custom_call", output_to_operand_aliasing={{0}: (12, {}), {1}: (13, {}), {2}: (14, {}), {3}: (15, {})} | custom-call | tf_op jit(solution)/shard_map/forward_far_rows/pallas_call | solution.py:480
  363.4 19.2 %backward_far_rows.2 = (bf16[4,128,128,128]{3,2,1,0:T(8,128)(2,1)}, bf16[4,128,4096]{2,1,0:T(8,128)(2,1)}, bf16[4,128,256]{2,1,0:T(8,128)(2,1)}, f32[8,128]{1,0:T(8,128)}) custom-call(s32[8]{0:T(128)} %stack.327.refs_0_, s32[128]{0:T(128)} %bitcast.116, ...), custom_call_target="tpu_custom_call", output_to_operand_aliasing={{0}: (13, {}), {1}: (14, {}), {2}: (15, {})} | custom-call | tf_op jit(solution)/shard_map/backward_far_rows/pallas_call | solution.py:556
  383.6 19.2 %backward_far_rows.3 = (bf16[4,128,128,128]{3,2,1,0:T(8,128)(2,1)}, bf16[4,128,4096]{2,1,0:T(8,128)(2,1)}, bf16[4,128,256]{2,1,0:T(8,128)(2,1)}, f32[8,128]{1,0:T(8,128)}) custom-call(s32[8]{0:T(128)} %stack.261.refs_0_, s32[128]{0:T(128)} %bitcast.117, ...), custom_call_target="tpu_custom_call", output_to_operand_aliasing={{0}: (13, {}), {1}: (14, {}), {2}: (15, {})} | custom-call | tf_op jit(solution)/shard_map/backward_far_rows/pallas_call | solution.py:556
  402.7 15.8 %down_gradients.1 = (bf16[64,128,128]{2,1,0:T(8,128)(2,1)}, bf16[64,128,128]{2,1,0:T(8,128)(2,1)}, bf16[16,10240]{1,0:T(8,128)(2,1)}, bf16[16,10240]{1,0:T(8,128)(2,1)}) custom-call(s32[8]{0:T(128)} %stack.258.refs_0_, s32[128]{0:T(128)} %bitcast.118, bf16[4,128,128,128]{3,2,1,0:T(8,128)(2,1)} %get-tuple-element.269.refs_2_, ...), custom_call_target="tpu_custom_call" | custom-call | tf_op jit(solution)/shard_map/down_gradients/pallas_call | solution.py:673
  422.3 15.8 %up_gradients.1 = (bf16[64,128,128]{2,1,0:T(8,128)(2,1)}, bf16[64,128,128]{2,1,0:T(8,128)(2,1)}, bf16[16,12288]{1,0:T(8,128)(2,1)}, bf16[16,12288]{1,0:T(8,128)(2,1)}) custom-call(s32[8]{0:T(128)} %stack.258.refs_0_, s32[128]{0:T(128)} %select_reduce_fusion.refs_2_.refs_1_, bf16[4,128,128,128]{3,2,1,0:T(8,128)(2,1)} %get-tuple-element.260.refs_2_, ...), custom_call_target="tpu_custom_call" | custom-call | tf_op jit(solution)/shard_map/up_gradients/pallas_call | solution.py:673
  (199 shorter events, 118.0 us)
Async XLA Ops:
  14.6 32.8 %collective-permute-start.5 = (bf16[32,4096]{1,0:T(8,128)(2,1)}, bf16[32,4096]{1,0:T(8,128)(2,1)S(1)}, u32[]{:S(2)}, u32[]{:S(2)}) collective-permute-start(bf16[32,4096]{1,0:T(8,128)(2,1)} %get-tuple-element.149), channel_id=1, source_target_pairs={{0,8},{8,16},{1,9},{9,17},{2,10},{10,18},{3,11},{11,19},{4,12},{12... | collective-permute-start | bytes 786440 | tf_op jit(solution)/shard_map/ppermute | solution.py:783
  17.1 65.0 %collective-permute-start.3 = (bf16[4,32,4096]{2,1,0:T(8,128)(2,1)}, bf16[4,32,4096]{2,1,0:T(8,128)(2,1)S(1)}, u32[]{:S(2)}, u32[]{:S(2)}) collective-permute-start(bf16[4,32,4096]{2,1,0:T(8,128)(2,1)} %broadcast_select_fusion), channel_id=1, source_target_pairs={{0,1},{1,2},{2,3},{3,0},{24,25},{25,26},{26,27},{27,24},{4,5},{5,6... | collective-permute-start | bytes 3145736 | tf_op jit(solution)/shard_map/ppermute | solution.py:734
  18.4 69.3 %collective-permute-start.10 = (bf16[4,32,4096]{2,1,0:T(8,128)(2,1)}, bf16[4,32,4096]{2,1,0:T(8,128)(2,1)S(1)}, u32[]{:S(2)}, u32[]{:S(2)}) collective-permute-start(bf16[4,32,4096]{2,1,0:T(8,128)(2,1)} %broadcast_select_fusion), channel_id=1, source_target_pairs={{0,3},{1,0},{2,1},{3,2},{24,27},{25,24},{26,25},{27,26},{4,7},{5,4... | collective-permute-start | bytes 3145736 | tf_op jit(solution)/shard_map/ppermute | solution.py:734
  57.6 41.2 %collective-permute-start.8 = (bf16[4,32,4096]{2,1,0:T(8,128)(2,1)}, bf16[4,32,4096]{2,1,0:T(8,128)(2,1)}, u32[]{:S(2)}, u32[]{:S(2)}) collective-permute-start(bf16[4,32,4096]{2,1,0:T(8,128)(2,1)} %broadcast_select_fusion), channel_id=1, source_target_pairs={{0,2},{1,3},{2,0},{3,1},{24,26},{25,27},{26,24},{27,25},{4,6},{5,7... | collective-permute-start | bytes 3145736 | tf_op jit(solution)/shard_map/ppermute | solution.py:734
  111.2 35.3 %collective-permute-start.12 = (bf16[2,32,4096]{2,1,0:T(8,128)(2,1)S(1)}, bf16[2,32,4096]{2,1,0:T(8,128)(2,1)S(1)}, u32[]{:S(2)}, u32[]{:S(2)}) collective-permute-start(bf16[2,32,4096]{2,1,0:T(8,128)(2,1)S(1)} %slice.44), channel_id=1, source_target_pairs={{8,9},{9,10},{10,11},{11,8},{16,17},{17,18},{18,19},{19,16},{24,25... | collective-permute-start | bytes 1572872 | tf_op jit(solution)/shard_map/ppermute | solution.py:734
  128.0 18.4 %collective-permute-start.11 = (bf16[32,4096]{1,0:T(8,128)(2,1)}, bf16[32,4096]{1,0:T(8,128)(2,1)S(1)}, u32[]{:S(2)}, u32[]{:S(2)}) collective-permute-start(bf16[32,4096]{1,0:T(8,128)(2,1)} %get-tuple-element.182), channel_id=1, source_target_pairs={{24,16},{16,8},{25,17},{17,9},{26,18},{18,10},{27,19},{19,11},{28,... | collective-permute-start | bytes 786440 | tf_op jit(solution)/shard_map/ppermute | solution.py:793
  142.6 29.1 %collective-permute-start.17 = (bf16[2,32,4096]{2,1,0:T(8,128)(2,1)S(1)}, bf16[2,32,4096]{2,1,0:T(8,128)(2,1)S(1)}, u32[]{:S(2)}, u32[]{:S(2)}) collective-permute-start(bf16[2,32,4096]{2,1,0:T(8,128)(2,1)S(1)} %slice.45), channel_id=1, source_target_pairs={{8,11},{9,8},{10,9},{11,10},{16,19},{17,16},{18,17},{19,18},{24,27... | collective-permute-start | bytes 1572872 | tf_op jit(solution)/shard_map/ppermute | solution.py:734
  158.9 27.5 %collective-permute-start.16 = (bf16[2,32,4096]{2,1,0:T(8,128)(2,1)S(1)}, bf16[2,32,4096]{2,1,0:T(8,128)(2,1)S(1)}, u32[]{:S(2)}, u32[]{:S(2)}) collective-permute-start(bf16[2,32,4096]{2,1,0:T(8,128)(2,1)S(1)} %slice.45), channel_id=1, source_target_pairs={{8,10},{9,11},{10,8},{11,9},{16,18},{17,19},{18,16},{19,17},{24,26... | collective-permute-start | bytes 1572872 | tf_op jit(solution)/shard_map/ppermute | solution.py:734
  169.8 21.9 %collective-permute-start.14 = (bf16[32,4096]{1,0:T(8,128)(2,1)}, bf16[32,4096]{1,0:T(8,128)(2,1)S(1)}, u32[]{:S(2)}, u32[]{:S(2)}) collective-permute-start(bf16[32,4096]{1,0:T(8,128)(2,1)} %get-tuple-element.196), channel_id=1, source_target_pairs={{24,16},{16,8},{8,0},{25,17},{17,9},{9,1},{26,18},{18,10},{10,2},{... | collective-permute-start | bytes 786440 | tf_op jit(solution)/shard_map/ppermute | solution.py:793
  188.2 33.9 %collective-permute-start.19 = (bf16[2,32,4096]{2,1,0:T(8,128)(2,1)S(1)}, bf16[2,32,4096]{2,1,0:T(8,128)(2,1)S(1)}, u32[]{:S(2)}, u32[]{:S(2)}) collective-permute-start(bf16[2,32,4096]{2,1,0:T(8,128)(2,1)S(1)} %slice.46), channel_id=1, source_target_pairs={{8,9},{9,10},{10,11},{11,8},{16,17},{17,18},{18,19},{19,16},{24,25... | collective-permute-start | bytes 1572872 | tf_op jit(solution)/shard_map/ppermute | solution.py:734
  205.9 48.7 %collective-permute-start.22 = (bf16[2,32,4096]{2,1,0:T(8,128)(2,1)S(1)}, bf16[2,32,4096]{2,1,0:T(8,128)(2,1)S(1)}, u32[]{:S(2)}, u32[]{:S(2)}) collective-permute-start(bf16[2,32,4096]{2,1,0:T(8,128)(2,1)S(1)} %slice.46), channel_id=1, source_target_pairs={{8,10},{9,11},{10,8},{11,9},{16,18},{17,19},{18,16},{19,17},{24,26... | collective-permute-start | bytes 1572872 | tf_op jit(solution)/shard_map/ppermute | solution.py:734
  211.8 42.8 %collective-permute-start.21 = (bf16[2,32,4096]{2,1,0:T(8,128)(2,1)S(1)}, bf16[2,32,4096]{2,1,0:T(8,128)(2,1)S(1)}, u32[]{:S(2)}, u32[]{:S(2)}) collective-permute-start(bf16[2,32,4096]{2,1,0:T(8,128)(2,1)S(1)} %slice.46), channel_id=1, source_target_pairs={{8,11},{9,8},{10,9},{11,10},{16,19},{17,16},{18,17},{19,18},{24,27... | collective-permute-start | bytes 1572872 | tf_op jit(solution)/shard_map/ppermute | solution.py:734
  234.4 20.3 %collective-permute-start.20 = (bf16[32,4096]{1,0:T(8,128)(2,1)}, bf16[32,4096]{1,0:T(8,128)(2,1)S(1)}, u32[]{:S(2)}, u32[]{:S(2)}) collective-permute-start(bf16[32,4096]{1,0:T(8,128)(2,1)} %get-tuple-element.223), channel_id=1, source_target_pairs={{16,8},{8,0},{17,9},{9,1},{18,10},{10,2},{19,11},{11,3},{20,12},{1... | collective-permute-start | bytes 786440 | tf_op jit(solution)/shard_map/ppermute | solution.py:793
  237.4 41.2 %collective-permute-start.26 = (bf16[2,32,4096]{2,1,0:T(8,128)(2,1)S(1)}, bf16[2,32,4096]{2,1,0:T(8,128)(2,1)S(1)}, u32[]{:S(2)}, u32[]{:S(2)}) collective-permute-start(bf16[2,32,4096]{2,1,0:T(8,128)(2,1)S(1)} %slice.48), channel_id=1, source_target_pairs={{0,3},{1,0},{2,1},{3,2},{8,11},{9,8},{10,9},{11,10},{16,19},{17,16... | collective-permute-start | bytes 1572872 | tf_op jit(solution)/shard_map/ppermute | solution.py:734
  241.6 37.2 %collective-permute-start.25 = (bf16[2,32,4096]{2,1,0:T(8,128)(2,1)S(1)}, bf16[2,32,4096]{2,1,0:T(8,128)(2,1)S(1)}, u32[]{:S(2)}, u32[]{:S(2)}) collective-permute-start(bf16[2,32,4096]{2,1,0:T(8,128)(2,1)S(1)} %slice.48), channel_id=1, source_target_pairs={{0,1},{1,2},{2,3},{3,0},{8,9},{9,10},{10,11},{11,8},{16,17},{17,18... | collective-permute-start | bytes 1572872 | tf_op jit(solution)/shard_map/ppermute | solution.py:734
  257.4 54.9 %collective-permute-start.24 = (bf16[2,32,4096]{2,1,0:T(8,128)(2,1)S(1)}, bf16[2,32,4096]{2,1,0:T(8,128)(2,1)S(1)}, u32[]{:S(2)}, u32[]{:S(2)}) collective-permute-start(bf16[2,32,4096]{2,1,0:T(8,128)(2,1)S(1)} %slice.47), channel_id=1, source_target_pairs={{0,2},{1,3},{2,0},{3,1},{8,10},{9,11},{10,8},{11,9},{16,18},{17,19... | collective-permute-start | bytes 1572872 | tf_op jit(solution)/shard_map/ppermute | solution.py:734
  262.9 49.4 %collective-permute-start.23 = (bf16[32,4096]{1,0:T(8,128)(2,1)}, bf16[32,4096]{1,0:T(8,128)(2,1)S(1)}, u32[]{:S(2)}, u32[]{:S(2)}) collective-permute-start(bf16[32,4096]{1,0:T(8,128)(2,1)} %get-tuple-element.230), channel_id=1, source_target_pairs={{8,0},{9,1},{10,2},{11,3},{12,4},{13,5},{14,6},{15,7}} | collective-permute-start | bytes 786440 | tf_op jit(solution)/shard_map/ppermute | solution.py:793
  314.9 44.5 %collective-permute-start.28 = (bf16[2,32,4096]{2,1,0:T(8,128)(2,1)S(1)}, bf16[2,32,4096]{2,1,0:T(8,128)(2,1)S(1)}, u32[]{:S(2)}, u32[]{:S(2)}) collective-permute-start(bf16[2,32,4096]{2,1,0:T(8,128)(2,1)S(1)} %slice.49), channel_id=1, source_target_pairs={{0,3},{1,0},{2,1},{3,2},{8,11},{9,8},{10,9},{11,10},{16,19},{17,16... | collective-permute-start | bytes 1572872 | tf_op jit(solution)/shard_map/ppermute | solution.py:734
  317.5 65.0 %collective-permute-start.27 = (bf16[2,32,4096]{2,1,0:T(8,128)(2,1)S(1)}, bf16[2,32,4096]{2,1,0:T(8,128)(2,1)S(1)}, u32[]{:S(2)}, u32[]{:S(2)}) collective-permute-start(bf16[2,32,4096]{2,1,0:T(8,128)(2,1)S(1)} %slice.49), channel_id=1, source_target_pairs={{0,1},{1,2},{2,3},{3,0},{8,9},{9,10},{10,11},{11,8},{16,17},{17,18... | collective-permute-start | bytes 1572872 | tf_op jit(solution)/shard_map/ppermute | solution.py:734
  354.7 27.9 %collective-permute-start.29 = (bf16[2,32,4096]{2,1,0:T(8,128)(2,1)S(1)}, bf16[2,32,4096]{2,1,0:T(8,128)(2,1)S(1)}, u32[]{:S(2)}, u32[]{:S(2)}) collective-permute-start(bf16[2,32,4096]{2,1,0:T(8,128)(2,1)S(1)} %slice.49), channel_id=1, source_target_pairs={{0,2},{1,3},{2,0},{3,1},{8,10},{9,11},{10,8},{11,9},{16,18},{17,19... | collective-permute-start | bytes 1572872 | tf_op jit(solution)/shard_map/ppermute | solution.py:734
  357.9 63.7 %collective-permute-start.32 = (f32[1,4096]{1,0:T(1,128)S(1)}, f32[1,4096]{1,0:T(1,128)S(1)}, u32[]{:S(2)}, u32[]{:S(2)}) collective-permute-start(f32[1,4096]{1,0:T(1,128)S(1)} %bitcast.119), channel_id=1, source_target_pairs={{0,3},{1,0},{2,1},{3,2},{8,11},{9,8},{10,9},{11,10},{16,19},{17,16... | collective-permute-start | bytes 49160 | tf_op jit(solution)/shard_map/ppermute | solution.py:734
  359.4 62.2 %collective-permute-start.31 = (f32[1,4096]{1,0:T(1,128)S(1)}, f32[1,4096]{1,0:T(1,128)S(1)}, u32[]{:S(2)}, u32[]{:S(2)}) collective-permute-start(f32[1,4096]{1,0:T(1,128)S(1)} %bitcast.120), channel_id=1, source_target_pairs={{0,2},{1,3},{2,0},{3,1},{8,10},{9,11},{10,8},{11,9},{16,18},{17,19... | collective-permute-start | bytes 49160 | tf_op jit(solution)/shard_map/ppermute | solution.py:734
  359.4 62.2 %collective-permute-start.30 = (f32[1,4096]{1,0:T(1,128)S(1)}, f32[1,4096]{1,0:T(1,128)S(1)}, u32[]{:S(2)}, u32[]{:S(2)}) collective-permute-start(f32[1,4096]{1,0:T(1,128)S(1)} %bitcast.121), channel_id=1, source_target_pairs={{0,1},{1,2},{2,3},{3,0},{8,9},{9,10},{10,11},{11,8},{16,17},{17,18... | collective-permute-start | bytes 49160 | tf_op jit(solution)/shard_map/ppermute | solution.py:734
  418.5 20.2 %collective-permute-start.36 = (bf16[16,10240]{1,0:T(8,128)(2,1)}, bf16[16,10240]{1,0:T(8,128)(2,1)S(1)}, u32[]{:S(2)}, u32[]{:S(2)}) collective-permute-start(bf16[16,10240]{1,0:T(8,128)(2,1)} %get-tuple-element.274), channel_id=1, source_target_pairs={{0,4},{4,0},{1,5},{5,1},{2,6},{6,2},{3,7},{7,3},{8,12},{12,8},{9,1... | collective-permute-start | bytes 983048 | tf_op jit(solution)/shard_map/ppermute | solution.py:864
  (52 other events, 406.7 us)

commit v6 on v5

--- a/solution.py
+++ b/solution.py
@@ -832,7 +832,7 @@
             g_early = enqueue(lambda: bbufs[1][early, 0:rows], outer)
         if t == slots - 1:
             g_late = enqueue(lambda: bbufs[1][late, 0:rows], outer)
-        hold = 2 if t == slots - 1 else 1
+        hold = 2 if t >= slots - 2 else 1
         send_one(hold)
         if t != slots - 2:
             send_one(hold)
@@ -859,15 +859,17 @@
     hidb, slpb, nrmb, _, lowf = fbufs
     sc = scalars(zero, sec == 0)
 
-    def over_fsdp(pieces):
+    def over_fsdp(pieces, ahead=()):
         if parts == 2:
             got = lax.ppermute(pieces[1], "fsdp", swap)
+            got = lax.optimization_barrier((got, *ahead))[0]
             return (pieces[0].astype(F32) + got.astype(F32))[None]
         return lax.psum_scatter(pieces[0], "fsdp", scatter_dimension=0, tiled=False).astype(F32)[None]
 
     dn_g, dn_small = weight_grads(dims, False, sc, dno, hidb, gb, lowb, lowf)
     up_g, up_small = weight_grads(dims, True, sc, grouped, gpb, nrmb, lowf, lowb, gain)
-    dn, dns, up, ups = (over_fsdp(p) for p in (dn_g, dn_small, up_g, up_small))
+    dn, dns = over_fsdp(dn_g), over_fsdp(dn_small)
+    up, ups = over_fsdp(up_g, (dn,)), over_fsdp(up_small)
     mw, hw = dims.mh * BLK, dims.hh * BLK
     return (
         ups[:, 0, mw + hw :],

time: 453 us -> 453 us (level)
  no operation moved by 1% of the time
where the time goes in v6:
time: 453 us; the launch traced here: 451 us
  Pallas kernels  226 us (50%)
  starting transfers between devices  88.2 us (19%)
  waiting for transfers between devices  86.9 us (19%)
  local copies, waits for them, and re-layouts  38.6 us (9%)
  other arithmetic  10.2 us (2%)
    pallas_call x3, Pallas kernels, fwd_far(): pl.pallas_call(kernel, out_shape=tuple((jax.ShapeDtypeStruct(b.shape, b.d...  67.2 us
    ppermute x18, starting transfers between devices, shifted(): return lax.ppermute(block, ('section', 'dp'), pairs)  50.6 us
    pallas_call x7, Pallas kernels, bwd_slot(): pl.pallas_call(kernel, out_shape=(jax.ShapeDtypeStruct((rows, dims.width)...  48.9 us
    pallas_call x7, Pallas kernels, fwd_slot(): pl.pallas_call(kernel, out_shape=(jax.ShapeDtypeStruct((rows, dims.width)...  40.1 us
    ppermute x18, waiting for transfers between devices, shifted(): return lax.ppermute(block, ('section', 'dp'), pairs)  38.8 us
    pallas_call x2, Pallas kernels, bwd_far(): pl.pallas_call(kernel, out_shape=tuple((jax.ShapeDtypeStruct(b.shape, b.d...  38.4 us
    ppermute x6, waiting for transfers between devices, forward(): frecv = lax.ppermute(y, 'section', pairs)  37.2 us
    pallas_call x2, Pallas kernels, weight_grads(): pl.pallas_call(kernel, out_shape=tuple(shapes), in_specs=[SMEM] * 2 + [AN...  31.6 us
  transfers between devices with their start and end apart: 37, of which 12 were waited for; matrix products, arithmetic and copies ran while one was open for 8% of the time, Pallas kernels for 47%

profile of v6, /device:TPU:13, one launch (start us, length us, event | category | flops | bytes accessed | tf_op | source)
XLA Modules:
  0.0 451.5 jit_solution(2418548450888069074)
XLA Ops:
  19.1 28.3 %collective-permute-done.5.refs_4_ = bf16[32,4096]{1,0:T(8,128)(2,1)S(1)} collective-permute-done((bf16[32,4096]{1,0:T(8,128)(2,1)}, bf16[32,4096]{1,0:T(8,128)(2,1)S(1)}, u32[]{:S(2)}, u32[]{:S(2)}) %collective-permute-start.5) | collective-permute-done | bytes 262176 | tf_op jit(solution)/shard_map/ppermute | solution.py:783
  48.2 9.5 %forward_rows.9 = (bf16[32,4096]{1,0:T(8,128)(2,1)}, bf16[4,128,128,128]{3,2,1,0:T(8,128)(2,1)}, bf16[4,128,128,128]{3,2,1,0:T(8,128)(2,1)}, bf16[4,128,4096]{2,...) custom-call(s32[8]{0:T(128)} %stack.303.refs_0_, ...), custom_call_target="tpu_custom_call", output_to_operand_aliasing={{1}: (11, {}), {2}: (12, {}), {3}: (13, {}), {4}: (14, {}),... | custom-call | tf_op jit(solution)/shard_map/forward_rows/pallas_call | solution.py:302
  62.7 6.7 %collective-permute-done.6.refs_4_ = bf16[32,4096]{1,0:T(8,128)(2,1)S(1)} collective-permute-done((bf16[32,4096]{1,0:T(8,128)(2,1)}, bf16[32,4096]{1,0:T(8,128)(2,1)S(1)}, u32[]{:S(2)}, u32[]{:S(2)}) %collective-permute-start.6) | collective-permute-done | bytes 262176 | tf_op jit(solution)/shard_map/ppermute | solution.py:783
  70.2 9.3 %forward_rows.10 = (bf16[32,4096]{1,0:T(8,128)(2,1)}, bf16[4,128,128,128]{3,2,1,0:T(8,128)(2,1)}, bf16[4,128,128,128]{3,2,1,0:T(8,128)(2,1)}, bf16[4,128,4096]{2...) custom-call(s32[8]{0:T(128)} %stack.299.refs_0_, ...), custom_call_target="tpu_custom_call", output_to_operand_aliasing={{1}: (11, {}), {2}: (12, {}), {3}: (13, {}), {4}: (14, {}),... | custom-call | tf_op jit(solution)/shard_map/forward_rows/pallas_call | solution.py:302
  88.4 9.3 %forward_rows.11 = (bf16[32,4096]{1,0:T(8,128)(2,1)}, bf16[4,128,128,128]{3,2,1,0:T(8,128)(2,1)}, bf16[4,128,128,128]{3,2,1,0:T(8,128)(2,1)}, bf16[4,128,4096]{2...) custom-call(s32[8]{0:T(128)} %stack.311.refs_0_, ...), custom_call_target="tpu_custom_call", output_to_operand_aliasing={{1}: (11, {}), {2}: (12, {}), {3}: (13, {}), {4}: (14, {}),... | custom-call | tf_op jit(solution)/shard_map/forward_rows/pallas_call | solution.py:302
  99.5 11.7 %backward_rows.8 = (bf16[32,4096]{1,0:T(8,128)(2,1)}, bf16[4,128,128,128]{3,2,1,0:T(8,128)(2,1)}, bf16[4,128,4096]{2,1,0:T(8,128)(2,1)}, bf16[4,128,256]{2,1,0:T(8,128)(2,1)}, f32[4,8,4096]{2,1,0:T(8,128)}) custom-call(s32[8]{0:T(128)} %stack.287.refs_0_, s32[128]{0:T(128)} %bitcast.108, ...), custom_call_target="tpu_custom_call", output_to_operand_aliasing={{1}: (13, {}), {2}: (14, {}), {3}: (15, {}), {4}: (16, {})} | custom-call | tf_op jit(solution)/shard_map/backward_rows/pallas_call | solution.py:397
  114.5 13.6 %collective-permute-start.13 = (bf16[32,4096]{1,0:T(8,128)(2,1)S(1)}, bf16[32,4096]{1,0:T(8,128)(2,1)S(1)}, u32[]{:S(2)}, u32[]{:S(2)}) collective-permute-start(bf16[32,4096]{1,0:T(8,128)(2,1)S(1)} %copy-done.38), channel_id=1, source_target_pairs={{8,16},{16,24},{9,17},{17,25},{10,18},{18,26},{11,19},{19,27},{12,... | collective-permute-start | bytes 786440 | tf_op jit(solution)/shard_map/ppermute | solution.py:783
  132.0 9.5 %forward_rows.12 = (bf16[32,4096]{1,0:T(8,128)(2,1)}, bf16[4,128,128,128]{3,2,1,0:T(8,128)(2,1)}, bf16[4,128,128,128]{3,2,1,0:T(8,128)(2,1)}, bf16[4,128,4096]{2...) custom-call(s32[8]{0:T(128)} %stack.315.refs_0_, ...), custom_call_target="tpu_custom_call", output_to_operand_aliasing={{1}: (11, {}), {2}: (12, {}), {3}: (13, {}), {4}: (14, {}),... | custom-call | tf_op jit(solution)/shard_map/forward_rows/pallas_call | solution.py:302
  147.2 11.7 %backward_rows.9 = (bf16[32,4096]{1,0:T(8,128)(2,1)}, bf16[4,128,128,128]{3,2,1,0:T(8,128)(2,1)}, bf16[4,128,4096]{2,1,0:T(8,128)(2,1)}, bf16[4,128,256]{2,1,0:T(8,128)(2,1)}, f32[4,8,4096]{2,1,0:T(8,128)}) custom-call(s32[8]{0:T(128)} %stack.283.refs_0_, s32[128]{0:T(128)} %bitcast.110, ...), custom_call_target="tpu_custom_call", output_to_operand_aliasing={{1}: (13, {}), {2}: (14, {}), {3}: (15, {}), {4}: (16, {})} | custom-call | tf_op jit(solution)/shard_map/backward_rows/pallas_call | solution.py:397
  158.9 5.5 %collective-permute-start.16 = (bf16[2,32,4096]{2,1,0:T(8,128)(2,1)S(1)}, bf16[2,32,4096]{2,1,0:T(8,128)(2,1)S(1)}, u32[]{:S(2)}, u32[]{:S(2)}) collective-permute-start(bf16[2,32,4096]{2,1,0:T(8,128)(2,1)S(1)} %slice.45), channel_id=1, source_target_pairs={{8,10},{9,11},{10,8},{11,9},{16,18},{17,19},{18,16},{19,17},{24,26... | collective-permute-start | bytes 1572872 | tf_op jit(solution)/shard_map/ppermute | solution.py:734
  172.7 13.6 %collective-permute-done.16.refs_7_ = bf16[2,32,4096]{2,1,0:T(8,128)(2,1)S(1)} collective-permute-done((bf16[2,32,4096]{2,1,0:T(8,128)(2,1)S(1)}, bf16[2,32,4096]{2,1,0:T(8,128)(2,1)S(1)}, u32[]{:S(2)}, u32[]{:S(2)}) %collective-permute-start.16) | collective-permute-done | bytes 524320 | tf_op jit(solution)/shard_map/ppermute | solution.py:734
  192.4 11.5 %backward_rows.10 = (bf16[32,4096]{1,0:T(8,128)(2,1)}, bf16[4,128,128,128]{3,2,1,0:T(8,128)(2,1)}, bf16[4,128,4096]{2,1,0:T(8,128)(2,1)}, bf16[4,128,256]{2,1,0:T(8,128)(2,1)}, f32[4,8,4096]{2,1,0:T(8,128)}) custom-call(s32[8]{0:T(128)} %stack.279.refs_0_, ...), custom_call_target="tpu_custom_call", output_to_operand_aliasing={{1}: (13, {}), {2}: (14, {}), {3}: (15, {}), {4}: (16, {})} | custom-call | tf_op jit(solution)/shard_map/backward_rows/pallas_call | solution.py:397
  205.9 5.9 %collective-permute-start.22 = (bf16[2,32,4096]{2,1,0:T(8,128)(2,1)S(1)}, bf16[2,32,4096]{2,1,0:T(8,128)(2,1)S(1)}, u32[]{:S(2)}, u32[]{:S(2)}) collective-permute-start(bf16[2,32,4096]{2,1,0:T(8,128)(2,1)S(1)} %slice.46), channel_id=1, source_target_pairs={{8,10},{9,11},{10,8},{11,9},{16,18},{17,19},{18,16},{19,17},{24,26... | collective-permute-start | bytes 1572872 | tf_op jit(solution)/shard_map/ppermute | solution.py:734
  214.4 7.7 %collective-permute-done.18.refs_4_ = bf16[32,4096]{1,0:T(8,128)(2,1)S(1)} collective-permute-done((bf16[32,4096]{1,0:T(8,128)(2,1)}, bf16[32,4096]{1,0:T(8,128)(2,1)S(1)}, u32[]{:S(2)}, u32[]{:S(2)}) %collective-permute-start.18) | collective-permute-done | bytes 262176 | tf_op jit(solution)/shard_map/ppermute | solution.py:793
  222.8 11.6 %backward_rows.11 = (bf16[32,4096]{1,0:T(8,128)(2,1)}, bf16[4,128,128,128]{3,2,1,0:T(8,128)(2,1)}, bf16[4,128,4096]{2,1,0:T(8,128)(2,1)}, bf16[4,128,256]{2,1,0:T(8,128)(2,1)}, f32[4,8,4096]{2,1,0:T(8,128)}) custom-call(s32[8]{0:T(128)} %stack.275.refs_0_, ...), custom_call_target="tpu_custom_call", output_to_operand_aliasing={{1}: (13, {}), {2}: (14, {}), {3}: (15, {}), {4}: (16, {})} | custom-call | tf_op jit(solution)/shard_map/backward_rows/pallas_call | solution.py:397
  243.6 11.7 %collective-permute-done.22.refs_7_ = bf16[2,32,4096]{2,1,0:T(8,128)(2,1)S(1)} collective-permute-done((bf16[2,32,4096]{2,1,0:T(8,128)(2,1)S(1)}, bf16[2,32,4096]{2,1,0:T(8,128)(2,1)S(1)}, u32[]{:S(2)}, u32[]{:S(2)}) %collective-permute-start.22) | collective-permute-done | bytes 524320 | tf_op jit(solution)/shard_map/ppermute | solution.py:734
  258.0 5.5 %collective-permute-start.28 = (bf16[2,32,4096]{2,1,0:T(8,128)(2,1)S(1)}, bf16[2,32,4096]{2,1,0:T(8,128)(2,1)S(1)}, u32[]{:S(2)}, u32[]{:S(2)}) collective-permute-start(bf16[2,32,4096]{2,1,0:T(8,128)(2,1)S(1)} %slice.49), channel_id=1, source_target_pairs={{0,2},{1,3},{2,0},{3,1},{8,10},{9,11},{10,8},{11,9},{16,18},{17,19... | collective-permute-start | bytes 1572872 | tf_op jit(solution)/shard_map/ppermute | solution.py:734
  265.5 13.1 %collective-permute-done.25.refs_8_ = bf16[2,32,4096]{2,1,0:T(8,128)(2,1)S(1)} collective-permute-done((bf16[2,32,4096]{2,1,0:T(8,128)(2,1)S(1)}, bf16[2,32,4096]{2,1,0:T(8,128)(2,1)S(1)}, u32[]{:S(2)}, u32[]{:S(2)}) %collective-permute-start.25) | collective-permute-done | bytes 524320 | tf_op jit(solution)/shard_map/ppermute | solution.py:734
  279.0 33.4 %forward_far_rows.4 = (bf16[4,128,128,128]{3,2,1,0:T(8,128)(2,1)}, bf16[4,128,128,128]{3,2,1,0:T(8,128)(2,1)}, bf16[4,128,4096]{2,1,0:T(8,128)(2,1)}, bf16[4,128,256]{2,1,0:T(8,128)(2,1)}, f32[8,128]{1,0:T(8,128)}) custom-call(s32[8]{0:T(128)} %stack.323.refs_0_, ...), custom_call_target="tpu_custom_call", output_to_operand_aliasing={{0}: (9, {}), {1}: (10, {}), {2}: (11, {}), {3}: (12, {})} | custom-call | tf_op jit(solution)/shard_map/forward_far_rows/pallas_call | solution.py:480
  321.8 32.9 %forward_far_rows.5 = (bf16[4,128,128,128]{3,2,1,0:T(8,128)(2,1)}, bf16[4,128,128,128]{3,2,1,0:T(8,128)(2,1)}, bf16[4,128,4096]{2,1,0:T(8,128)(2,1)}, bf16[4,128,256]{2,1,0:T(8,128)(2,1)}, f32[8,128]{1,0:T(8,128)}) custom-call(s32[8]{0:T(128)} %stack.326.refs_0_, ...), custom_call_target="tpu_custom_call", output_to_operand_aliasing={{0}: (12, {}), {1}: (13, {}), {2}: (14, {}), {3}: (15, {})} | custom-call | tf_op jit(solution)/shard_map/forward_far_rows/pallas_call | solution.py:480
  363.3 19.2 %backward_far_rows.2 = (bf16[4,128,128,128]{3,2,1,0:T(8,128)(2,1)}, bf16[4,128,4096]{2,1,0:T(8,128)(2,1)}, bf16[4,128,256]{2,1,0:T(8,128)(2,1)}, f32[8,128]{1,0:T(8,128)}) custom-call(s32[8]{0:T(128)} %stack.327.refs_0_, s32[128]{0:T(128)} %bitcast.116, ...), custom_call_target="tpu_custom_call", output_to_operand_aliasing={{0}: (13, {}), {1}: (14, {}), {2}: (15, {})} | custom-call | tf_op jit(solution)/shard_map/backward_far_rows/pallas_call | solution.py:556
  383.5 19.2 %backward_far_rows.3 = (bf16[4,128,128,128]{3,2,1,0:T(8,128)(2,1)}, bf16[4,128,4096]{2,1,0:T(8,128)(2,1)}, bf16[4,128,256]{2,1,0:T(8,128)(2,1)}, f32[8,128]{1,0:T(8,128)}) custom-call(s32[8]{0:T(128)} %stack.261.refs_0_, s32[128]{0:T(128)} %bitcast.117, ...), custom_call_target="tpu_custom_call", output_to_operand_aliasing={{0}: (13, {}), {1}: (14, {}), {2}: (15, {})} | custom-call | tf_op jit(solution)/shard_map/backward_far_rows/pallas_call | solution.py:556
  402.7 15.8 %down_gradients.1 = (bf16[64,128,128]{2,1,0:T(8,128)(2,1)}, bf16[64,128,128]{2,1,0:T(8,128)(2,1)}, bf16[16,10240]{1,0:T(8,128)(2,1)}, bf16[16,10240]{1,0:T(8,128)(2,1)}) custom-call(s32[8]{0:T(128)} %stack.258.refs_0_, s32[128]{0:T(128)} %bitcast.118, bf16[4,128,128,128]{3,2,1,0:T(8,128)(2,1)} %get-tuple-element.268.refs_2_, ...), custom_call_target="tpu_custom_call" | custom-call | tf_op jit(solution)/shard_map/down_gradients/pallas_call | solution.py:673
  422.2 15.8 %up_gradients.1 = (bf16[64,128,128]{2,1,0:T(8,128)(2,1)}, bf16[64,128,128]{2,1,0:T(8,128)(2,1)}, bf16[16,12288]{1,0:T(8,128)(2,1)}, bf16[16,12288]{1,0:T(8,128)(2,1)}) custom-call(s32[8]{0:T(128)} %stack.258.refs_0_, s32[128]{0:T(128)} %select_reduce_fusion.refs_2_.refs_1_, bf16[4,128,128,128]{3,2,1,0:T(8,128)(2,1)} %get-tuple-element.259.refs_2_, ...), custom_call_target="tpu_custom_call" | custom-call | tf_op jit(solution)/shard_map/up_gradients/pallas_call | solution.py:673
  (199 shorter events, 118.0 us)
Async XLA Ops:
  14.6 32.8 %collective-permute-start.5 = (bf16[32,4096]{1,0:T(8,128)(2,1)}, bf16[32,4096]{1,0:T(8,128)(2,1)S(1)}, u32[]{:S(2)}, u32[]{:S(2)}) collective-permute-start(bf16[32,4096]{1,0:T(8,128)(2,1)} %get-tuple-element.149), channel_id=1, source_target_pairs={{0,8},{8,16},{1,9},{9,17},{2,10},{10,18},{3,11},{11,19},{4,12},{12... | collective-permute-start | bytes 786440 | tf_op jit(solution)/shard_map/ppermute | solution.py:783
  17.1 65.0 %collective-permute-start.3 = (bf16[4,32,4096]{2,1,0:T(8,128)(2,1)}, bf16[4,32,4096]{2,1,0:T(8,128)(2,1)S(1)}, u32[]{:S(2)}, u32[]{:S(2)}) collective-permute-start(bf16[4,32,4096]{2,1,0:T(8,128)(2,1)} %broadcast_select_fusion), channel_id=1, source_target_pairs={{0,1},{1,2},{2,3},{3,0},{24,25},{25,26},{26,27},{27,24},{4,5},{5,6... | collective-permute-start | bytes 3145736 | tf_op jit(solution)/shard_map/ppermute | solution.py:734
  18.4 69.3 %collective-permute-start.10 = (bf16[4,32,4096]{2,1,0:T(8,128)(2,1)}, bf16[4,32,4096]{2,1,0:T(8,128)(2,1)S(1)}, u32[]{:S(2)}, u32[]{:S(2)}) collective-permute-start(bf16[4,32,4096]{2,1,0:T(8,128)(2,1)} %broadcast_select_fusion), channel_id=1, source_target_pairs={{0,3},{1,0},{2,1},{3,2},{24,27},{25,24},{26,25},{27,26},{4,7},{5,4... | collective-permute-start | bytes 3145736 | tf_op jit(solution)/shard_map/ppermute | solution.py:734
  57.6 41.2 %collective-permute-start.8 = (bf16[4,32,4096]{2,1,0:T(8,128)(2,1)}, bf16[4,32,4096]{2,1,0:T(8,128)(2,1)}, u32[]{:S(2)}, u32[]{:S(2)}) collective-permute-start(bf16[4,32,4096]{2,1,0:T(8,128)(2,1)} %broadcast_select_fusion), channel_id=1, source_target_pairs={{0,2},{1,3},{2,0},{3,1},{24,26},{25,27},{26,24},{27,25},{4,6},{5,7... | collective-permute-start | bytes 3145736 | tf_op jit(solution)/shard_map/ppermute | solution.py:734
  111.2 35.2 %collective-permute-start.12 = (bf16[2,32,4096]{2,1,0:T(8,128)(2,1)S(1)}, bf16[2,32,4096]{2,1,0:T(8,128)(2,1)S(1)}, u32[]{:S(2)}, u32[]{:S(2)}) collective-permute-start(bf16[2,32,4096]{2,1,0:T(8,128)(2,1)S(1)} %slice.44), channel_id=1, source_target_pairs={{8,9},{9,10},{10,11},{11,8},{16,17},{17,18},{18,19},{19,16},{24,25... | collective-permute-start | bytes 1572872 | tf_op jit(solution)/shard_map/ppermute | solution.py:734
  128.0 18.4 %collective-permute-start.11 = (bf16[32,4096]{1,0:T(8,128)(2,1)}, bf16[32,4096]{1,0:T(8,128)(2,1)S(1)}, u32[]{:S(2)}, u32[]{:S(2)}) collective-permute-start(bf16[32,4096]{1,0:T(8,128)(2,1)} %get-tuple-element.182), channel_id=1, source_target_pairs={{24,16},{16,8},{25,17},{17,9},{26,18},{18,10},{27,19},{19,11},{28,... | collective-permute-start | bytes 786440 | tf_op jit(solution)/shard_map/ppermute | solution.py:793
  142.6 29.1 %collective-permute-start.17 = (bf16[2,32,4096]{2,1,0:T(8,128)(2,1)S(1)}, bf16[2,32,4096]{2,1,0:T(8,128)(2,1)S(1)}, u32[]{:S(2)}, u32[]{:S(2)}) collective-permute-start(bf16[2,32,4096]{2,1,0:T(8,128)(2,1)S(1)} %slice.45), channel_id=1, source_target_pairs={{8,11},{9,8},{10,9},{11,10},{16,19},{17,16},{18,17},{19,18},{24,27... | collective-permute-start | bytes 1572872 | tf_op jit(solution)/shard_map/ppermute | solution.py:734
  158.9 27.4 %collective-permute-start.16 = (bf16[2,32,4096]{2,1,0:T(8,128)(2,1)S(1)}, bf16[2,32,4096]{2,1,0:T(8,128)(2,1)S(1)}, u32[]{:S(2)}, u32[]{:S(2)}) collective-permute-start(bf16[2,32,4096]{2,1,0:T(8,128)(2,1)S(1)} %slice.45), channel_id=1, source_target_pairs={{8,10},{9,11},{10,8},{11,9},{16,18},{17,19},{18,16},{19,17},{24,26... | collective-permute-start | bytes 1572872 | tf_op jit(solution)/shard_map/ppermute | solution.py:734
  169.8 21.9 %collective-permute-start.14 = (bf16[32,4096]{1,0:T(8,128)(2,1)}, bf16[32,4096]{1,0:T(8,128)(2,1)S(1)}, u32[]{:S(2)}, u32[]{:S(2)}) collective-permute-start(bf16[32,4096]{1,0:T(8,128)(2,1)} %get-tuple-element.196), channel_id=1, source_target_pairs={{24,16},{16,8},{8,0},{25,17},{17,9},{9,1},{26,18},{18,10},{10,2},{... | collective-permute-start | bytes 786440 | tf_op jit(solution)/shard_map/ppermute | solution.py:793
  188.2 33.9 %collective-permute-start.19 = (bf16[2,32,4096]{2,1,0:T(8,128)(2,1)S(1)}, bf16[2,32,4096]{2,1,0:T(8,128)(2,1)S(1)}, u32[]{:S(2)}, u32[]{:S(2)}) collective-permute-start(bf16[2,32,4096]{2,1,0:T(8,128)(2,1)S(1)} %slice.46), channel_id=1, source_target_pairs={{8,9},{9,10},{10,11},{11,8},{16,17},{17,18},{18,19},{19,16},{24,25... | collective-permute-start | bytes 1572872 | tf_op jit(solution)/shard_map/ppermute | solution.py:734
  205.9 49.3 %collective-permute-start.22 = (bf16[2,32,4096]{2,1,0:T(8,128)(2,1)S(1)}, bf16[2,32,4096]{2,1,0:T(8,128)(2,1)S(1)}, u32[]{:S(2)}, u32[]{:S(2)}) collective-permute-start(bf16[2,32,4096]{2,1,0:T(8,128)(2,1)S(1)} %slice.46), channel_id=1, source_target_pairs={{8,10},{9,11},{10,8},{11,9},{16,18},{17,19},{18,16},{19,17},{24,26... | collective-permute-start | bytes 1572872 | tf_op jit(solution)/shard_map/ppermute | solution.py:734
  211.8 43.4 %collective-permute-start.21 = (bf16[2,32,4096]{2,1,0:T(8,128)(2,1)S(1)}, bf16[2,32,4096]{2,1,0:T(8,128)(2,1)S(1)}, u32[]{:S(2)}, u32[]{:S(2)}) collective-permute-start(bf16[2,32,4096]{2,1,0:T(8,128)(2,1)S(1)} %slice.46), channel_id=1, source_target_pairs={{8,11},{9,8},{10,9},{11,10},{16,19},{17,16},{18,17},{19,18},{24,27... | collective-permute-start | bytes 1572872 | tf_op jit(solution)/shard_map/ppermute | solution.py:734
  234.4 20.8 %collective-permute-start.20 = (bf16[32,4096]{1,0:T(8,128)(2,1)}, bf16[32,4096]{1,0:T(8,128)(2,1)S(1)}, u32[]{:S(2)}, u32[]{:S(2)}) collective-permute-start(bf16[32,4096]{1,0:T(8,128)(2,1)} %get-tuple-element.223), channel_id=1, source_target_pairs={{16,8},{8,0},{17,9},{9,1},{18,10},{10,2},{19,11},{11,3},{20,12},{1... | collective-permute-start | bytes 786440 | tf_op jit(solution)/shard_map/ppermute | solution.py:793
  236.8 41.8 %collective-permute-start.25 = (bf16[2,32,4096]{2,1,0:T(8,128)(2,1)S(1)}, bf16[2,32,4096]{2,1,0:T(8,128)(2,1)S(1)}, u32[]{:S(2)}, u32[]{:S(2)}) collective-permute-start(bf16[2,32,4096]{2,1,0:T(8,128)(2,1)S(1)} %slice.47), channel_id=1, source_target_pairs={{0,3},{1,0},{2,1},{3,2},{8,11},{9,8},{10,9},{11,10},{16,19},{17,16... | collective-permute-start | bytes 1572872 | tf_op jit(solution)/shard_map/ppermute | solution.py:734
  241.0 38.0 %collective-permute-start.24 = (bf16[2,32,4096]{2,1,0:T(8,128)(2,1)S(1)}, bf16[2,32,4096]{2,1,0:T(8,128)(2,1)S(1)}, u32[]{:S(2)}, u32[]{:S(2)}) collective-permute-start(bf16[2,32,4096]{2,1,0:T(8,128)(2,1)S(1)} %slice.47), channel_id=1, source_target_pairs={{0,1},{1,2},{2,3},{3,0},{8,9},{9,10},{10,11},{11,8},{16,17},{17,18... | collective-permute-start | bytes 1572872 | tf_op jit(solution)/shard_map/ppermute | solution.py:734
  258.0 63.8 %collective-permute-start.28 = (bf16[2,32,4096]{2,1,0:T(8,128)(2,1)S(1)}, bf16[2,32,4096]{2,1,0:T(8,128)(2,1)S(1)}, u32[]{:S(2)}, u32[]{:S(2)}) collective-permute-start(bf16[2,32,4096]{2,1,0:T(8,128)(2,1)S(1)} %slice.49), channel_id=1, source_target_pairs={{0,2},{1,3},{2,0},{3,1},{8,10},{9,11},{10,8},{11,9},{16,18},{17,19... | collective-permute-start | bytes 1572872 | tf_op jit(solution)/shard_map/ppermute | solution.py:734
  263.5 48.9 %collective-permute-start.23 = (bf16[32,4096]{1,0:T(8,128)(2,1)}, bf16[32,4096]{1,0:T(8,128)(2,1)S(1)}, u32[]{:S(2)}, u32[]{:S(2)}) collective-permute-start(bf16[32,4096]{1,0:T(8,128)(2,1)} %get-tuple-element.230), channel_id=1, source_target_pairs={{8,0},{9,1},{10,2},{11,3},{12,4},{13,5},{14,6},{15,7}} | collective-permute-start | bytes 786440 | tf_op jit(solution)/shard_map/ppermute | solution.py:793
  315.0 44.4 %collective-permute-start.27 = (bf16[2,32,4096]{2,1,0:T(8,128)(2,1)S(1)}, bf16[2,32,4096]{2,1,0:T(8,128)(2,1)S(1)}, u32[]{:S(2)}, u32[]{:S(2)}) collective-permute-start(bf16[2,32,4096]{2,1,0:T(8,128)(2,1)S(1)} %slice.48), channel_id=1, source_target_pairs={{0,3},{1,0},{2,1},{3,2},{8,11},{9,8},{10,9},{11,10},{16,19},{17,16... | collective-permute-start | bytes 1572872 | tf_op jit(solution)/shard_map/ppermute | solution.py:734
  317.6 64.9 %collective-permute-start.26 = (bf16[2,32,4096]{2,1,0:T(8,128)(2,1)S(1)}, bf16[2,32,4096]{2,1,0:T(8,128)(2,1)S(1)}, u32[]{:S(2)}, u32[]{:S(2)}) collective-permute-start(bf16[2,32,4096]{2,1,0:T(8,128)(2,1)S(1)} %slice.48), channel_id=1, source_target_pairs={{0,1},{1,2},{2,3},{3,0},{8,9},{9,10},{10,11},{11,8},{16,17},{17,18... | collective-permute-start | bytes 1572872 | tf_op jit(solution)/shard_map/ppermute | solution.py:734
  354.7 27.9 %collective-permute-start.29 = (bf16[2,32,4096]{2,1,0:T(8,128)(2,1)S(1)}, bf16[2,32,4096]{2,1,0:T(8,128)(2,1)S(1)}, u32[]{:S(2)}, u32[]{:S(2)}) collective-permute-start(bf16[2,32,4096]{2,1,0:T(8,128)(2,1)S(1)} %slice.48), channel_id=1, source_target_pairs={{0,2},{1,3},{2,0},{3,1},{8,10},{9,11},{10,8},{11,9},{16,18},{17,19... | collective-permute-start | bytes 1572872 | tf_op jit(solution)/shard_map/ppermute | solution.py:734
  357.9 63.7 %collective-permute-start.32 = (f32[1,4096]{1,0:T(1,128)S(1)}, f32[1,4096]{1,0:T(1,128)S(1)}, u32[]{:S(2)}, u32[]{:S(2)}) collective-permute-start(f32[1,4096]{1,0:T(1,128)S(1)} %bitcast.119), channel_id=1, source_target_pairs={{0,3},{1,0},{2,1},{3,2},{8,11},{9,8},{10,9},{11,10},{16,19},{17,16... | collective-permute-start | bytes 49160 | tf_op jit(solution)/shard_map/ppermute | solution.py:734
  359.4 62.2 %collective-permute-start.31 = (f32[1,4096]{1,0:T(1,128)S(1)}, f32[1,4096]{1,0:T(1,128)S(1)}, u32[]{:S(2)}, u32[]{:S(2)}) collective-permute-start(f32[1,4096]{1,0:T(1,128)S(1)} %bitcast.120), channel_id=1, source_target_pairs={{0,2},{1,3},{2,0},{3,1},{8,10},{9,11},{10,8},{11,9},{16,18},{17,19... | collective-permute-start | bytes 49160 | tf_op jit(solution)/shard_map/ppermute | solution.py:734
  359.4 62.2 %collective-permute-start.30 = (f32[1,4096]{1,0:T(1,128)S(1)}, f32[1,4096]{1,0:T(1,128)S(1)}, u32[]{:S(2)}, u32[]{:S(2)}) collective-permute-start(f32[1,4096]{1,0:T(1,128)S(1)} %bitcast.121), channel_id=1, source_target_pairs={{0,1},{1,2},{2,3},{3,0},{8,9},{9,10},{10,11},{11,8},{16,17},{17,18... | collective-permute-start | bytes 49160 | tf_op jit(solution)/shard_map/ppermute | solution.py:734
  418.5 20.2 %collective-permute-start.36 = (bf16[16,10240]{1,0:T(8,128)(2,1)}, bf16[16,10240]{1,0:T(8,128)(2,1)S(1)}, u32[]{:S(2)}, u32[]{:S(2)}) collective-permute-start(bf16[16,10240]{1,0:T(8,128)(2,1)} %get-tuple-element.274), channel_id=1, source_target_pairs={{0,4},{4,0},{1,5},{5,1},{2,6},{6,2},{3,7},{7,3},{8,12},{12,8},{9,1... | collective-permute-start | bytes 983048 | tf_op jit(solution)/shard_map/ppermute | solution.py:864
  (52 other events, 438.3 us)

commit v7 on v6

--- a/solution.py
+++ b/solution.py
@@ -462,7 +462,7 @@
             done(small)
             fwd_norm(dims, x_s, small_s, nrm_s, low_s)
             done(up)
-            fwd_hidden(dims, small_s, up_s, upo, nrm_s, hid_s, slp_s, low_s, 4)
+            fwd_hidden(dims, small_s, up_s, upo, nrm_s, hid_s, slp_s, low_s, 8)
             at = slice(rows, rows + far)
             outs = []
             for q in range(count):

time: 453 us -> 445 us (0.982)
  Pallas kernels: 226 us -> 217 us
    pallas_call x3, Pallas kernels: 67.2 us -> 58.5 us  [fwd_far(): pl.pallas_call(kernel, out_shape=tuple((jax.ShapeDtypeStruct(b.shape, b.d...]
  transfers between devices with their start and end apart: 37 -> 37, of which waited for: 12 -> 12; matrix products, arithmetic and copies ran while one was open for 8% -> 8% of each run, Pallas kernels for 47% -> 46%
where the time goes in v7:
time: 445 us; the launch traced here: 443 us
  Pallas kernels  217 us (49%)
  starting transfers between devices  88.4 us (20%)
  waiting for transfers between devices  86.7 us (19%)
  local copies, waits for them, and re-layouts  38.6 us (9%)
  other arithmetic  10.2 us (2%)
    pallas_call x3, Pallas kernels, fwd_far(): pl.pallas_call(kernel, out_shape=tuple((jax.ShapeDtypeStruct(b.shape, b.d...  58.5 us
    ppermute x18, starting transfers between devices, shifted(): return lax.ppermute(block, ('section', 'dp'), pairs)  50.7 us
    pallas_call x7, Pallas kernels, bwd_slot(): pl.pallas_call(kernel, out_shape=(jax.ShapeDtypeStruct((rows, dims.width)...  48.9 us
    pallas_call x7, Pallas kernels, fwd_slot(): pl.pallas_call(kernel, out_shape=(jax.ShapeDtypeStruct((rows, dims.width)...  40.1 us
    ppermute x18, waiting for transfers between devices, shifted(): return lax.ppermute(block, ('section', 'dp'), pairs)  38.6 us
    pallas_call x2, Pallas kernels, bwd_far(): pl.pallas_call(kernel, out_shape=tuple((jax.ShapeDtypeStruct(b.shape, b.d...  38.4 us
    ppermute x6, waiting for transfers between devices, forward(): frecv = lax.ppermute(y, 'section', pairs)  37.2 us
    pallas_call x2, Pallas kernels, weight_grads(): pl.pallas_call(kernel, out_shape=tuple(shapes), in_specs=[SMEM] * 2 + [AN...  31.6 us
  transfers between devices with their start and end apart: 37, of which 12 were waited for; matrix products, arithmetic and copies ran while one was open for 8% of the time, Pallas kernels for 46%

profile of v7, /device:TPU:13, one launch (start us, length us, event | category | flops | bytes accessed | tf_op | source)
XLA Modules:
  0.0 442.8 jit_solution(14076480336275562263)
XLA Ops:
  19.1 28.3 %collective-permute-done.5.refs_4_ = bf16[32,4096]{1,0:T(8,128)(2,1)S(1)} collective-permute-done((bf16[32,4096]{1,0:T(8,128)(2,1)}, bf16[32,4096]{1,0:T(8,128)(2,1)S(1)}, u32[]{:S(2)}, u32[]{:S(2)}) %collective-permute-start.5) | collective-permute-done | bytes 262176 | tf_op jit(solution)/shard_map/ppermute | solution.py:783
  48.2 9.5 %forward_rows.9 = (bf16[32,4096]{1,0:T(8,128)(2,1)}, bf16[4,128,128,128]{3,2,1,0:T(8,128)(2,1)}, bf16[4,128,128,128]{3,2,1,0:T(8,128)(2,1)}, bf16[4,128,4096]{2,...) custom-call(s32[8]{0:T(128)} %stack.303.refs_0_, ...), custom_call_target="tpu_custom_call", output_to_operand_aliasing={{1}: (11, {}), {2}: (12, {}), {3}: (13, {}), {4}: (14, {}),... | custom-call | tf_op jit(solution)/shard_map/forward_rows/pallas_call | solution.py:302
  62.7 6.7 %collective-permute-done.6.refs_4_ = bf16[32,4096]{1,0:T(8,128)(2,1)S(1)} collective-permute-done((bf16[32,4096]{1,0:T(8,128)(2,1)}, bf16[32,4096]{1,0:T(8,128)(2,1)S(1)}, u32[]{:S(2)}, u32[]{:S(2)}) %collective-permute-start.6) | collective-permute-done | bytes 262176 | tf_op jit(solution)/shard_map/ppermute | solution.py:783
  70.2 9.3 %forward_rows.10 = (bf16[32,4096]{1,0:T(8,128)(2,1)}, bf16[4,128,128,128]{3,2,1,0:T(8,128)(2,1)}, bf16[4,128,128,128]{3,2,1,0:T(8,128)(2,1)}, bf16[4,128,4096]{2...) custom-call(s32[8]{0:T(128)} %stack.299.refs_0_, ...), custom_call_target="tpu_custom_call", output_to_operand_aliasing={{1}: (11, {}), {2}: (12, {}), {3}: (13, {}), {4}: (14, {}),... | custom-call | tf_op jit(solution)/shard_map/forward_rows/pallas_call | solution.py:302
  88.4 9.3 %forward_rows.11 = (bf16[32,4096]{1,0:T(8,128)(2,1)}, bf16[4,128,128,128]{3,2,1,0:T(8,128)(2,1)}, bf16[4,128,128,128]{3,2,1,0:T(8,128)(2,1)}, bf16[4,128,4096]{2...) custom-call(s32[8]{0:T(128)} %stack.311.refs_0_, ...), custom_call_target="tpu_custom_call", output_to_operand_aliasing={{1}: (11, {}), {2}: (12, {}), {3}: (13, {}), {4}: (14, {}),... | custom-call | tf_op jit(solution)/shard_map/forward_rows/pallas_call | solution.py:302
  99.6 11.7 %backward_rows.8 = (bf16[32,4096]{1,0:T(8,128)(2,1)}, bf16[4,128,128,128]{3,2,1,0:T(8,128)(2,1)}, bf16[4,128,4096]{2,1,0:T(8,128)(2,1)}, bf16[4,128,256]{2,1,0:T(8,128)(2,1)}, f32[4,8,4096]{2,1,0:T(8,128)}) custom-call(s32[8]{0:T(128)} %stack.287.refs_0_, s32[128]{0:T(128)} %bitcast.108, ...), custom_call_target="tpu_custom_call", output_to_operand_aliasing={{1}: (13, {}), {2}: (14, {}), {3}: (15, {}), {4}: (16, {})} | custom-call | tf_op jit(solution)/shard_map/backward_rows/pallas_call | solution.py:397
  114.5 13.5 %collective-permute-start.13 = (bf16[32,4096]{1,0:T(8,128)(2,1)S(1)}, bf16[32,4096]{1,0:T(8,128)(2,1)S(1)}, u32[]{:S(2)}, u32[]{:S(2)}) collective-permute-start(bf16[32,4096]{1,0:T(8,128)(2,1)S(1)} %copy-done.38), channel_id=1, source_target_pairs={{8,16},{16,24},{9,17},{17,25},{10,18},{18,26},{11,19},{19,27},{12,... | collective-permute-start | bytes 786440 | tf_op jit(solution)/shard_map/ppermute | solution.py:783
  132.0 9.5 %forward_rows.12 = (bf16[32,4096]{1,0:T(8,128)(2,1)}, bf16[4,128,128,128]{3,2,1,0:T(8,128)(2,1)}, bf16[4,128,128,128]{3,2,1,0:T(8,128)(2,1)}, bf16[4,128,4096]{2...) custom-call(s32[8]{0:T(128)} %stack.315.refs_0_, ...), custom_call_target="tpu_custom_call", output_to_operand_aliasing={{1}: (11, {}), {2}: (12, {}), {3}: (13, {}), {4}: (14, {}),... | custom-call | tf_op jit(solution)/shard_map/forward_rows/pallas_call | solution.py:302
  147.2 11.7 %backward_rows.9 = (bf16[32,4096]{1,0:T(8,128)(2,1)}, bf16[4,128,128,128]{3,2,1,0:T(8,128)(2,1)}, bf16[4,128,4096]{2,1,0:T(8,128)(2,1)}, bf16[4,128,256]{2,1,0:T(8,128)(2,1)}, f32[4,8,4096]{2,1,0:T(8,128)}) custom-call(s32[8]{0:T(128)} %stack.283.refs_0_, s32[128]{0:T(128)} %bitcast.110, ...), custom_call_target="tpu_custom_call", output_to_operand_aliasing={{1}: (13, {}), {2}: (14, {}), {3}: (15, {}), {4}: (16, {})} | custom-call | tf_op jit(solution)/shard_map/backward_rows/pallas_call | solution.py:397
  158.9 5.5 %collective-permute-start.16 = (bf16[2,32,4096]{2,1,0:T(8,128)(2,1)S(1)}, bf16[2,32,4096]{2,1,0:T(8,128)(2,1)S(1)}, u32[]{:S(2)}, u32[]{:S(2)}) collective-permute-start(bf16[2,32,4096]{2,1,0:T(8,128)(2,1)S(1)} %slice.45), channel_id=1, source_target_pairs={{8,10},{9,11},{10,8},{11,9},{16,18},{17,19},{18,16},{19,17},{24,26... | collective-permute-start | bytes 1572872 | tf_op jit(solution)/shard_map/ppermute | solution.py:734
  172.7 13.6 %collective-permute-done.16.refs_7_ = bf16[2,32,4096]{2,1,0:T(8,128)(2,1)S(1)} collective-permute-done((bf16[2,32,4096]{2,1,0:T(8,128)(2,1)S(1)}, bf16[2,32,4096]{2,1,0:T(8,128)(2,1)S(1)}, u32[]{:S(2)}, u32[]{:S(2)}) %collective-permute-start.16) | collective-permute-done | bytes 524320 | tf_op jit(solution)/shard_map/ppermute | solution.py:734
  192.5 11.5 %backward_rows.10 = (bf16[32,4096]{1,0:T(8,128)(2,1)}, bf16[4,128,128,128]{3,2,1,0:T(8,128)(2,1)}, bf16[4,128,4096]{2,1,0:T(8,128)(2,1)}, bf16[4,128,256]{2,1,0:T(8,128)(2,1)}, f32[4,8,4096]{2,1,0:T(8,128)}) custom-call(s32[8]{0:T(128)} %stack.279.refs_0_, ...), custom_call_target="tpu_custom_call", output_to_operand_aliasing={{1}: (13, {}), {2}: (14, {}), {3}: (15, {}), {4}: (16, {})} | custom-call | tf_op jit(solution)/shard_map/backward_rows/pallas_call | solution.py:397
  205.9 5.9 %collective-permute-start.22 = (bf16[2,32,4096]{2,1,0:T(8,128)(2,1)S(1)}, bf16[2,32,4096]{2,1,0:T(8,128)(2,1)S(1)}, u32[]{:S(2)}, u32[]{:S(2)}) collective-permute-start(bf16[2,32,4096]{2,1,0:T(8,128)(2,1)S(1)} %slice.46), channel_id=1, source_target_pairs={{8,10},{9,11},{10,8},{11,9},{16,18},{17,19},{18,16},{19,17},{24,26... | collective-permute-start | bytes 1572872 | tf_op jit(solution)/shard_map/ppermute | solution.py:734
  214.4 7.7 %collective-permute-done.18.refs_4_ = bf16[32,4096]{1,0:T(8,128)(2,1)S(1)} collective-permute-done((bf16[32,4096]{1,0:T(8,128)(2,1)}, bf16[32,4096]{1,0:T(8,128)(2,1)S(1)}, u32[]{:S(2)}, u32[]{:S(2)}) %collective-permute-start.18) | collective-permute-done | bytes 262176 | tf_op jit(solution)/shard_map/ppermute | solution.py:793
  222.8 11.6 %backward_rows.11 = (bf16[32,4096]{1,0:T(8,128)(2,1)}, bf16[4,128,128,128]{3,2,1,0:T(8,128)(2,1)}, bf16[4,128,4096]{2,1,0:T(8,128)(2,1)}, bf16[4,128,256]{2,1,0:T(8,128)(2,1)}, f32[4,8,4096]{2,1,0:T(8,128)}) custom-call(s32[8]{0:T(128)} %stack.275.refs_0_, ...), custom_call_target="tpu_custom_call", output_to_operand_aliasing={{1}: (13, {}), {2}: (14, {}), {3}: (15, {}), {4}: (16, {})} | custom-call | tf_op jit(solution)/shard_map/backward_rows/pallas_call | solution.py:397
  243.5 11.7 %collective-permute-done.22.refs_7_ = bf16[2,32,4096]{2,1,0:T(8,128)(2,1)S(1)} collective-permute-done((bf16[2,32,4096]{2,1,0:T(8,128)(2,1)S(1)}, bf16[2,32,4096]{2,1,0:T(8,128)(2,1)S(1)}, u32[]{:S(2)}, u32[]{:S(2)}) %collective-permute-start.22) | collective-permute-done | bytes 524320 | tf_op jit(solution)/shard_map/ppermute | solution.py:734
  258.0 5.5 %collective-permute-start.28 = (bf16[2,32,4096]{2,1,0:T(8,128)(2,1)S(1)}, bf16[2,32,4096]{2,1,0:T(8,128)(2,1)S(1)}, u32[]{:S(2)}, u32[]{:S(2)}) collective-permute-start(bf16[2,32,4096]{2,1,0:T(8,128)(2,1)S(1)} %slice.49), channel_id=1, source_target_pairs={{0,2},{1,3},{2,0},{3,1},{8,10},{9,11},{10,8},{11,9},{16,18},{17,19... | collective-permute-start | bytes 1572872 | tf_op jit(solution)/shard_map/ppermute | solution.py:734
  265.8 12.8 %collective-permute-done.25.refs_8_ = bf16[2,32,4096]{2,1,0:T(8,128)(2,1)S(1)} collective-permute-done((bf16[2,32,4096]{2,1,0:T(8,128)(2,1)S(1)}, bf16[2,32,4096]{2,1,0:T(8,128)(2,1)S(1)}, u32[]{:S(2)}, u32[]{:S(2)}) %collective-permute-start.25) | collective-permute-done | bytes 524320 | tf_op jit(solution)/shard_map/ppermute | solution.py:734
  279.0 28.9 %forward_far_rows.4 = (bf16[4,128,128,128]{3,2,1,0:T(8,128)(2,1)}, bf16[4,128,128,128]{3,2,1,0:T(8,128)(2,1)}, bf16[4,128,4096]{2,1,0:T(8,128)(2,1)}, bf16[4,128,256]{2,1,0:T(8,128)(2,1)}, f32[8,128]{1,0:T(8,128)}) custom-call(s32[8]{0:T(128)} %stack.323.refs_0_, ...), custom_call_target="tpu_custom_call", output_to_operand_aliasing={{0}: (9, {}), {1}: (10, {}), {2}: (11, {}), {3}: (12, {})} | custom-call | tf_op jit(solution)/shard_map/forward_far_rows/pallas_call | solution.py:480
  317.3 28.6 %forward_far_rows.5 = (bf16[4,128,128,128]{3,2,1,0:T(8,128)(2,1)}, bf16[4,128,128,128]{3,2,1,0:T(8,128)(2,1)}, bf16[4,128,4096]{2,1,0:T(8,128)(2,1)}, bf16[4,128,256]{2,1,0:T(8,128)(2,1)}, f32[8,128]{1,0:T(8,128)}) custom-call(s32[8]{0:T(128)} %stack.326.refs_0_, ...), custom_call_target="tpu_custom_call", output_to_operand_aliasing={{0}: (12, {}), {1}: (13, {}), {2}: (14, {}), {3}: (15, {})} | custom-call | tf_op jit(solution)/shard_map/forward_far_rows/pallas_call | solution.py:480
  354.6 19.2 %backward_far_rows.2 = (bf16[4,128,128,128]{3,2,1,0:T(8,128)(2,1)}, bf16[4,128,4096]{2,1,0:T(8,128)(2,1)}, bf16[4,128,256]{2,1,0:T(8,128)(2,1)}, f32[8,128]{1,0:T(8,128)}) custom-call(s32[8]{0:T(128)} %stack.327.refs_0_, s32[128]{0:T(128)} %bitcast.116, ...), custom_call_target="tpu_custom_call", output_to_operand_aliasing={{0}: (13, {}), {1}: (14, {}), {2}: (15, {})} | custom-call | tf_op jit(solution)/shard_map/backward_far_rows/pallas_call | solution.py:556
  374.8 19.2 %backward_far_rows.3 = (bf16[4,128,128,128]{3,2,1,0:T(8,128)(2,1)}, bf16[4,128,4096]{2,1,0:T(8,128)(2,1)}, bf16[4,128,256]{2,1,0:T(8,128)(2,1)}, f32[8,128]{1,0:T(8,128)}) custom-call(s32[8]{0:T(128)} %stack.261.refs_0_, s32[128]{0:T(128)} %bitcast.117, ...), custom_call_target="tpu_custom_call", output_to_operand_aliasing={{0}: (13, {}), {1}: (14, {}), {2}: (15, {})} | custom-call | tf_op jit(solution)/shard_map/backward_far_rows/pallas_call | solution.py:556
  394.0 15.8 %down_gradients.1 = (bf16[64,128,128]{2,1,0:T(8,128)(2,1)}, bf16[64,128,128]{2,1,0:T(8,128)(2,1)}, bf16[16,10240]{1,0:T(8,128)(2,1)}, bf16[16,10240]{1,0:T(8,128)(2,1)}) custom-call(s32[8]{0:T(128)} %stack.258.refs_0_, s32[128]{0:T(128)} %bitcast.118, bf16[4,128,128,128]{3,2,1,0:T(8,128)(2,1)} %get-tuple-element.268.refs_2_, ...), custom_call_target="tpu_custom_call" | custom-call | tf_op jit(solution)/shard_map/down_gradients/pallas_call | solution.py:673
  413.6 15.8 %up_gradients.1 = (bf16[64,128,128]{2,1,0:T(8,128)(2,1)}, bf16[64,128,128]{2,1,0:T(8,128)(2,1)}, bf16[16,12288]{1,0:T(8,128)(2,1)}, bf16[16,12288]{1,0:T(8,128)(2,1)}) custom-call(s32[8]{0:T(128)} %stack.258.refs_0_, s32[128]{0:T(128)} %select_reduce_fusion.refs_2_.refs_1_, bf16[4,128,128,128]{3,2,1,0:T(8,128)(2,1)} %get-tuple-element.259.refs_2_, ...), custom_call_target="tpu_custom_call" | custom-call | tf_op jit(solution)/shard_map/up_gradients/pallas_call | solution.py:673
  (199 shorter events, 118.2 us)
Async XLA Ops:
  14.6 32.9 %collective-permute-start.5 = (bf16[32,4096]{1,0:T(8,128)(2,1)}, bf16[32,4096]{1,0:T(8,128)(2,1)S(1)}, u32[]{:S(2)}, u32[]{:S(2)}) collective-permute-start(bf16[32,4096]{1,0:T(8,128)(2,1)} %get-tuple-element.149), channel_id=1, source_target_pairs={{0,8},{8,16},{1,9},{9,17},{2,10},{10,18},{3,11},{11,19},{4,12},{12... | collective-permute-start | bytes 786440 | tf_op jit(solution)/shard_map/ppermute | solution.py:783
  17.1 65.0 %collective-permute-start.3 = (bf16[4,32,4096]{2,1,0:T(8,128)(2,1)}, bf16[4,32,4096]{2,1,0:T(8,128)(2,1)S(1)}, u32[]{:S(2)}, u32[]{:S(2)}) collective-permute-start(bf16[4,32,4096]{2,1,0:T(8,128)(2,1)} %broadcast_select_fusion), channel_id=1, source_target_pairs={{0,1},{1,2},{2,3},{3,0},{24,25},{25,26},{26,27},{27,24},{4,5},{5,6... | collective-permute-start | bytes 3145736 | tf_op jit(solution)/shard_map/ppermute | solution.py:734
  18.4 69.3 %collective-permute-start.10 = (bf16[4,32,4096]{2,1,0:T(8,128)(2,1)}, bf16[4,32,4096]{2,1,0:T(8,128)(2,1)S(1)}, u32[]{:S(2)}, u32[]{:S(2)}) collective-permute-start(bf16[4,32,4096]{2,1,0:T(8,128)(2,1)} %broadcast_select_fusion), channel_id=1, source_target_pairs={{0,3},{1,0},{2,1},{3,2},{24,27},{25,24},{26,25},{27,26},{4,7},{5,4... | collective-permute-start | bytes 3145736 | tf_op jit(solution)/shard_map/ppermute | solution.py:734
  57.6 41.2 %collective-permute-start.8 = (bf16[4,32,4096]{2,1,0:T(8,128)(2,1)}, bf16[4,32,4096]{2,1,0:T(8,128)(2,1)}, u32[]{:S(2)}, u32[]{:S(2)}) collective-permute-start(bf16[4,32,4096]{2,1,0:T(8,128)(2,1)} %broadcast_select_fusion), channel_id=1, source_target_pairs={{0,2},{1,3},{2,0},{3,1},{24,26},{25,27},{26,24},{27,25},{4,6},{5,7... | collective-permute-start | bytes 3145736 | tf_op jit(solution)/shard_map/ppermute | solution.py:734
  111.3 35.2 %collective-permute-start.12 = (bf16[2,32,4096]{2,1,0:T(8,128)(2,1)S(1)}, bf16[2,32,4096]{2,1,0:T(8,128)(2,1)S(1)}, u32[]{:S(2)}, u32[]{:S(2)}) collective-permute-start(bf16[2,32,4096]{2,1,0:T(8,128)(2,1)S(1)} %slice.44), channel_id=1, source_target_pairs={{8,9},{9,10},{10,11},{11,8},{16,17},{17,18},{18,19},{19,16},{24,25... | collective-permute-start | bytes 1572872 | tf_op jit(solution)/shard_map/ppermute | solution.py:734
  128.0 18.5 %collective-permute-start.11 = (bf16[32,4096]{1,0:T(8,128)(2,1)}, bf16[32,4096]{1,0:T(8,128)(2,1)S(1)}, u32[]{:S(2)}, u32[]{:S(2)}) collective-permute-start(bf16[32,4096]{1,0:T(8,128)(2,1)} %get-tuple-element.182), channel_id=1, source_target_pairs={{24,16},{16,8},{25,17},{17,9},{26,18},{18,10},{27,19},{19,11},{28,... | collective-permute-start | bytes 786440 | tf_op jit(solution)/shard_map/ppermute | solution.py:793
  142.6 29.1 %collective-permute-start.17 = (bf16[2,32,4096]{2,1,0:T(8,128)(2,1)S(1)}, bf16[2,32,4096]{2,1,0:T(8,128)(2,1)S(1)}, u32[]{:S(2)}, u32[]{:S(2)}) collective-permute-start(bf16[2,32,4096]{2,1,0:T(8,128)(2,1)S(1)} %slice.45), channel_id=1, source_target_pairs={{8,11},{9,8},{10,9},{11,10},{16,19},{17,16},{18,17},{19,18},{24,27... | collective-permute-start | bytes 1572872 | tf_op jit(solution)/shard_map/ppermute | solution.py:734
  158.9 27.4 %collective-permute-start.16 = (bf16[2,32,4096]{2,1,0:T(8,128)(2,1)S(1)}, bf16[2,32,4096]{2,1,0:T(8,128)(2,1)S(1)}, u32[]{:S(2)}, u32[]{:S(2)}) collective-permute-start(bf16[2,32,4096]{2,1,0:T(8,128)(2,1)S(1)} %slice.45), channel_id=1, source_target_pairs={{8,10},{9,11},{10,8},{11,9},{16,18},{17,19},{18,16},{19,17},{24,26... | collective-permute-start | bytes 1572872 | tf_op jit(solution)/shard_map/ppermute | solution.py:734
  169.8 21.9 %collective-permute-start.14 = (bf16[32,4096]{1,0:T(8,128)(2,1)}, bf16[32,4096]{1,0:T(8,128)(2,1)S(1)}, u32[]{:S(2)}, u32[]{:S(2)}) collective-permute-start(bf16[32,4096]{1,0:T(8,128)(2,1)} %get-tuple-element.196), channel_id=1, source_target_pairs={{24,16},{16,8},{8,0},{25,17},{17,9},{9,1},{26,18},{18,10},{10,2},{... | collective-permute-start | bytes 786440 | tf_op jit(solution)/shard_map/ppermute | solution.py:793
  188.2 33.9 %collective-permute-start.19 = (bf16[2,32,4096]{2,1,0:T(8,128)(2,1)S(1)}, bf16[2,32,4096]{2,1,0:T(8,128)(2,1)S(1)}, u32[]{:S(2)}, u32[]{:S(2)}) collective-permute-start(bf16[2,32,4096]{2,1,0:T(8,128)(2,1)S(1)} %slice.46), channel_id=1, source_target_pairs={{8,9},{9,10},{10,11},{11,8},{16,17},{17,18},{18,19},{19,16},{24,25... | collective-permute-start | bytes 1572872 | tf_op jit(solution)/shard_map/ppermute | solution.py:734
  205.9 49.4 %collective-permute-start.22 = (bf16[2,32,4096]{2,1,0:T(8,128)(2,1)S(1)}, bf16[2,32,4096]{2,1,0:T(8,128)(2,1)S(1)}, u32[]{:S(2)}, u32[]{:S(2)}) collective-permute-start(bf16[2,32,4096]{2,1,0:T(8,128)(2,1)S(1)} %slice.46), channel_id=1, source_target_pairs={{8,10},{9,11},{10,8},{11,9},{16,18},{17,19},{18,16},{19,17},{24,26... | collective-permute-start | bytes 1572872 | tf_op jit(solution)/shard_map/ppermute | solution.py:734
  211.8 43.5 %collective-permute-start.21 = (bf16[2,32,4096]{2,1,0:T(8,128)(2,1)S(1)}, bf16[2,32,4096]{2,1,0:T(8,128)(2,1)S(1)}, u32[]{:S(2)}, u32[]{:S(2)}) collective-permute-start(bf16[2,32,4096]{2,1,0:T(8,128)(2,1)S(1)} %slice.46), channel_id=1, source_target_pairs={{8,11},{9,8},{10,9},{11,10},{16,19},{17,16},{18,17},{19,18},{24,27... | collective-permute-start | bytes 1572872 | tf_op jit(solution)/shard_map/ppermute | solution.py:734
  234.4 20.9 %collective-permute-start.20 = (bf16[32,4096]{1,0:T(8,128)(2,1)}, bf16[32,4096]{1,0:T(8,128)(2,1)S(1)}, u32[]{:S(2)}, u32[]{:S(2)}) collective-permute-start(bf16[32,4096]{1,0:T(8,128)(2,1)} %get-tuple-element.223), channel_id=1, source_target_pairs={{16,8},{8,0},{17,9},{9,1},{18,10},{10,2},{19,11},{11,3},{20,12},{1... | collective-permute-start | bytes 786440 | tf_op jit(solution)/shard_map/ppermute | solution.py:793
  236.8 41.8 %collective-permute-start.25 = (bf16[2,32,4096]{2,1,0:T(8,128)(2,1)S(1)}, bf16[2,32,4096]{2,1,0:T(8,128)(2,1)S(1)}, u32[]{:S(2)}, u32[]{:S(2)}) collective-permute-start(bf16[2,32,4096]{2,1,0:T(8,128)(2,1)S(1)} %slice.47), channel_id=1, source_target_pairs={{0,3},{1,0},{2,1},{3,2},{8,11},{9,8},{10,9},{11,10},{16,19},{17,16... | collective-permute-start | bytes 1572872 | tf_op jit(solution)/shard_map/ppermute | solution.py:734
  241.0 38.0 %collective-permute-start.24 = (bf16[2,32,4096]{2,1,0:T(8,128)(2,1)S(1)}, bf16[2,32,4096]{2,1,0:T(8,128)(2,1)S(1)}, u32[]{:S(2)}, u32[]{:S(2)}) collective-permute-start(bf16[2,32,4096]{2,1,0:T(8,128)(2,1)S(1)} %slice.47), channel_id=1, source_target_pairs={{0,1},{1,2},{2,3},{3,0},{8,9},{9,10},{10,11},{11,8},{16,17},{17,18... | collective-permute-start | bytes 1572872 | tf_op jit(solution)/shard_map/ppermute | solution.py:734
  258.0 59.3 %collective-permute-start.28 = (bf16[2,32,4096]{2,1,0:T(8,128)(2,1)S(1)}, bf16[2,32,4096]{2,1,0:T(8,128)(2,1)S(1)}, u32[]{:S(2)}, u32[]{:S(2)}) collective-permute-start(bf16[2,32,4096]{2,1,0:T(8,128)(2,1)S(1)} %slice.49), channel_id=1, source_target_pairs={{0,2},{1,3},{2,0},{3,1},{8,10},{9,11},{10,8},{11,9},{16,18},{17,19... | collective-permute-start | bytes 1572872 | tf_op jit(solution)/shard_map/ppermute | solution.py:734
  263.5 44.4 %collective-permute-start.23 = (bf16[32,4096]{1,0:T(8,128)(2,1)}, bf16[32,4096]{1,0:T(8,128)(2,1)S(1)}, u32[]{:S(2)}, u32[]{:S(2)}) collective-permute-start(bf16[32,4096]{1,0:T(8,128)(2,1)} %get-tuple-element.230), channel_id=1, source_target_pairs={{8,0},{9,1},{10,2},{11,3},{12,4},{13,5},{14,6},{15,7}} | collective-permute-start | bytes 786440 | tf_op jit(solution)/shard_map/ppermute | solution.py:793
  310.6 40.1 %collective-permute-start.27 = (bf16[2,32,4096]{2,1,0:T(8,128)(2,1)S(1)}, bf16[2,32,4096]{2,1,0:T(8,128)(2,1)S(1)}, u32[]{:S(2)}, u32[]{:S(2)}) collective-permute-start(bf16[2,32,4096]{2,1,0:T(8,128)(2,1)S(1)} %slice.48), channel_id=1, source_target_pairs={{0,3},{1,0},{2,1},{3,2},{8,11},{9,8},{10,9},{11,10},{16,19},{17,16... | collective-permute-start | bytes 1572872 | tf_op jit(solution)/shard_map/ppermute | solution.py:734
  313.2 60.7 %collective-permute-start.26 = (bf16[2,32,4096]{2,1,0:T(8,128)(2,1)S(1)}, bf16[2,32,4096]{2,1,0:T(8,128)(2,1)S(1)}, u32[]{:S(2)}, u32[]{:S(2)}) collective-permute-start(bf16[2,32,4096]{2,1,0:T(8,128)(2,1)S(1)} %slice.48), channel_id=1, source_target_pairs={{0,1},{1,2},{2,3},{3,0},{8,9},{9,10},{10,11},{11,8},{16,17},{17,18... | collective-permute-start | bytes 1572872 | tf_op jit(solution)/shard_map/ppermute | solution.py:734
  346.0 27.9 %collective-permute-start.29 = (bf16[2,32,4096]{2,1,0:T(8,128)(2,1)S(1)}, bf16[2,32,4096]{2,1,0:T(8,128)(2,1)S(1)}, u32[]{:S(2)}, u32[]{:S(2)}) collective-permute-start(bf16[2,32,4096]{2,1,0:T(8,128)(2,1)S(1)} %slice.48), channel_id=1, source_target_pairs={{0,2},{1,3},{2,0},{3,1},{8,10},{9,11},{10,8},{11,9},{16,18},{17,19... | collective-permute-start | bytes 1572872 | tf_op jit(solution)/shard_map/ppermute | solution.py:734
  349.2 63.7 %collective-permute-start.32 = (f32[1,4096]{1,0:T(1,128)S(1)}, f32[1,4096]{1,0:T(1,128)S(1)}, u32[]{:S(2)}, u32[]{:S(2)}) collective-permute-start(f32[1,4096]{1,0:T(1,128)S(1)} %bitcast.119), channel_id=1, source_target_pairs={{0,3},{1,0},{2,1},{3,2},{8,11},{9,8},{10,9},{11,10},{16,19},{17,16... | collective-permute-start | bytes 49160 | tf_op jit(solution)/shard_map/ppermute | solution.py:734
  350.7 62.2 %collective-permute-start.31 = (f32[1,4096]{1,0:T(1,128)S(1)}, f32[1,4096]{1,0:T(1,128)S(1)}, u32[]{:S(2)}, u32[]{:S(2)}) collective-permute-start(f32[1,4096]{1,0:T(1,128)S(1)} %bitcast.120), channel_id=1, source_target_pairs={{0,2},{1,3},{2,0},{3,1},{8,10},{9,11},{10,8},{11,9},{16,18},{17,19... | collective-permute-start | bytes 49160 | tf_op jit(solution)/shard_map/ppermute | solution.py:734
  350.7 62.2 %collective-permute-start.30 = (f32[1,4096]{1,0:T(1,128)S(1)}, f32[1,4096]{1,0:T(1,128)S(1)}, u32[]{:S(2)}, u32[]{:S(2)}) collective-permute-start(f32[1,4096]{1,0:T(1,128)S(1)} %bitcast.121), channel_id=1, source_target_pairs={{0,1},{1,2},{2,3},{3,0},{8,9},{9,10},{10,11},{11,8},{16,17},{17,18... | collective-permute-start | bytes 49160 | tf_op jit(solution)/shard_map/ppermute | solution.py:734
  409.8 20.2 %collective-permute-start.36 = (bf16[16,10240]{1,0:T(8,128)(2,1)}, bf16[16,10240]{1,0:T(8,128)(2,1)S(1)}, u32[]{:S(2)}, u32[]{:S(2)}) collective-permute-start(bf16[16,10240]{1,0:T(8,128)(2,1)} %get-tuple-element.274), channel_id=1, source_target_pairs={{0,4},{4,0},{1,5},{5,1},{2,6},{6,2},{3,7},{7,3},{8,12},{12,8},{9,1... | collective-permute-start | bytes 983048 | tf_op jit(solution)/shard_map/ppermute | solution.py:864
  (52 other events, 420.8 us)
